TPU v7x, 32 devices: a whole 2x2x4 slice. The times are simulated.
32 devices in a mesh: dp: 4 (over y, core), chan: 8 (over z, x).
Axes of the slice: x: 2, y: 2, z: 4, core: 2. Of those that a mesh axis runs over, the one named last changes fastest.
Arguments:
- inputs: bfloat16 [2, 6272, 2048], P(None, 'dp', 'chan'), may hold values from -6 to 6
- cotangent: bfloat16 [2, 6272, 2048], P(None, 'dp', 'chan'), may hold values from -6 to 6
- w_first: float32 [2048, 512], P('chan', 'dp'), may hold values from -0.125 to 0.125
- first_m: float32 [2048, 512], P('chan', 'dp'), may hold values from -256 to 256
- first_v: float32 [2048, 512], P('chan', 'dp'), may hold values from 940.8 to 7526.4
- w_middle: float32 [3, 3, 512, 512], P(None, None, 'chan', 'dp'), may hold values from -0.09375 to 0.09375
- middle_m: float32 [3, 3, 512, 512], P(None, None, 'chan', 'dp'), may hold values from -256 to 256
- middle_v: float32 [3, 3, 512, 512], P(None, None, 'chan', 'dp'), may hold values from 940.8 to 7526.4
- w_last: float32 [512, 2048], P('chan', 'dp'), may hold values from -0.25 to 0.25
- last_m: float32 [512, 2048], P('chan', 'dp'), may hold values from -256 to 256
- last_v: float32 [512, 2048], P('chan', 'dp'), may hold values from 940.8 to 7526.4
- mid_params: float32 [4, 512], P(None, 'chan'), may hold values from 0.5 to 1.5
- mid_m: float32 [4, 512], P(None, 'chan'), may hold values from -256 to 256
- mid_v: float32 [4, 512], P(None, 'chan'), may hold values from 940.8 to 7526.4
- out_params: float32 [2, 2048], P(None, 'chan'), may hold values from 0.5 to 1.5
- out_m: float32 [2, 2048], P(None, 'chan'), may hold values from -256 to 256
- out_v: float32 [2, 2048], P(None, 'chan'), may hold values from 940.8 to 7526.4
- image_counts: int32 [2, 4], replicated, may hold values from 1 to 32, 96 in all within a row
Outputs:
- block_out: float32 [2, 6272, 2048], P(None, 'dp', 'chan')
- input_grad: float32 [2, 6272, 2048], P(None, 'dp', 'chan')
- first_new: float32 [2048, 512], P('chan', 'dp')
- first_m_new: float32 [2048, 512], P('chan', 'dp')
- first_v_new: float32 [2048, 512], P('chan', 'dp')
- middle_new: float32 [3, 3, 512, 512], P(None, None, 'chan', 'dp')
- middle_m_new: float32 [3, 3, 512, 512], P(None, None, 'chan', 'dp')
- middle_v_new: float32 [3, 3, 512, 512], P(None, None, 'chan', 'dp')
- last_new: float32 [512, 2048], P('chan', 'dp')
- last_m_new: float32 [512, 2048], P('chan', 'dp')
- last_v_new: float32 [512, 2048], P('chan', 'dp')
- mid_new: float32 [4, 512], P(None, 'chan')
- mid_m_new: float32 [4, 512], P(None, 'chan')
- mid_v_new: float32 [4, 512], P(None, 'chan')
- out_new: float32 [2, 2048], P(None, 'chan')
- out_m_new: float32 [2, 2048], P(None, 'chan')
- out_v_new: float32 [2, 2048], P(None, 'chan')
Inputs may be any that keep to these rules, and one draw needn't show every extreme that they name: image_counts[m, g] live images stand first among the 32 slots of index g of dp; each micro-batch has exactly (384) // 4 live images, and some index holds 32.
All inputs are finite; a program needn't handle non-finite values.
Results may differ from a plain program's by a relative error of at most 0.03.
Values may be sent and summed in bfloat16 or wider, within the bound.
No kernel may reach another device: no remote copies, remote signals or barrier semaphores. Data moves between devices by JAX's collectives and lax.ppermute only.
A program may use at most 128 MiB of HBM per device.

v0:
```python
import jax
import jax.numpy as jnp
from jax import lax
from jax.sharding import PartitionSpec as P

STEPS = 5


norm_eps = 1e-05
adam_eps = 1e-08
adam_beta = 0.5
decay_rate = 0.05
rate_first = 0.02
rate_middle = 0.015
rate_last = 0.04
rate_norm = 0.25


def silu_slope(value):
    sigma = jax.nn.sigmoid(value)
    return sigma * (1.0 + value * (1.0 - sigma))


def cross_rows(left, right):
    return lax.dot_general(
        left, right, (((0,), (0,)), ((), ())), preferred_element_type=jnp.float32
    )


def cross_cols(left, right):
    return lax.dot_general(
        left, right, (((1,), (1,)), ((), ())), preferred_element_type=jnp.float32
    )


def patches(acts, images):
    grid = acts.reshape(images, 7, 7, acts.shape[1])
    padded = jnp.pad(grid, ((0, 0), (1, 1), (1, 1), (0, 0)))
    pieces = [
        padded[:, row_off : row_off + 7, col_off : col_off + 7, :]
        for row_off in range(3)
        for col_off in range(3)
    ]
    return jnp.concatenate(pieces, axis=3).reshape(images * 49, 9 * acts.shape[1])


def unpatch(grads, images, width):
    grid = grads.reshape(images, 7, 7, 9, width)
    total = jnp.zeros((images, 9, 9, width), jnp.float32)
    for row_off in range(3):
        for col_off in range(3):
            piece = grid[:, :, :, row_off * 3 + col_off, :]
            total = total + jnp.pad(
                piece, ((0, 0), (row_off, 2 - row_off), (col_off, 2 - col_off), (0, 0))
            )
    return total[:, 1:8, 1:8, :].reshape(images * 49, width)


def normalize(pre, live_rows, live_count):
    sums = lax.psum(
        (jnp.sum(live_rows * pre, axis=0), jnp.sum(live_rows * pre * pre, axis=0)), "dp"
    )
    average = sums[0] / live_count
    variance = sums[1] / live_count - average * average
    inv_std = lax.rsqrt(variance + norm_eps)
    return ((pre - average) * inv_std, inv_std)


def norm_back(upstream, normed, inv_std, gain_row, live_rows, live_count):
    sums = lax.psum((jnp.sum(upstream, axis=0), jnp.sum(upstream * normed, axis=0)), "dp")
    grad_pre = (
        live_rows * gain_row * inv_std * (upstream - (sums[0] + normed * sums[1]) / live_count)
    )
    return (grad_pre.astype(jnp.bfloat16), sums[1], sums[0])


def mid_collect(grads):
    return lax.all_gather(grads, "chan", axis=1, tiled=True)


def adamw(weight, gradient, moment_one, moment_two, step_rate):
    one_new = adam_beta * moment_one + (1.0 - adam_beta) * gradient
    two_new = adam_beta * moment_two + (1.0 - adam_beta) * gradient * gradient
    correct = 1.0 - adam_beta**STEPS
    weight_new = weight - step_rate * (
        one_new / correct / (jnp.sqrt(two_new / correct) + adam_eps) + decay_rate * weight
    )
    return (weight_new, one_new, two_new)


def local(
    inputs,
    cotangent,
    w_first,
    first_m,
    first_v,
    w_middle,
    middle_m,
    middle_v,
    w_last,
    last_m,
    last_v,
    mid_params,
    mid_m,
    mid_v,
    out_params,
    out_m,
    out_v,
    image_counts,
):
    dp_index = lax.axis_index("dp")
    micro_count = inputs.shape[0]
    pixels = inputs.shape[1]
    images = pixels // 49
    in_local = inputs.shape[2]
    mid_local = w_middle.shape[2]
    first_all, middle_all, last_all = (
        lax.all_gather(w_first.astype(jnp.bfloat16), "dp", axis=1, tiled=True),
        lax.all_gather(w_middle.astype(jnp.bfloat16), "dp", axis=3, tiled=True),
        lax.all_gather(w_last.astype(jnp.bfloat16), "dp", axis=1, tiled=True),
    )
    width_mid = first_all.shape[1]
    width_full = last_all.shape[1]
    middle_rows = middle_all.reshape(9 * mid_local, width_mid)
    grad_first = jnp.zeros((in_local, width_mid), jnp.float32)
    grad_middle = jnp.zeros((9 * mid_local, width_mid), jnp.float32)
    grad_last = jnp.zeros((mid_local, width_full), jnp.float32)
    grad_mid_params = jnp.zeros((4, mid_local), jnp.float32)
    grad_out_params = jnp.zeros((2, in_local), jnp.float32)
    outputs = []
    input_grads = []
    for batch_index in range(micro_count):
        counts_row = image_counts[batch_index]
        own_count = lax.dynamic_index_in_dim(counts_row, dp_index, keepdims=False)
        live_rows = (jnp.arange(pixels) // 49 < own_count).astype(jnp.float32)[:, None]
        live_count = 49.0 * jnp.sum(counts_row).astype(jnp.float32)
        block_in = inputs[batch_index]
        pre_first = lax.psum_scatter(
            jnp.dot(block_in, first_all, preferred_element_type=jnp.float32),
            "chan",
            scatter_dimension=1,
            tiled=True,
        )
        normed_first, inv_first = normalize(pre_first, live_rows, live_count)
        z_first = mid_params[0] * normed_first + mid_params[1]
        act_first = (z_first * jax.nn.sigmoid(z_first)).astype(jnp.bfloat16)
        columns = patches(act_first, images)
        pre_middle = lax.psum_scatter(
            jnp.dot(columns, middle_rows, preferred_element_type=jnp.float32).astype(jnp.bfloat16),
            "chan",
            scatter_dimension=1,
            tiled=True,
        ).astype(jnp.float32)
        normed_middle, inv_middle = normalize(pre_middle, live_rows, live_count)
        z_middle = mid_params[2] * normed_middle + mid_params[3]
        act_middle = (z_middle * jax.nn.sigmoid(z_middle)).astype(jnp.bfloat16)
        pre_last = lax.psum_scatter(
            jnp.dot(act_middle, last_all, preferred_element_type=jnp.float32).astype(jnp.bfloat16),
            "chan",
            scatter_dimension=1,
            tiled=True,
        ).astype(jnp.float32)
        normed_last, inv_last = normalize(pre_last, live_rows, live_count)
        summed = out_params[0] * normed_last + out_params[1] + block_in.astype(jnp.float32)
        outputs.append(live_rows * summed * jax.nn.sigmoid(summed))
        grad_summed = cotangent[batch_index].astype(jnp.float32) * live_rows * silu_slope(summed)
        grad_pre_last, gain_last, shift_last = norm_back(
            grad_summed, normed_last, inv_last, out_params[0], live_rows, live_count
        )
        grad_last_whole = lax.all_gather(grad_pre_last, "chan", axis=1, tiled=True)
        grad_act_middle = cross_cols(grad_last_whole, last_all)
        grad_last = grad_last + cross_rows(act_middle, grad_last_whole)
        upstream_middle = grad_act_middle * silu_slope(z_middle)
        grad_pre_middle, gain_middle, shift_middle = norm_back(
            upstream_middle, normed_middle, inv_middle, mid_params[2], live_rows, live_count
        )
        grad_middle_whole = mid_collect(grad_pre_middle)
        grad_columns = cross_cols(grad_middle_whole, middle_rows)
        grad_act_first = unpatch(grad_columns, images, mid_local)
        grad_middle = grad_middle + cross_rows(columns, grad_middle_whole)
        upstream_first = grad_act_first * silu_slope(z_first)
        grad_pre_first, gain_first, shift_first = norm_back(
            upstream_first, normed_first, inv_first, mid_params[0], live_rows, live_count
        )
        grad_first_whole = mid_collect(grad_pre_first)
        input_grads.append(grad_summed + cross_cols(grad_first_whole, first_all))
        grad_first = grad_first + cross_rows(block_in, grad_first_whole)
        grad_mid_params = grad_mid_params + jnp.stack(
            [gain_first, shift_first, gain_middle, shift_middle]
        )
        grad_out_params = grad_out_params + jnp.stack([gain_last, shift_last])
    owned_first, owned_middle, owned_last = (
        lax.psum_scatter(
            grad_first.astype(jnp.bfloat16), "dp", scatter_dimension=1, tiled=True
        ).astype(jnp.float32),
        lax.psum_scatter(
            grad_middle.reshape(3, 3, mid_local, width_mid).astype(jnp.bfloat16),
            "dp",
            scatter_dimension=3,
            tiled=True,
        ).astype(jnp.float32),
        lax.psum_scatter(
            grad_last.astype(jnp.bfloat16), "dp", scatter_dimension=1, tiled=True
        ).astype(jnp.float32),
    )
    first_new, first_m_new, first_v_new = adamw(w_first, owned_first, first_m, first_v, rate_first)
    middle_new, middle_m_new, middle_v_new = adamw(
        w_middle, owned_middle, middle_m, middle_v, rate_middle
    )
    last_new, last_m_new, last_v_new = adamw(w_last, owned_last, last_m, last_v, rate_last)
    mid_new, mid_m_new, mid_v_new = adamw(mid_params, grad_mid_params, mid_m, mid_v, rate_norm)
    out_new, out_m_new, out_v_new = adamw(out_params, grad_out_params, out_m, out_v, rate_norm)
    return (
        jnp.stack(outputs),
        jnp.stack(input_grads),
        first_new,
        first_m_new,
        first_v_new,
        middle_new,
        middle_m_new,
        middle_v_new,
        last_new,
        last_m_new,
        last_v_new,
        mid_new,
        mid_m_new,
        mid_v_new,
        out_new,
        out_m_new,
        out_v_new,
    )


def solution(mesh):
    placed = (
        P(None, "dp", "chan"),
        P(None, "dp", "chan"),
        P("chan", "dp"),
        P("chan", "dp"),
        P("chan", "dp"),
        P(None, None, "chan", "dp"),
        P(None, None, "chan", "dp"),
        P(None, None, "chan", "dp"),
        P("chan", "dp"),
        P("chan", "dp"),
        P("chan", "dp"),
        P(None, "chan"),
        P(None, "chan"),
        P(None, "chan"),
        P(None, "chan"),
        P(None, "chan"),
        P(None, "chan"),
        P(),
    )
    return jax.shard_map(
        local,
        mesh=mesh,
        in_specs=placed,
        out_specs=(
            P(None, "dp", "chan"),
            P(None, "dp", "chan"),
            P("chan", "dp"),
            P("chan", "dp"),
            P("chan", "dp"),
            P(None, None, "chan", "dp"),
            P(None, None, "chan", "dp"),
            P(None, None, "chan", "dp"),
            P("chan", "dp"),
            P("chan", "dp"),
            P("chan", "dp"),
            P(None, "chan"),
            P(None, "chan"),
            P(None, "chan"),
            P(None, "chan"),
            P(None, "chan"),
            P(None, "chan"),
        ),
        check_vma=False,
    )
```

profile of v0, /device:TPU:0, one launch (start us, length us, event | category | flops | bytes accessed | tf_op | source)
XLA Modules:
  0.0 1125.7 jit_solution(10540089122748818967)
XLA Ops:
  8.1 7.2 all_gather.27
  27.4 8.1 all_gather.28
  35.5 62.3 %reduce-scatter.18.cloned.1.call-done = f32[1568,64]{0,1:T(8,128)} async-done(((f32[1568,512]{0,1:T(8,128)}), f32[1568,64]{0,1:T(8,128)}) %reduce-scatter.18.cloned.1.call-update) | async-done | bytes 401424 | tf_op jit(solution)/shard_map/reduce_scatter | solution.py:138
  99.0 79.7 %reduce-scatter.12.cloned.1.call-done = f32[1568,64]{0,1:T(8,128)} async-done(((f32[1568,512]{0,1:T(8,128)}), f32[1568,64]{0,1:T(8,128)}) %reduce-scatter.12.cloned.1.call-update) | async-done | bytes 401424 | tf_op jit(solution)/shard_map/reduce_scatter | solution.py:138
  179.8 6.2 all-reduce.25
  242.5 34.3 %reduce-scatter.20.cloned.1.call-done = bf16[1568,64]{0,1:T(8,128)(2,1)} async-done(((bf16[1568,512]{0,1:T(8,128)(2,1)}), bf16[1568,64]{0,1:T(8,128)(2,1)}) %reduce-scatter.20.cloned.1.call-update) | async-done | bytes 200720 | tf_op jit(solution)/shard_map/reduce_scatter | solution.py:148
  277.9 66.9 %reduce-scatter.14.cloned.1.call-done = bf16[1568,64]{0,1:T(8,128)(2,1)} async-done(((bf16[1568,512]{0,1:T(8,128)(2,1)}), bf16[1568,64]{0,1:T(8,128)(2,1)}) %reduce-scatter.14.cloned.1.call-update) | async-done | bytes 200720 | tf_op jit(solution)/shard_map/reduce_scatter | solution.py:148
  364.0 112.7 %reduce-scatter.16.cloned.1.call-done = bf16[1568,256]{1,0:T(8,128)(2,1)} async-done(((bf16[1568,2048]{1,0:T(8,128)(2,1)}), bf16[1568,256]{1,0:T(8,128)(2,1)}) %reduce-scatter.16.cloned.1.call-update) | async-done | bytes 802832 | tf_op jit(solution)/shard_map/reduce_scatter | solution.py:157
  478.3 121.8 %reduce-scatter.22.cloned.1.call-done = bf16[1568,256]{1,0:T(8,128)(2,1)} async-done(((bf16[1568,2048]{1,0:T(8,128)(2,1)}), bf16[1568,256]{1,0:T(8,128)(2,1)}) %reduce-scatter.22.cloned.1.call-update) | async-done | bytes 802832 | tf_op jit(solution)/shard_map/reduce_scatter | solution.py:157
  601.6 6.0 all-reduce.23
  607.6 6.0 fusion.110
  613.5 7.2 all-reduce.22
  624.9 99.6 %all-gather.13.cloned.1.call-done = bf16[1568,2048]{1,0:T(8,128)(2,1)} async-done(((bf16[1568,256]{1,0:T(8,128)(2,1)}), bf16[1568,2048]{1,0:T(8,128)(2,1)}) %all-gather.13.cloned.1.call-update) | async-done | bytes 6422544 | tf_op jit(solution)/shard_map/all_gather | solution.py:170
  724.4 6.4 fusion.115
  730.8 95.4 %all-gather.7.cloned.1.call-done = bf16[1568,2048]{1,0:T(8,128)(2,1)} async-done(((bf16[1568,256]{1,0:T(8,128)(2,1)}), bf16[1568,2048]{1,0:T(8,128)(2,1)}) %all-gather.7.cloned.1.call-update) | async-done | bytes 6422544 | tf_op jit(solution)/shard_map/all_gather | solution.py:170
  826.2 6.4 fusion.113
  832.6 6.3 all-reduce.21
  851.9 33.1 %all-gather.15.cloned.1.call-done = bf16[1568,512]{0,1:T(8,128)(2,1)} async-done(((bf16[1568,64]{0,1:T(8,128)(2,1)}), bf16[1568,512]{0,1:T(8,128)(2,1)}) %all-gather.15.cloned.1.call-update) | async-done | bytes 1605648 | tf_op jit(solution)/shard_map/all_gather | solution.py:78
  892.3 39.6 %all-gather.9.cloned.1.call-done = bf16[1568,512]{0,1:T(8,128)(2,1)} async-done(((bf16[1568,64]{0,1:T(8,128)(2,1)}), bf16[1568,512]{0,1:T(8,128)(2,1)}) %all-gather.9.cloned.1.call-update) | async-done | bytes 1605648 | tf_op jit(solution)/shard_map/all_gather | solution.py:78
  971.1 6.1 slice_bitcast_fusion.8
  991.3 6.9 all-reduce.20
  1020.5 26.1 %all-gather.11.cloned.1.call-done = bf16[1568,512]{0,1:T(8,128)(2,1)} async-done(((bf16[1568,64]{0,1:T(8,128)(2,1)}), bf16[1568,512]{0,1:T(8,128)(2,1)}) %all-gather.11.cloned.1.call-update) | async-done | bytes 1605648 | tf_op jit(solution)/shard_map/all_gather | solution.py:78
  1049.7 43.4 %all-gather.17.cloned.1.call-done = bf16[1568,512]{0,1:T(8,128)(2,1)} async-done(((bf16[1568,64]{0,1:T(8,128)(2,1)}), bf16[1568,512]{0,1:T(8,128)(2,1)}) %all-gather.17.cloned.1.call-update) | async-done | bytes 1605648 | tf_op jit(solution)/shard_map/all_gather | solution.py:78
  1101.1 14.4 %reduce-scatter.24.cloned.1.call-done = bf16[256,128]{0,1:T(8,128)(2,1)} async-done(((bf16[256,512]{0,1:T(8,128)(2,1)}), bf16[256,128]{0,1:T(8,128)(2,1)}) %reduce-scatter.24.cloned.1.call-update) | async-done | bytes 65552 | tf_op jit(solution)/shard_map/reduce_scatter | solution.py:193
  (256 shorter events, 207.4 us)
Async XLA Ops:
  7.2 90.6 %reduce-scatter.18.cloned.1.call-start = ((), (), s32[]{:S(2)}) async-start(), calls=%async_computation.12 | async-start | bytes 3833856 | tf_op jit(solution)/shard_map/reduce_scatter | solution.py:138
  18.9 159.7 %reduce-scatter.12.cloned.1.call-start = ((), (), s32[]{:S(2)}) async-start(), calls=%async_computation.9 | async-start | bytes 3833856 | tf_op jit(solution)/shard_map/reduce_scatter | solution.py:138
  22.8 12.7 %copy-start.33 = (f32[4,64]{1,0:T(4,128)S(1)}, f32[4,64]{1,0:T(4,128)}, u32[]{:S(2)}) copy-start(f32[4,64]{1,0:T(4,128)} %param.29) | copy-start | bytes 3076
  22.8 253.9 %reduce-scatter.20.cloned.1.call-start = ((), (), s32[]{:S(2)}) async-start(), calls=%async_computation.13 | async-start | bytes 1916928 | tf_op jit(solution)/shard_map/reduce_scatter | solution.py:148
  35.5 153.8 %copy-start.35 = (f32[64]{0:T(128)}, f32[64]{0:T(128)S(1)}, u32[]{:S(2)}) copy-start(f32[64]{0:T(128)S(1)} %get-tuple-element.191) | copy-start | bytes 772
  212.2 132.6 %reduce-scatter.14.cloned.1.call-start = ((), (), s32[]{:S(2)}) async-start(), calls=%async_computation.10 | async-start | bytes 1916928 | tf_op jit(solution)/shard_map/reduce_scatter | solution.py:148
  235.8 241.0 %reduce-scatter.16.cloned.1.call-start = ((), (), s32[]{:S(2)}) async-start(), calls=%async_computation.11 | async-start | bytes 7225344 | tf_op jit(solution)/shard_map/reduce_scatter | solution.py:157
  242.5 114.8 %copy-start.7 = (bf16[64,2048]{1,0:T(8,128)(2,1)}, bf16[64,2048]{1,0:T(8,128)(2,1)S(1)}, u32[]{:S(2)}) copy-start(bf16[64,2048]{1,0:T(8,128)(2,1)S(1)} %all_gather.29) | copy-start | bytes 786436
  357.2 242.9 %reduce-scatter.22.cloned.1.call-start = ((), (), s32[]{:S(2)}) async-start(), calls=%async_computation.14 | async-start | bytes 7225344 | tf_op jit(solution)/shard_map/reduce_scatter | solution.py:157
  362.8 361.6 %all-gather.13.cloned.1.call-start = ((), (), s32[]{:S(2)}) async-start(), calls=%async_computation.18 | async-start | bytes 7225344 | tf_op jit(solution)/shard_map/all_gather | solution.py:170
  624.1 202.2 %all-gather.7.cloned.1.call-start = ((), (), s32[]{:S(2)}) async-start(), calls=%async_computation.15 | async-start | bytes 7225344 | tf_op jit(solution)/shard_map/all_gather | solution.py:170
  624.8 260.2 %all-gather.15.cloned.1.call-start = ((), (), s32[]{:S(2)}) async-start(), calls=%async_computation.19 | async-start | bytes 1916928 | tf_op jit(solution)/shard_map/all_gather | solution.py:78
  841.6 90.3 %all-gather.9.cloned.1.call-start = ((), (), s32[]{:S(2)}) async-start(), calls=%async_computation.16 | async-start | bytes 1916928 | tf_op jit(solution)/shard_map/all_gather | solution.py:78
  842.2 169.9 %reduce-scatter.26.cloned.1.call-start = ((), (), s32[]{:S(2)}) async-start(), calls=%async_computation.22 | async-start | bytes 327680 | tf_op jit(solution)/shard_map/reduce_scatter | solution.py:202
  851.7 162.9 %reduce-scatter.28.cloned.1.call-start = ((), (), s32[]{:S(2)}) async-start(), calls=%async_computation.23 | async-start | bytes 819200
  977.2 69.4 %all-gather.11.cloned.1.call-start = ((), (), s32[]{:S(2)}) async-start(), calls=%async_computation.17 | async-start | bytes 1916928 | tf_op jit(solution)/shard_map/all_gather | solution.py:78
  998.2 8.6 copy-start.38
  998.2 8.6 copy-start.39
  998.2 8.6 copy-start.40
  1001.1 92.0 %all-gather.17.cloned.1.call-start = ((), (), s32[]{:S(2)}) async-start(), calls=%async_computation.20 | async-start | bytes 1916928 | tf_op jit(solution)/shard_map/all_gather | solution.py:78
  1001.7 113.8 %reduce-scatter.24.cloned.1.call-start = ((), (), s32[]{:S(2)}) async-start(), calls=%async_computation.21 | async-start | bytes 327680 | tf_op jit(solution)/shard_map/reduce_scatter | solution.py:193
  1099.2 16.3 %copy-start.24 = (f32[256,128]{0,1:T(8,128)S(1)}, f32[256,128]{0,1:T(8,128)}, u32[]{:S(2)}) copy-start(f32[256,128]{0,1:T(8,128)} %copy.156) | copy-start | bytes 393220
  1099.2 16.3 %copy-start.25 = (f32[256,128]{0,1:T(8,128)S(1)}, f32[256,128]{0,1:T(8,128)}, u32[]{:S(2)}) copy-start(f32[256,128]{0,1:T(8,128)} %copy.153) | copy-start | bytes 393220
  1099.2 16.3 %copy-start.26 = (f32[256,128]{0,1:T(8,128)S(1)}, f32[256,128]{0,1:T(8,128)}, u32[]{:S(2)}) copy-start(f32[256,128]{0,1:T(8,128)} %copy.154) | copy-start | bytes 393220
  (37 other events, 97.2 us)
Sparse Core Ops, SparseCore 0:
  19.1 78.7 reduce-scatter.17
  101.9 76.7 reduce-scatter.11
  212.4 64.3 reduce-scatter.19
  280.4 64.3 reduce-scatter.13
  357.4 119.3 reduce-scatter.15
  480.7 119.3 reduce-scatter.21
  624.2 100.2 all-gather.12
  726.5 99.6 all-gather.6
  841.7 43.2 all-gather.14
  887.6 44.2 all-gather.8
  934.9 18.9 reduce-scatter.25
  977.3 21.5 reduce-scatter.27
  1001.3 45.2 all-gather.10
  1048.9 44.2 all-gather.16
  1096.4 18.9 reduce-scatter.23
where the time goes:
time: 1130 us
  waiting for transfers between devices  831 us (74%)
  local copies, waits for them, and re-layouts  103 us (9%)
  matrix products  65.2 us (6%)
  blocking collectives  59.3 us (5%)
  other arithmetic  49.4 us (4%)
  between operations  16.3 us (1%)
    reduce_scatter x2, waiting for transfers between devices, local(): lax.psum_scatter(jnp.dot(act_middle, last_all, preferred_element_type=jnp...  235 us
    all_gather x2, waiting for transfers between devices, local(): grad_last_whole = lax.all_gather(grad_pre_last, 'chan', axis=1, tiled=True)  195 us
    all_gather x4, waiting for transfers between devices, mid_collect(): return lax.all_gather(grads, 'chan', axis=1, tiled=True)  142 us
    reduce_scatter x2, waiting for transfers between devices, local(): lax.psum_scatter(jnp.dot(block_in, first_all, preferred_element_type=jnp....  142 us
    reduce_scatter x2, waiting for transfers between devices, local(): lax.psum_scatter(jnp.dot(columns, middle_rows, preferred_element_type=jnp...  101 us
    unnamed x118, local copies, waits for them, and re-layouts  30.1 us
    concatenate x34, local copies, waits for them, and re-layouts, patches(): jnp.concatenate(pieces, axis=3).reshape(images * 49, 9 * acts.shape[1])  25.6 us
    dot_general x6, matrix products, cross_cols(): lax.dot_general(left, right, (((1,), (1,)), ((), ())), preferred_element_...  24.3 us
  transfers between devices with their start and end apart: 15, of which 13 were waited for; matrix products, arithmetic and copies ran while one was open for 13% of the time, Pallas kernels for 0%

commit v1 on v0

v1 whole, which is shorter than its diff:
```python
import functools

import jax
import jax.numpy as jnp
import numpy as np
from jax import lax
from jax.experimental import pallas as pl
from jax.experimental.pallas import tpu as pltpu
from jax.sharding import PartitionSpec as P

STEPS = 5
SIDE = 7
PIXELS = SIDE * SIDE
TAPS = 9
F32 = jnp.float32
BF16 = jnp.bfloat16

norm_eps = 1e-05
adam_eps = 1e-08
adam_beta = 0.5
decay_rate = 0.05
rate_first = 0.02
rate_middle = 0.015
rate_last = 0.04
rate_norm = 0.25


def sigmoid(value):
    return 0.5 * jnp.tanh(0.5 * value) + 0.5


def silu_slope(value):
    sigma = sigmoid(value)
    return sigma * (1.0 + value * (1.0 - sigma))


def moments(stat, count):
    average = stat[0:1] / count
    variance = stat[1:2] / count - average * average
    return average, lax.rsqrt(variance + norm_eps)


def adamw(weight, gradient, moment_one, moment_two, step_rate):
    one_new = adam_beta * moment_one + (1.0 - adam_beta) * gradient
    two_new = adam_beta * moment_two + (1.0 - adam_beta) * gradient * gradient
    correct = 1.0 - adam_beta**STEPS
    weight_new = weight - step_rate * (
        one_new / correct / (jnp.sqrt(two_new / correct) + adam_eps) + decay_rate * weight
    )
    return (weight_new, one_new, two_new)


def ring_of(size):
    across = max(size // 4, 1)
    along = size // across
    order = [(z, 0) for z in range(along)]
    outward = True
    for z in reversed(range(along)):
        steps = list(range(1, across))
        order += [(z, x) for x in (steps if outward else steps[::-1])]
        outward = not outward
    return [z * across + x for z, x in order]


class Ring:
    def __init__(self, size):
        self.size = size
        self.order = ring_of(size)
        ahead = [(self.order[i], self.order[(i + 1) % size]) for i in range(size)]
        self.ahead = ahead
        self.back = [(b, a) for a, b in ahead]
        place = np.argsort(np.array(self.order))
        self.table = np.array(
            [[self.order[(place[c] + k) % size] for k in range(size)] for c in range(size)],
            np.int32,
        )

    def fw(self, x):
        return lax.ppermute(x, "chan", self.ahead)

    def bw(self, x):
        return lax.ppermute(x, "chan", self.back)

    def gather(self, x, axis):
        size, half = self.size, x.shape[axis] // 2
        pieces = [None] * size
        pieces[0] = x
        a = b = x
        for step in range(1, size // 2):
            a, b = self.fw(a), self.bw(b)
            pieces[size - step], pieces[step] = a, b
        low = self.fw(lax.slice_in_dim(a, 0, half, axis=axis))
        high = self.bw(lax.slice_in_dim(b, half, x.shape[axis], axis=axis))
        pieces[size // 2] = (low, high)
        return pieces

    def scatter(self, parts, axis):
        size = self.size
        width = parts[0].shape[axis]
        half = width // 2
        middle = parts[size // 2]
        f = self.fw(lax.slice_in_dim(middle, 0, half, axis=axis))
        b = self.bw(lax.slice_in_dim(middle, half, width, axis=axis))
        for step in range(size // 2 - 1, 0, -1):
            left, right = parts[step], parts[size - step]
            if step == size // 2 - 1:
                f = jnp.concatenate(
                    [
                        add16(lax.slice_in_dim(left, 0, half, axis=axis), f),
                        lax.slice_in_dim(left, half, width, axis=axis),
                    ],
                    axis,
                )
                b = jnp.concatenate(
                    [
                        lax.slice_in_dim(right, 0, half, axis=axis),
                        add16(lax.slice_in_dim(right, half, width, axis=axis), b),
                    ],
                    axis,
                )
            else:
                f, b = add16(left, f), add16(right, b)
            f, b = self.fw(f), self.bw(b)
        return f, b


def add16(one, two):
    return (one.astype(F32) + two.astype(F32)).astype(BF16)


def swap(x, axis, bit, size):
    return lax.ppermute(x, axis, [(i, i ^ bit) for i in range(size)])


def bits_below(size):
    return [1 << k for k in range(size.bit_length() - 1)]


def sum_over(x, axis, bits, size):
    for bit in bits:
        x = x + swap(x, axis, bit, size)
    return x


def run(body, meta, grid, ins, outs, scratch=(), vmem=48, cost=None):
    return pl.pallas_call(
        body,
        grid_spec=pltpu.PrefetchScalarGridSpec(
            num_scalar_prefetch=1,
            grid=grid,
            in_specs=[pl.BlockSpec(b, m) for _, b, m in ins],
            out_specs=[pl.BlockSpec(b, m) for _, _, b, m in outs],
            scratch_shapes=list(scratch),
        ),
        out_shape=[jax.ShapeDtypeStruct(s, d) for s, d, _, _ in outs],
        compiler_params=pltpu.CompilerParams(vmem_limit_bytes=vmem << 20),
        cost_estimate=pl.CostEstimate(
            flops=cost[0], bytes_accessed=cost[1], transcendentals=0
        )
        if cost
        else None,
    )(meta, *[a for a, _, _ in ins])


def whole(x):
    zeros = (0,) * x.ndim
    return (x, x.shape, lambda *_: zeros)


def whole_out(shape, dtype):
    zeros = (0,) * len(shape)
    return (shape, dtype, shape, lambda *_: zeros)


class Sizes:
    def __init__(self, chunks, micro, images):
        self.chunks = chunks
        self.micro = micro
        self.images = images
        self.rows = PIXELS * images
        self.padded = SIDE * 8 * images
        self.live = chunks
        self.batch = 2 * chunks
        self.count = 3 * chunks
        self.planes = 3 * chunks + micro

    def own_count(self, meta):
        batch = meta[self.batch]
        count = meta[self.count]
        for m in range(1, self.micro):
            count = jnp.where(batch == m, meta[self.count + m], count)
        return count.astype(F32)


def split_lanes(value, native):
    for q in range(native.shape[0]):
        native[q] = value[:, q * 128 : (q + 1) * 128]


def to_padded(sz, native, padded):
    n = sz.images
    for q in range(native.shape[0]):
        for i in range(SIDE):
            for j in range(SIDE):
                at = (i * 8 + j) * n
                padded[at : at + n, q * 128 : (q + 1) * 128] = native[
                    q, pl.ds(i * SIDE + j, n, stride=PIXELS), :
                ]
    for i in range(SIDE):
        at = (i * 8 + 7) * n
        padded[at : at + n, :] = jnp.zeros((n, padded.shape[1]), F32)


def to_native(sz, padded, native, out):
    n = sz.images
    for q in range(native.shape[0]):
        for i in range(SIDE):
            for j in range(SIDE):
                at = (i * 8 + j) * n
                native[q, pl.ds(i * SIDE + j, n, stride=PIXELS), :] = padded[
                    at : at + n, q * 128 : (q + 1) * 128
                ]
        out[:, q * 128 : (q + 1) * 128] = native[q].astype(out.dtype)


def row_mask(sz, width, live):
    rows = lax.broadcasted_iota(jnp.int32, (sz.padded, width), 0)
    n = sz.images
    inside = lax.rem(lax.div(rows, n), 8) < SIDE
    if live is None:
        return inside
    return jnp.logical_and(inside, lax.rem(rows, n) < live)


def put_sums(stat, one, two):
    stat[0:1, :] = jnp.sum(one, axis=0, keepdims=True)
    stat[1:2, :] = jnp.sum(two, axis=0, keepdims=True)


def lay_taps(sz, value, strip, taps):
    n = sz.images
    width = strip.shape[1]
    strip[0 : 9 * n, :] = jnp.zeros((9 * n, width), F32)
    strip[65 * n : 74 * n, :] = jnp.zeros((9 * n, width), F32)
    strip[9 * n : 65 * n, :] = value
    for b in range(3):
        taps[b] = strip[b * n : b * n + 72 * n, :].astype(BF16)


def first_body(sz, meta, f, b, own, pre, stat, native):
    split_lanes(f[...].astype(F32) + b[...].astype(F32) + own[0].astype(F32), native)
    to_padded(sz, native, pre)
    value = pre[...]
    kept = jnp.where(row_mask(sz, value.shape[1], meta[sz.live]), value, 0.0)
    put_sums(stat, kept, kept * kept)


def conv_body(sz, meta, pre, stat, params, weight, out, raw, stat_out, taps, strip, total, native):
    step = pl.program_id(0)
    n = sz.images
    width = pre.shape[1]

    @pl.when(step == 0)
    def _():
        average, inv = moments(stat[...], sz.own_count(meta))
        z = params[0:1] * ((pre[...] - average) * inv) + params[1:2]
        act = jnp.where(row_mask(sz, width, None), z * sigmoid(z), 0.0)
        lay_taps(sz, act, strip, taps)
        total[...] = jnp.zeros_like(total)

    at = pl.multiple_of(step * 8 * n, 8 * n)
    for b in range(3):
        total[...] += jnp.dot(
            taps[b, pl.ds(at, sz.padded), :], weight[0, b], preferred_element_type=F32
        )

    @pl.when(step == 2)
    def _():
        value = jnp.where(row_mask(sz, width, None), total[...], 0.0)
        out[...] = value
        to_native(sz, total, native, raw)
        kept = jnp.where(row_mask(sz, width, meta[sz.live]), value, 0.0)
        put_sums(stat_out, kept, kept * kept)


def pick(sz, stat, batch):
    found = stat[0:2]
    for m in range(1, sz.micro):
        found = jnp.where(batch == m, stat[2 * m : 2 * m + 2], found)
    return found


def pick_count(sz, meta, batch):
    count = meta[sz.count]
    for m in range(1, sz.micro):
        count = jnp.where(batch == m, meta[sz.count + m], count)
    return count.astype(F32)


def add_sums(sz, stat, batch, one, two):
    sums = jnp.concatenate(
        [jnp.sum(one, axis=0, keepdims=True), jnp.sum(two, axis=0, keepdims=True)], axis=0
    )
    for m in range(sz.micro):
        stat[2 * m : 2 * m + 2, :] += jnp.where(batch == m, sums, 0.0)


def stage_piece(pieces, place, step):
    for k, piece in enumerate(pieces):

        @pl.when(step == k)
        def _(piece=piece):
            if len(piece) == 1:
                place[...] = piece[0][...]
            else:
                half = piece[0].shape[1]
                place[:, :half] = piece[0][...]
                place[:, half:] = piece[1][...]


def split_refs(layout, refs):
    pieces, at = [], 0
    for many in layout:
        pieces.append(refs[at : at + many])
        at += many
    return pieces, refs[at:]


def expand_body(sz, layout, meta, *refs):
    pieces, rest = split_refs(layout, refs)
    stat, params, weight, act, pre, stat_out, place = rest
    step = pl.program_id(0)
    stage_piece(pieces, place, step)
    batch = meta[sz.batch + step]
    average, inv = moments(pick(sz, stat[...], batch), pick_count(sz, meta, batch))
    z = params[2:3] * ((place[...].astype(F32) - average) * inv) + params[3:4]
    acted = (z * sigmoid(z)).astype(BF16)
    act[0] = acted
    value = jnp.dot(acted, weight[...], preferred_element_type=F32)
    pre[0] = value

    @pl.when(step == 0)
    def _():
        stat_out[...] = jnp.zeros_like(stat_out)

    rows = lax.broadcasted_iota(jnp.int32, value.shape, 0)
    kept = jnp.where(rows < PIXELS * meta[sz.live + step], value, 0.0)
    add_sums(sz, stat_out, batch, kept, kept * kept)


def out_body(sz, meta, pre, stat, params, x, cot, out, grad, stat_out):
    step = pl.program_id(0)
    batch = meta[sz.batch + step]
    average, inv = moments(pick(sz, stat[...], batch), pick_count(sz, meta, batch))
    normed = (pre[0] - average) * inv
    summed = params[0:1] * normed + params[1:2] + x[0].astype(F32)
    sigma = sigmoid(summed)
    rows = lax.broadcasted_iota(jnp.int32, summed.shape, 0)
    live = rows < PIXELS * meta[sz.live + step]
    out[0] = jnp.where(live, summed * sigma, 0.0)
    upstream = jnp.where(
        live, cot[0].astype(F32) * (sigma * (1.0 + summed * (1.0 - sigma))), 0.0
    )
    grad[0] = upstream

    @pl.when(step == 0)
    def _():
        stat_out[...] = jnp.zeros_like(stat_out)

    add_sums(sz, stat_out, batch, upstream, upstream * normed)


def shrink_body(sz, meta, pre, stat, params, grad, sums, weight, back, part):
    step = pl.program_id(0)
    batch = meta[sz.batch + step]
    count = pick_count(sz, meta, batch)
    average, inv = moments(pick(sz, stat[...], batch), count)
    both = pick(sz, sums[...], batch)
    normed = (pre[0] - average) * inv
    rows = lax.broadcasted_iota(jnp.int32, normed.shape, 0)
    live = rows < PIXELS * meta[sz.live + step]
    value = params[0:1] * inv * (grad[0] - (both[0:1] + normed * both[1:2]) / count)
    value = jnp.where(live, value, 0.0).astype(BF16)
    back[0] = value
    part[0] = lax.dot_general(
        value, weight[...], (((1,), (1,)), ((), ())), preferred_element_type=F32
    ).astype(BF16)


def middle_up_body(sz, meta, f, b, own, pre, stat, params, up, stat_out, native, padded):
    split_lanes(f[...].astype(F32) + b[...].astype(F32) + own[0].astype(F32), native)
    to_padded(sz, native, padded)
    average, inv = moments(stat[...], sz.own_count(meta))
    normed = (pre[...] - average) * inv
    z = params[2:3] * normed + params[3:4]
    value = jnp.where(
        row_mask(sz, pre.shape[1], meta[sz.live]), padded[...] * silu_slope(z), 0.0
    )
    up[...] = value
    put_sums(stat_out, value, value * normed)


def conv_back_body(
    sz,
    meta,
    up,
    sums,
    pre_two,
    stat_two,
    pre_one,
    stat_one,
    params,
    weight,
    back,
    up_one,
    stat_out,
    strip,
    taps,
    total,
):
    step = pl.program_id(0)
    n = sz.images
    width = up.shape[1]

    @pl.when(step == 0)
    def _():
        count = sz.own_count(meta)
        average, inv = moments(stat_two[...], count)
        normed = (pre_two[...] - average) * inv
        value = params[2:3] * inv * (up[...] - (sums[0:1] + normed * sums[1:2]) / count)
        value = jnp.where(row_mask(sz, width, meta[sz.live]), value, 0.0)
        back[...] = value.astype(BF16)
        lay_taps(sz, value, strip, taps)
        total[...] = jnp.zeros_like(total)

    at = pl.multiple_of((2 - step) * 8 * n, 8 * n)
    for b in range(3):
        total[...] += lax.dot_general(
            taps[2 - b, pl.ds(at, sz.padded), :],
            weight[0, b],
            (((1,), (1,)), ((), ())),
            preferred_element_type=F32,
        )

    @pl.when(step == 2)
    def _():
        average, inv = moments(stat_one[...], sz.own_count(meta))
        normed = (pre_one[...] - average) * inv
        z = params[0:1] * normed + params[1:2]
        value = jnp.where(
            row_mask(sz, width, meta[sz.live]), total[...] * silu_slope(z), 0.0
        )
        up_one[...] = value
        put_sums(stat_out, value, value * normed)


def first_back_body(sz, meta, up, sums, pre, stat, params, back, padded, native):
    count = sz.own_count(meta)
    average, inv = moments(stat[...], count)
    normed = (pre[...] - average) * inv
    value = params[0:1] * inv * (up[...] - (sums[0:1] + normed * sums[1:2]) / count)
    padded[...] = jnp.where(row_mask(sz, pre.shape[1], meta[sz.live]), value, 0.0)
    to_native(sz, padded, native, back)


def input_body(sz, layout, meta, *refs):
    pieces, rest = split_refs(layout, refs)
    grad, x, weight, out, grad_weight, place, total = rest
    step = pl.program_id(0)
    stage_piece(pieces, place, step)
    value = place[...]
    out[0] = grad[0] + lax.dot_general(
        value, weight[...], (((1,), (1,)), ((), ())), preferred_element_type=F32
    )

    @pl.when(step == 0)
    def _():
        total[...] = jnp.zeros_like(total)

    total[...] += lax.dot_general(
        x[0], value, (((0,), (0,)), ((), ())), preferred_element_type=F32
    )

    @pl.when(step == sz.chunks - 1)
    def _():
        grad_weight[...] = total[...].astype(BF16)


def middle_grad_body(sz, dp, meta, taps, back, out, whole_grad):
    step = pl.program_id(0)
    n = sz.images
    at = pl.multiple_of(lax.div(step, 3) * 8 * n, 8 * n)
    window = taps[lax.rem(step, 3), pl.ds(at, sz.padded), :]
    value = lax.dot_general(
        window, back[...], (((0,), (0,)), ((), ())), preferred_element_type=F32
    )
    lanes = value.shape[1] // dp
    for d in range(dp):
        whole_grad[d] = value[:, d * lanes : (d + 1) * lanes]
    depth = value.shape[0] // sz.chunks
    for p in range(dp):
        for k in range(sz.chunks):
            at = pl.multiple_of(meta[k] * depth, depth)
            out[p, k, 0] = whole_grad[meta[sz.planes + p], pl.ds(at, depth), :].astype(BF16)


def assemble_body(sz, half, meta, near, far, out):
    @pl.when(pl.program_id(0) < half)
    def _():
        out[...] = near[0, 0]

    @pl.when(pl.program_id(0) >= half)
    def _():
        out[...] = far[0, 0]


def last_assemble_body(meta, blocks, out):
    lanes = blocks.shape[3]
    for b in range(blocks.shape[1]):
        out[:, b * lanes : (b + 1) * lanes] = blocks[0, b]


def copy_body(meta, source, out):
    out[...] = source[...]


def reorder(sz, meta, x, inward):
    rest = x.shape[2:]

    def ordered(p, k, meta):
        return (p, k) + (0,) * len(rest)

    def placed(p, k, meta):
        return (meta[sz.planes + p], meta[k]) + (0,) * len(rest)

    (moved,) = run(
        copy_body,
        meta,
        x.shape[:2],
        [(x, (1, 1) + rest, placed if inward else ordered)],
        [(x.shape, x.dtype, (1, 1) + rest, ordered if inward else placed)],
        vmem=16,
    )
    return moved


def last_grad_body(sz, meta, act, back, out, total):
    step = pl.program_id(0)

    @pl.when(step == 0)
    def _():
        total[...] = jnp.zeros_like(total)

    total[...] += lax.dot_general(
        act[0], back[0], (((0,), (0,)), ((), ())), preferred_element_type=F32
    )

    @pl.when(step == sz.chunks - 1)
    def _():
        depth = out.shape[1]
        for k in range(sz.chunks):
            at = pl.multiple_of(meta[k] * depth, depth)
            out[k] = total[pl.ds(at, depth), :].astype(BF16)


def pieces_in(sz, pieces):
    ins, layout = [], []
    for piece in pieces:
        parts = piece if isinstance(piece, tuple) else (piece,)
        layout.append(len(parts))
        ins += [whole(p) for p in parts]
    return ins, layout


def local(
    dp,
    chan,
    inputs,
    cotangent,
    w_first,
    first_m,
    first_v,
    w_middle,
    middle_m,
    middle_v,
    w_last,
    last_m,
    last_v,
    mid_params,
    mid_m,
    mid_v,
    out_params,
    out_m,
    out_v,
    image_counts,
):
    ring = Ring(chan)
    d = lax.axis_index("dp")
    c = lax.axis_index("chan")
    micro, pixels, deep = inputs.shape
    images = micro * pixels // PIXELS // chan
    sz = Sizes(chan, micro, images)
    rows, padded = sz.rows, sz.padded
    per_batch = chan // micro
    depth, lanes = w_middle.shape[2], w_middle.shape[3]
    mid = depth * chan
    half = dp // 2
    last_blocks = w_last.shape[1] // lanes
    own_blocks = deep // lanes
    ratio = last_blocks // own_blocks

    at = lax.dynamic_index_in_dim(jnp.asarray(ring.table), c, keepdims=False)
    batch = at // per_batch
    own_counts = lax.dynamic_index_in_dim(image_counts, d, axis=1, keepdims=False)
    counts_at = own_counts[0]
    for m in range(1, micro):
        counts_at = jnp.where(batch == m, own_counts[m], counts_at)
    live = jnp.clip(counts_at - images * (at % per_batch), 0, images)
    planes = d ^ jnp.asarray([(p % half) * 2 + p // half for p in range(dp)], jnp.int32)
    meta = jnp.concatenate(
        [at, live, batch, PIXELS * jnp.sum(image_counts, axis=1), planes]
    ).astype(jnp.int32)

    first = w_first.astype(BF16)
    for bit in bits_below(dp):
        other = swap(first, "dp", bit, dp)
        first = jnp.where(
            (d & bit) == 0,
            jnp.concatenate([first, other], axis=1),
            jnp.concatenate([other, first], axis=1),
        )
    one = mid_params.astype(BF16)
    left = mid_params - one.astype(F32)
    two = left.astype(BF16)
    three = (left - two.astype(F32)).astype(BF16)
    param_rows = jnp.concatenate([one, two, three], axis=0)
    param_rows = jnp.pad(param_rows, ((0, 4), (0, lanes - depth)))
    low_last = w_last.astype(BF16)
    payload = jnp.concatenate(
        [w_middle.astype(BF16).reshape(TAPS * depth, lanes)]
        + [low_last[:, b * lanes : (b + 1) * lanes] for b in range(last_blocks)]
        + [param_rows],
        axis=0,
    )
    got = ring.gather(payload, 0)
    got[chan // 2] = jnp.concatenate(got[chan // 2], axis=0)
    got = jnp.stack(got)
    mids = got[:, : TAPS * depth]
    lasts = got[:, TAPS * depth : (TAPS + last_blocks) * depth].reshape(
        chan, ratio, own_blocks, depth, lanes
    )
    tail = got[:, (TAPS + last_blocks) * depth :, :depth].astype(F32)
    tail = (tail[:, 8:12] + tail[:, 4:8]) + tail[:, 0:4]
    here = (at[None, :] == jnp.arange(chan)[:, None])[:, :, None, None]
    params = jnp.sum(jnp.where(here, tail[None], 0.0), axis=1)
    params = params.transpose(1, 0, 2).reshape(4, mid)

    near = mids[None]
    for bit in bits_below(dp)[1:]:
        near = jnp.concatenate([near, swap(near, "dp", bit, dp)], axis=0)
    far = swap(near, "dp", 1, dp)
    if lanes % 128 == 0:
        near = near.reshape(half, chan, TAPS, depth, lanes)
        far = far.reshape(half, chan, TAPS, depth, lanes)
        (middle,) = run(
            functools.partial(assemble_body, sz, half),
            meta,
            (dp, chan),
            [
                (
                    near,
                    (1, 1, TAPS, depth, lanes),
                    lambda p, k, meta: (
                        jnp.minimum(p, half - 1),
                        jnp.where(p < half, k, chan - 1),
                        0,
                        0,
                        0,
                    ),
                ),
                (
                    far,
                    (1, 1, TAPS, depth, lanes),
                    lambda p, k, meta: (
                        jnp.maximum(p - half, 0),
                        jnp.where(p < half, 0, k),
                        0,
                        0,
                        0,
                    ),
                ),
            ],
            [
                (
                    (TAPS, mid, mid),
                    BF16,
                    (TAPS, depth, lanes),
                    lambda p, k, meta: (0, meta[k], meta[sz.planes + p]),
                )
            ],
            vmem=16,
            cost=(0, 4 * TAPS * mid * mid),
        )
    else:
        both = jnp.concatenate([near, far], axis=0)
        middle = (
            reorder(sz, meta, both, False)
            .reshape(dp, chan, TAPS, depth, lanes)
            .transpose(2, 1, 3, 0, 4)
            .reshape(TAPS, mid, mid)
        )
    middle = middle.reshape(3, 3, mid, mid)

    own_last = lax.dynamic_index_in_dim(lasts, c % ratio, axis=1, keepdims=False)
    found = jnp.where(d == c // ratio, own_last, jnp.zeros_like(own_last))
    for shift in range(1, dp):
        moves = [
            ((k // ratio) * chan + k, ((k // ratio) ^ shift) * chan + k) for k in range(chan)
        ]
        found = found + lax.ppermute(own_last, ("dp", "chan"), moves)
    (last,) = run(
        last_assemble_body,
        meta,
        (chan,),
        [(found, (1, own_blocks, depth, lanes), lambda k, meta: (k, 0, 0, 0))],
        [((mid, deep), BF16, (depth, deep), lambda k, meta: (meta[k], 0))],
        vmem=16,
        cost=(0, 4 * mid * deep),
    )

    x = inputs.reshape(chan, rows, deep)
    cot = cotangent.reshape(chan, rows, deep)

    def at_place(k, meta):
        return (meta[k], 0, 0)

    def in_order(k, meta):
        return (k, 0, 0)

    def first_part_body(meta, x_ref, weight, out):
        out[0] = jnp.dot(x_ref[0], weight[...], preferred_element_type=F32).astype(BF16)

    (parts,) = run(
        first_part_body,
        meta,
        (chan,),
        [(x, (1, rows, deep), at_place), whole(first)],
        [((chan, rows, mid), BF16, (1, rows, mid), in_order)],
        vmem=16,
        cost=(2 * chan * rows * deep * mid, 2 * chan * rows * (deep + mid)),
    )
    f, b = ring.scatter(parts, 1)

    def head(stack):
        return (stack, (1,) + stack.shape[1:], lambda *_: (0, 0, 0))

    stat_bits = [k for k in bits_below(chan) if k < per_batch]

    def total_rows(stat):
        stat = sum_over(stat, "dp", bits_below(dp), dp)
        return sum_over(stat, "chan", stat_bits, chan)

    def all_batches(stat):
        for bit in bits_below(chan):
            if bit >= per_batch:
                other = swap(stat, "chan", bit, chan)
                stat = jnp.where(
                    (c & bit) == 0,
                    jnp.concatenate([stat, other], axis=0),
                    jnp.concatenate([other, stat], axis=0),
                )
        return stat

    pre_one, stat_one = run(
        functools.partial(first_body, sz),
        meta,
        (1,),
        [whole(f), whole(b), head(parts)],
        [whole_out((padded, mid), F32), whole_out((2, mid), F32)],
        [pltpu.VMEM((mid // 128, rows, 128), F32)],
        vmem=16,
        cost=(10 * padded * mid, 10 * padded * mid),
    )
    stat_one = total_rows(stat_one)

    tap_block = (1, 3, mid, mid)
    conv_flops = 2 * TAPS * padded * mid * mid
    conv_bytes = 2 * TAPS * mid * mid + 16 * padded * mid
    pre_two, raw, stat_two, taps = run(
        functools.partial(conv_body, sz),
        meta,
        (3,),
        [
            whole(pre_one),
            whole(stat_one),
            whole(params),
            (middle, tap_block, lambda s, meta: (s, 0, 0, 0)),
        ],
        [
            whole_out((padded, mid), F32),
            whole_out((rows, mid), BF16),
            whole_out((2, mid), F32),
            whole_out((3, 72 * images, mid), BF16),
        ],
        [
            pltpu.VMEM((74 * images, mid), F32),
            pltpu.VMEM((padded, mid), F32),
            pltpu.VMEM((mid // 128, rows, 128), F32),
        ],
        vmem=32,
        cost=(conv_flops, conv_bytes),
    )
    pieces = ring.gather(raw, 1)
    stat_two = total_rows(stat_two)
    stats_two = all_batches(stat_two)

    ins, layout = pieces_in(sz, pieces)
    act, pre_three, stat_three = run(
        functools.partial(expand_body, sz, layout),
        meta,
        (chan,),
        ins + [whole(stats_two), whole(params), whole(last)],
        [
            ((chan, rows, mid), BF16, (1, rows, mid), in_order),
            ((chan, rows, deep), F32, (1, rows, deep), in_order),
            whole_out((2 * micro, deep), F32),
        ],
        [pltpu.VMEM((rows, mid), BF16)],
        vmem=32,
        cost=(2 * chan * rows * deep * mid, chan * rows * (4 * mid + 4 * deep)),
    )
    stat_three = sum_over(stat_three, "dp", bits_below(dp), dp)
    block_out, grad_summed, sums_three = run(
        functools.partial(out_body, sz),
        meta,
        (chan,),
        [
            (pre_three, (1, rows, deep), in_order),
            whole(stat_three),
            whole(out_params),
            (x, (1, rows, deep), at_place),
            (cot, (1, rows, deep), at_place),
        ],
        [
            ((chan, rows, deep), F32, (1, rows, deep), at_place),
            ((chan, rows, deep), F32, (1, rows, deep), in_order),
            whole_out((2 * micro, deep), F32),
        ],
        vmem=24,
        cost=(20 * chan * rows * deep, 16 * chan * rows * deep),
    )
    sums_three = sum_over(sums_three, "dp", bits_below(dp), dp)
    back_last, back_parts = run(
        functools.partial(shrink_body, sz),
        meta,
        (chan,),
        [
            (pre_three, (1, rows, deep), in_order),
            whole(stat_three),
            whole(out_params),
            (grad_summed, (1, rows, deep), in_order),
            whole(sums_three),
            whole(last),
        ],
        [
            ((chan, rows, deep), BF16, (1, rows, deep), in_order),
            ((chan, rows, mid), BF16, (1, rows, mid), in_order),
        ],
        vmem=24,
        cost=(2 * chan * rows * deep * mid, chan * rows * (2 * mid + 10 * deep)),
    )
    f, b = ring.scatter(back_parts, 1)

    (grad_last,) = run(
        functools.partial(last_grad_body, sz),
        meta,
        (chan,),
        [(act, (1, rows, mid), in_order), (back_last, (1, rows, deep), in_order)],
        [whole_out((chan, depth, deep), BF16)],
        [pltpu.VMEM((mid, deep), F32)],
        vmem=16,
        cost=(2 * chan * rows * deep * mid, 2 * chan * rows * (mid + deep)),
    )
    for bit in bits_below(dp):
        grad_last = add16(grad_last, swap(grad_last, "dp", bit, dp))
    held = [
        jnp.where(c % ratio == r, grad_last, jnp.zeros_like(grad_last)) for r in range(ratio)
    ]
    held = jnp.concatenate(held, axis=2)
    held = jnp.where(d == c // ratio, held, jnp.zeros_like(held))
    last_f, last_b = ring.scatter(held, 1)
    owned_last = held[0].astype(F32) + last_f.astype(F32) + last_b.astype(F32)

    up_two, sums_two = run(
        functools.partial(middle_up_body, sz),
        meta,
        (1,),
        [
            whole(f),
            whole(b),
            head(back_parts),
            whole(pre_two),
            whole(stat_two),
            whole(params),
        ],
        [whole_out((padded, mid), F32), whole_out((2, mid), F32)],
        [pltpu.VMEM((mid // 128, rows, 128), F32), pltpu.VMEM((padded, mid), F32)],
        vmem=16,
        cost=(20 * padded * mid, 14 * padded * mid),
    )
    sums_two = total_rows(sums_two)
    back_two, up_one, sums_one = run(
        functools.partial(conv_back_body, sz),
        meta,
        (3,),
        [
            whole(up_two),
            whole(sums_two),
            whole(pre_two),
            whole(stat_two),
            whole(pre_one),
            whole(stat_one),
            whole(params),
            (middle, tap_block, lambda s, meta: (s, 0, 0, 0)),
        ],
        [
            whole_out((padded, mid), BF16),
            whole_out((padded, mid), F32),
            whole_out((2, mid), F32),
        ],
        [
            pltpu.VMEM((74 * images, mid), F32),
            pltpu.VMEM((3, 72 * images, mid), BF16),
            pltpu.VMEM((padded, mid), F32),
        ],
        vmem=32,
        cost=(conv_flops, conv_bytes),
    )
    sums_one = total_rows(sums_one)
    (back_one,) = run(
        functools.partial(first_back_body, sz),
        meta,
        (1,),
        [whole(up_one), whole(sums_one), whole(pre_one), whole(stat_one), whole(params)],
        [whole_out((rows, mid), BF16)],
        [pltpu.VMEM((padded, mid), F32), pltpu.VMEM((mid // 128, rows, 128), F32)],
        vmem=16,
        cost=(10 * padded * mid, 10 * padded * mid),
    )
    pieces = ring.gather(back_one, 1)

    if lanes % 128 == 0:
        (grad_middle,) = run(
            functools.partial(middle_grad_body, sz, dp),
            meta,
            (TAPS,),
            [whole(taps), whole(back_two)],
            [
                (
                    (dp, chan, TAPS, depth, lanes),
                    BF16,
                    (dp, chan, 1, depth, lanes),
                    lambda s, meta: (0, 0, s, 0, 0),
                )
            ],
            [pltpu.VMEM((dp, mid, lanes), F32)],
            vmem=32,
            cost=(conv_flops, conv_bytes),
        )
    else:

        def plain_grad_body(meta, taps, back, out):
            step = pl.program_id(0)
            start = pl.multiple_of(lax.div(step, 3) * 8 * images, 8 * images)
            window = taps[lax.rem(step, 3), pl.ds(start, padded), :]
            out[0] = lax.dot_general(
                window, back[...], (((0,), (0,)), ((), ())), preferred_element_type=F32
            ).astype(BF16)

        (grad_middle,) = run(
            plain_grad_body,
            meta,
            (TAPS,),
            [whole(taps), whole(back_two)],
            [((TAPS, mid, mid), BF16, (1, mid, mid), lambda s, meta: (s, 0, 0))],
            vmem=32,
            cost=(conv_flops, conv_bytes),
        )
        grad_middle = grad_middle.reshape(TAPS, chan, depth, dp, lanes).transpose(3, 1, 0, 2, 4)
        grad_middle = reorder(sz, meta, grad_middle, True)
    kept = grad_middle.reshape(dp, chan, TAPS * depth, lanes)
    for bit in [1] + bits_below(dp)[:0:-1]:
        cut = kept.shape[0] // 2
        kept = add16(kept[:cut], swap(kept[cut:], "dp", bit, dp))
    kept = kept[0]
    middle_f, middle_b = ring.scatter(kept, 0)
    owned_middle = kept[0].astype(F32) + middle_f.astype(F32) + middle_b.astype(F32)
    owned_middle = owned_middle.reshape(3, 3, depth, lanes)

    ins, layout = pieces_in(sz, pieces)
    input_grad, grad_first = run(
        functools.partial(input_body, sz, layout),
        meta,
        (chan,),
        ins
        + [
            (grad_summed, (1, rows, deep), in_order),
            (x, (1, rows, deep), at_place),
            whole(first),
        ],
        [
            ((chan, rows, deep), F32, (1, rows, deep), at_place),
            whole_out((deep, mid), BF16),
        ],
        [pltpu.VMEM((rows, mid), BF16), pltpu.VMEM((deep, mid), F32)],
        vmem=32,
        cost=(4 * chan * rows * deep * mid, chan * rows * (2 * mid + 10 * deep)),
    )
    owned_first = scatter_columns(grad_first, d, dp)

    sums_first, sums_middle = all_batches(sums_one), all_batches(sums_two)

    def over_batches(stat, row):
        total = stat[row]
        for m in range(1, micro):
            total = total + stat[2 * m + row]
        return total

    grad_mid = jnp.stack(
        [
            over_batches(sums_first, 1),
            over_batches(sums_first, 0),
            over_batches(sums_middle, 1),
            over_batches(sums_middle, 0),
        ]
    )
    grad_mid = lax.dynamic_slice_in_dim(grad_mid, c * depth, depth, axis=1)
    grad_out = jnp.stack([over_batches(sums_three, 1), over_batches(sums_three, 0)])

    return (
        block_out.reshape(inputs.shape),
        input_grad.reshape(inputs.shape),
        *adamw(w_first, owned_first, first_m, first_v, rate_first),
        *adamw(w_middle, owned_middle, middle_m, middle_v, rate_middle),
        *adamw(w_last, owned_last, last_m, last_v, rate_last),
        *adamw(mid_params, grad_mid, mid_m, mid_v, rate_norm),
        *adamw(out_params, grad_out, out_m, out_v, rate_norm),
    )


def scatter_columns(grad, d, dp):
    blocks = grad.reshape(grad.shape[0], dp, grad.shape[1] // dp)
    kept = [blocks[:, p] for p in range(dp)]
    for bit in bits_below(dp):
        kept = [
            jnp.where((d & bit) == 0, kept[q], kept[q ^ bit]) for q in range(len(kept))
        ]
    todo = {q: kept[q] for q in range(dp)}
    for bit in [1] + bits_below(dp)[:0:-1]:
        send = sorted(q for q in todo if q & bit)
        stay = sorted(q for q in todo if not q & bit)
        got = swap(jnp.stack([todo[q] for q in send]), "dp", bit, dp)
        todo = {
            q: todo[q].astype(F32) + got[send.index(q | bit)].astype(F32) for q in stay
        }
        if len(todo) > 1:
            todo = {q: v.astype(BF16) for q, v in todo.items()}
    return todo[0]


def solution(mesh):
    rows = P(None, "dp", "chan")
    flat = P("chan", "dp")
    square = P(None, None, "chan", "dp")
    vector = P(None, "chan")
    state = (flat,) * 3 + (square,) * 3 + (flat,) * 3 + (vector,) * 6
    return jax.shard_map(
        functools.partial(local, mesh.shape["dp"], mesh.shape["chan"]),
        mesh=mesh,
        in_specs=(rows, rows) + state + (P(),),
        out_specs=(rows, rows) + state,
        check_vma=False,
    )
```

time: 1130 us -> 379 us (0.34)
  waiting for transfers between devices: 831 us -> 175 us
  starting transfers between devices: 1.54 us -> 96.2 us
  local copies, waits for them, and re-layouts: 103 us -> 23.5 us
  matrix products: 65.2 us -> 0 us
  blocking collectives: 59.3 us -> 0 us
  Pallas kernels: 0 us -> 59 us
  other arithmetic: 49.4 us -> 22.7 us
  between operations: 16.3 us -> 1.77 us
    reduce_scatter x8 -> x0, waiting for transfers between devices: 492 us -> none  [the longest x2 235 us: local(): lax.psum_scatter(jnp.dot(act_middle, last_all, preferred_element_type=jnp...]
    all_gather x6 -> x0, waiting for transfers between devices: 337 us -> none  [the longest x2 195 us: local(): grad_last_whole = lax.all_gather(grad_pre_last, 'chan', axis=1, tiled=True)]
    ppermute x0 -> x92, waiting for transfers between devices: none -> 175 us  [the longest x28 66.1 us: fw(): return lax.ppermute(x, 'chan', self.ahead)]
    ppermute x0 -> x92, starting transfers between devices: none -> 96.2 us  [the longest x28 30.2 us: fw(): return lax.ppermute(x, 'chan', self.ahead)]
    dot_general x18 -> x0, matrix products: 65.2 us -> none  [the longest x6 24.3 us: cross_cols(): lax.dot_general(left, right, (((1,), (1,)), ((), ())), preferred_element_...]
    pallas_call x0 -> x14, Pallas kernels: none -> 59 us  [run(): pl.pallas_call(body, grid_spec=pltpu.PrefetchScalarGridSpec(num_scalar_pr...]
    psum x6 -> x0, blocking collectives: 38.2 us -> none  [the longest x3 20.4 us: norm_back(): lax.psum((jnp.sum(upstream, axis=0), jnp.sum(upstream * normed, axis=0)),...]
    concatenate x34 -> x1, local copies, waits for them, and re-layouts: 25.6 us -> 0.08 us  [local(): jnp.concatenate([at, live, batch, PIXELS * jnp.sum(image_counts, axis=1),...]
  transfers between devices with their start and end apart: 15 -> 92, of which waited for: 13 -> 52; matrix products, arithmetic and copies ran while one was open for 13% -> 7% of each run, Pallas kernels for 0% -> 5%
where the time goes in v1:
time: 379 us; the launch traced here: 378 us
  waiting for transfers between devices  175 us (46%)
  starting transfers between devices  96.2 us (25%)
  Pallas kernels  59 us (16%)
  local copies, waits for them, and re-layouts  23.5 us (6%)
  other arithmetic  22.7 us (6%)
    ppermute x28, waiting for transfers between devices, fw(): return lax.ppermute(x, 'chan', self.ahead)  66.1 us
    ppermute x28, waiting for transfers between devices, bw(): return lax.ppermute(x, 'chan', self.back)  63.2 us
    pallas_call x14, Pallas kernels, run(): pl.pallas_call(body, grid_spec=pltpu.PrefetchScalarGridSpec(num_scalar_pr...  59 us
    ppermute x33, waiting for transfers between devices, swap(): return lax.ppermute(x, axis, [(i, i ^ bit) for i in range(size)])  46.1 us
    ppermute x28, starting transfers between devices, fw(): return lax.ppermute(x, 'chan', self.ahead)  30.2 us
    ppermute x28, starting transfers between devices, bw(): return lax.ppermute(x, 'chan', self.back)  30 us
    ppermute x33, starting transfers between devices, swap(): return lax.ppermute(x, axis, [(i, i ^ bit) for i in range(size)])  28.3 us
    unnamed x93, local copies, waits for them, and re-layouts  11.4 us
  transfers between devices with their start and end apart: 92, of which 52 were waited for; matrix products, arithmetic and copies ran while one was open for 7% of the time, Pallas kernels for 5%

profile of v1, /device:TPU:0, one launch (start us, length us, event | category | flops | bytes accessed | tf_op | source)
XLA Modules:
  0.0 378.5 jit_solution(5381871551756529046)
XLA Ops:
  15.2 4.1 %collective-permute-done.1 = bf16[256,256]{1,0:T(8,128)(2,1)S(1)} collective-permute-done((bf16[256,256]{1,0:T(8,128)(2,1)S(1)}, bf16[256,256]{1,0:T(8,128)(2,1)S(1)}, u32[]{:S(2)}, u32[]{:S(2)}) %collective-permute-start.1) | collective-permute-done | bytes 131104 | tf_op jit(solution)/shard_map/ppermute | solution.py:132
  26.1 7.6 %collective-permute-done.15 = bf16[848,128]{1,0:T(8,128)(2,1)S(1)} collective-permute-done((bf16[848,128]{1,0:T(8,128)(2,1)S(1)}, bf16[848,128]{1,0:T(8,128)(2,1)S(1)}, u32[]{:S(2)}, u32[]{:S(2)}) %collective-permute-start.15) | collective-permute-done | bytes 217120 | tf_op jit(solution)/shard_map/ppermute | solution.py:82
  35.7 4.1 %collective-permute-done.16 = bf16[848,128]{1,0:T(8,128)(2,1)S(1)} collective-permute-done((bf16[848,128]{1,0:T(8,128)(2,1)S(1)}, bf16[848,128]{1,0:T(8,128)(2,1)S(1)}, u32[]{:S(2)}, u32[]{:S(2)}) %collective-permute-start.16) | collective-permute-done | bytes 217120 | tf_op jit(solution)/shard_map/ppermute | solution.py:82
  51.6 5.6 %collective-permute-done.2 = bf16[392,256]{1,0:T(8,128)(2,1)S(1)} collective-permute-done((bf16[392,256]{1,0:T(8,128)(2,1)S(1)}, bf16[392,256]{1,0:T(8,128)(2,1)S(1)}, u32[]{:S(2)}, u32[]{:S(2)}) %collective-permute-start.2) | collective-permute-done | bytes 200736 | tf_op jit(solution)/shard_map/ppermute | solution.py:79
  61.6 10.9 %collective-permute-done.22 = bf16[1,8,576,128]{3,2,1,0:T(8,128)(2,1)S(1)} collective-permute-done((bf16[1,8,576,128]{3,2,1,0:T(8,128)(2,1)S(1)}, bf16[1,8,576,128]{3,2,1,0:T(8,128)(2,1)S(1)}, u32[]{:S(2)}, u32[]{:S(2)}) %collective-permute-start.22) | collective-permute-done | bytes 1179680 | tf_op jit(solution)/shard_map/ppermute | solution.py:132
  76.6 9.7 %collective-permute-done.4 = bf16[392,512]{1,0:T(8,128)(2,1)S(1)} collective-permute-done((bf16[392,512]{1,0:T(8,128)(2,1)S(1)}, bf16[392,512]{1,0:T(8,128)(2,1)S(1)}, u32[]{:S(2)}, u32[]{:S(2)}) %collective-permute-start.4) | collective-permute-done | bytes 401440 | tf_op jit(solution)/shard_map/ppermute | solution.py:79
  86.7 10.6 %collective-permute-done.5.f = bf16[392,512]{1,0:T(8,128)(2,1)S(1)} collective-permute-done((bf16[392,512]{1,0:T(8,128)(2,1)S(1)}, bf16[392,512]{1,0:T(8,128)(2,1)S(1)}, u32[]{:S(2)}, u32[]{:S(2)}) %collective-permute-start.5) | collective-permute-done | bytes 401440 | tf_op jit(solution)/shard_map/ppermute | solution.py:79
  110.5 10.5 %shard_map.325 = bf16[9,512,512]{2,1,0:T(8,128)(2,1)S(1)} custom-call(s32[30]{0:T(128)S(1)} %concatenate.79.meta, bf16[2,8,9,64,128]{4,3,2,1,0:T(8,128)(2,1)S(1)} %pad_maximum_fusion.near, bf16[2,8,9,64,128]{4,3,2,1,0:T(8,128)(2,1)} %bitcast.24.far), custom_call_target="tpu_custom_call" | custom-call | bytes 9437184 | tf_op jit(solution)/shard_map/pallas_call | solution.py:146
  121.1 4.0 %shard_map.326 = (f32[448,512]{1,0:T(8,128)S(1)}, bf16[392,512]{1,0:T(8,128)(2,1)S(1)}, f32[2,512]{1,0:T(2,128)S(1)}, bf16[3,576,512]{2,1,0:T(8,128)(2,1)S(1)}) custom-call(s32[30]{0:T(128)S(1)} %concatenate.79.meta, f32[448,512]{1,0:T(8,128)S(1)} %get-tuple-element.38.pre.pre_one, f32[2,512]{1,0:T(2,128)S(1)} %add.323.stat.stat_one, ...), custom_call_target="tpu_custom_call" | custom-call | flops 2113929216 | bytes 8388608 | tf_op jit(solution)/shard_map/pallas_call | solution.py:146
  130.1 6.5 %collective-permute-done.27.refs_8_ = bf16[392,512]{1,0:T(8,128)(2,1)S(1)} collective-permute-done((bf16[392,512]{1,0:T(8,128)(2,1)S(1)}, bf16[392,512]{1,0:T(8,128)(2,1)S(1)}, u32[]{:S(2)}, u32[]{:S(2)}) %collective-permute-start.27) | collective-permute-done | bytes 401440 | tf_op jit(solution)/shard_map/ppermute | solution.py:79
  140.1 6.0 %collective-permute-done.28.refs_7_ = bf16[392,512]{1,0:T(8,128)(2,1)} collective-permute-done((bf16[392,512]{1,0:T(8,128)(2,1)S(1)}, bf16[392,512]{1,0:T(8,128)(2,1)}, u32[]{:S(2)}, u32[]{:S(2)}) %collective-permute-start.28) | collective-permute-done | bytes 401440 | tf_op jit(solution)/shard_map/ppermute | solution.py:79
  177.0 6.7 %shard_map.328 = (bf16[8,392,512]{2,1,0:T(8,128)(2,1)S(1)}, f32[8,392,256]{2,1,0:T(8,128)S(1)}, f32[4,256]{1,0:T(4,128)S(1)}) custom-call(s32[30]{0:T(128)S(1)} %concatenate.79.meta, bf16[392,512]{1,0:T(8,128)(2,1)S(1)} %copy-done.12, bf16[392,512]{1,0:T(8,128)(2,1)S(1)} %copy-done.16, bf16[392,512]{1,0:T(8,128)(2,1)} %collective-permute-done.25.refs_2_, ...), custom_call_target="tpu_custom_call" | custom-call | flops 822083584 | bytes 9633792 | tf_op jit(solution)/shard_map/pallas_call | solution.py:146
  188.6 5.2 %shard_map.329 = (f32[8,392,256]{2,1,0:T(8,128)}, f32[8,392,256]{2,1,0:T(8,128)S(1)}, f32[4,256]{1,0:T(4,128)S(1)}) custom-call(s32[30]{0:T(128)S(1)} %concatenate.79.meta, f32[8,392,256]{2,1,0:T(8,128)S(1)} %get-tuple-element.42.pre, f32[4,256]{1,0:T(4,128)S(1)} %add.336.stat, f32[2,256]{1,0:T(2,128)S(1)} %copy-done.17, bf16[8,392,256]{2,1,0:T(8,128)(2,1)S(1)} %bitcast.197, ...), custom_call_target="tpu_custom_call" | custom-call | flops 16056320 | bytes 12845056 | tf_op jit(solution)/shard_map/pallas_call | solution.py:146
  210.1 7.1 %collective-permute-done.49 = bf16[392,512]{1,0:T(8,128)(2,1)S(1)} collective-permute-done((bf16[392,512]{1,0:T(8,128)(2,1)S(1)}, bf16[392,512]{1,0:T(8,128)(2,1)S(1)}, u32[]{:S(2)}, u32[]{:S(2)}) %collective-permute-start.49) | collective-permute-done | bytes 401440 | tf_op jit(solution)/shard_map/ppermute | solution.py:82
  218.0 7.8 %collective-permute-done.50 = bf16[392,512]{1,0:T(8,128)(2,1)S(1)} collective-permute-done((bf16[392,512]{1,0:T(8,128)(2,1)S(1)}, bf16[392,512]{1,0:T(8,128)(2,1)S(1)}, u32[]{:S(2)}, u32[]{:S(2)}) %collective-permute-start.50) | collective-permute-done | bytes 401440 | tf_op jit(solution)/shard_map/ppermute | solution.py:82
  236.6 6.5 %collective-permute-done.51.b = bf16[392,512]{1,0:T(8,128)(2,1)S(1)} collective-permute-done((bf16[392,512]{1,0:T(8,128)(2,1)S(1)}, bf16[392,512]{1,0:T(8,128)(2,1)S(1)}, u32[]{:S(2)}, u32[]{:S(2)}) %collective-permute-start.51) | collective-permute-done | bytes 401440 | tf_op jit(solution)/shard_map/ppermute | solution.py:82
  262.9 4.2 %shard_map.332 = (bf16[448,512]{1,0:T(8,128)(2,1)S(1)}, f32[448,512]{1,0:T(8,128)S(1)}, f32[2,512]{1,0:T(2,128)S(1)}) custom-call(s32[30]{0:T(128)S(1)} %concatenate.79.meta, f32[448,512]{1,0:T(8,128)S(1)} %copy-done.19, f32[2,512]{1,0:T(2,128)S(1)} %add.348.sums, f32[448,512]{1,0:T(8,128)S(1)} %copy-done.10, f32[2,512]{1,0:T(2,128)S(1)} %add.329.stat.stat_two, ...), custom_call_target="tpu_custom_call" | custom-call | flops 2113929216 | bytes 8388608 | tf_op jit(solution)/shard_map/pallas_call | solution.py:146
  268.0 5.6 %shard_map.335 = bf16[4,8,9,64,128]{4,3,2,1,0:T(8,128)(2,1)S(1)} custom-call(s32[30]{0:T(128)S(1)} %concatenate.79.meta, bf16[3,576,512]{2,1,0:T(8,128)(2,1)S(1)} %copy-done.21, bf16[448,512]{1,0:T(8,128)(2,1)S(1)} %get-tuple-element.56.back), custom_call_target="tpu_custom_call" | custom-call | flops 2113929216 | bytes 8388608 | tf_op jit(solution)/shard_map/pallas_call | solution.py:146
  301.7 5.2 %collective-permute-done.60.refs_1_ = bf16[392,512]{1,0:T(8,128)(2,1)S(1)} collective-permute-done((bf16[392,512]{1,0:T(8,128)(2,1)S(1)}, bf16[392,512]{1,0:T(8,128)(2,1)S(1)}, u32[]{:S(2)}, u32[]{:S(2)}) %collective-permute-start.60) | collective-permute-done | bytes 401440 | tf_op jit(solution)/shard_map/ppermute | solution.py:82
  306.9 3.9 %collective-permute-start.91 = (f32[2,512]{1,0:T(2,128)S(1)}, f32[2,512]{1,0:T(2,128)S(1)}, u32[]{:S(2)}, u32[]{:S(2)}) collective-permute-start(f32[2,512]{1,0:T(2,128)S(1)} %add.348.sums), channel_id=1, source_target_pairs={{0,4},{1,5},{2,6},{3,7},{4,0},{5,1},{6,2},{7,3},{8,12},{9,13},{10,... | collective-permute-start | bytes 12296 | tf_op jit(solution)/shard_map/ppermute | solution.py:132
  318.0 4.1 %collective-permute-done.61.refs_2_ = bf16[392,512]{1,0:T(8,128)(2,1)S(1)} collective-permute-done((bf16[392,512]{1,0:T(8,128)(2,1)S(1)}, bf16[392,512]{1,0:T(8,128)(2,1)S(1)}, u32[]{:S(2)}, u32[]{:S(2)}) %collective-permute-start.61) | collective-permute-done | bytes 401440 | tf_op jit(solution)/shard_map/ppermute | solution.py:82
  324.5 7.7 %collective-permute-done.65.refs_6_ = bf16[392,512]{1,0:T(8,128)(2,1)S(1)} collective-permute-done((bf16[392,512]{1,0:T(8,128)(2,1)S(1)}, bf16[392,512]{1,0:T(8,128)(2,1)S(1)}, u32[]{:S(2)}, u32[]{:S(2)}) %collective-permute-start.65) | collective-permute-done | bytes 401440 | tf_op jit(solution)/shard_map/ppermute | solution.py:79
  340.3 8.8 %shard_map.334 = (f32[8,392,256]{2,1,0:T(8,128)}, bf16[256,512]{1,0:T(8,128)(2,1)S(1)}) custom-call(s32[30]{0:T(128)S(1)} %concatenate.79.meta, bf16[392,512]{1,0:T(8,128)(2,1)S(1)} %shard_map.333.refs_0_, bf16[392,512]{1,0:T(8,128)(2,1)S(1)} %collective-permute-done.60.refs_1_, bf16[392,512]{1,0:T(8,128)(2,1)S(1)} %collective-permute-done.61.refs_2_, ...), custom_call_target="tpu_custom_call" | custom-call | flops 1644167168 | bytes 11239424 | tf_op jit(solution)/shard_map/pallas_call | solution.py:146
  361.4 4.7 %collective-permute-done.74 = bf16[576,128]{1,0:T(8,128)(2,1)S(1)} collective-permute-done((bf16[576,128]{1,0:T(8,128)(2,1)S(1)}, bf16[576,128]{1,0:T(8,128)(2,1)S(1)}, u32[]{:S(2)}, u32[]{:S(2)}) %collective-permute-start.74) | collective-permute-done | bytes 147488 | tf_op jit(solution)/shard_map/ppermute | solution.py:79
  (388 shorter events, 219.7 us)
Async XLA Ops:
  3.6 20.4 %collective-permute-start.14 = (bf16[848,128]{1,0:T(8,128)(2,1)S(1)}, bf16[848,128]{1,0:T(8,128)(2,1)S(1)}, u32[]{:S(2)}, u32[]{:S(2)}) collective-permute-start(bf16[848,128]{1,0:T(8,128)(2,1)S(1)} %constant_dynamic-update-slice_fusion), channel_id=1, source_target_pairs={{2,0},{4,2},{6,4},{7,6},{5,7},{3,5},{1,3},{0,1},{10,8},{12,10},{14... | collective-permute-start | bytes 651272 | tf_op jit(solution)/shard_map/ppermute | solution.py:82
  6.5 19.0 %collective-permute-start.17 = (bf16[848,128]{1,0:T(8,128)(2,1)S(1)}, bf16[848,128]{1,0:T(8,128)(2,1)S(1)}, u32[]{:S(2)}, u32[]{:S(2)}) collective-permute-start(bf16[848,128]{1,0:T(8,128)(2,1)S(1)} %constant_dynamic-update-slice_fusion), channel_id=1, source_target_pairs={{0,2},{2,4},{4,6},{6,7},{7,5},{5,3},{3,1},{1,0},{8,10},{10,12},{12... | collective-permute-start | bytes 651272 | tf_op jit(solution)/shard_map/ppermute | solution.py:79
  22.3 27.9 %collective-permute-start.6 = (bf16[392,256]{1,0:T(8,128)(2,1)S(1)}, bf16[392,256]{1,0:T(8,128)(2,1)S(1)}, u32[]{:S(2)}, u32[]{:S(2)}) collective-permute-start(bf16[392,256]{1,0:T(8,128)(2,1)S(1)} %get-tuple-element.113), channel_id=1, source_target_pairs={{2,0},{4,2},{6,4},{7,6},{5,7},{3,5},{1,3},{0,1},{10,8},{12,10},{14... | collective-permute-start | bytes 602120 | tf_op jit(solution)/shard_map/ppermute | solution.py:82
  48.1 24.4 %collective-permute-start.22 = (bf16[1,8,576,128]{3,2,1,0:T(8,128)(2,1)S(1)}, bf16[1,8,576,128]{3,2,1,0:T(8,128)(2,1)S(1)}, u32[]{:S(2)}, u32[]{:S(2)}) collective-permute-start(bf16[1,8,576,128]{3,2,1,0:T(8,128)(2,1)S(1)} %get-tuple-element.95), channel_id=1, source_target_pairs={{0,16},{8,24},{16,0},{24,8},{1,17},{9,25},{17,1},{25,9},{2,18},{10... | collective-permute-start | bytes 3538952 | tf_op jit(solution)/shard_map/ppermute | solution.py:132
  57.3 16.9 %collective-permute-start.3 = (bf16[392,512]{1,0:T(8,128)(2,1)S(1)}, bf16[392,512]{1,0:T(8,128)(2,1)S(1)}, u32[]{:S(2)}, u32[]{:S(2)}) collective-permute-start(bf16[392,512]{1,0:T(8,128)(2,1)S(1)} %pad_maximum_fusion.2), channel_id=1, source_target_pairs={{0,2},{2,4},{4,6},{6,7},{7,5},{5,3},{3,1},{1,0},{8,10},{10,12},{12... | collective-permute-start | bytes 1204232 | tf_op jit(solution)/shard_map/ppermute | solution.py:79
  60.3 13.9 %collective-permute-start.8 = (bf16[392,512]{1,0:T(8,128)(2,1)S(1)}, bf16[392,512]{1,0:T(8,128)(2,1)S(1)}, u32[]{:S(2)}, u32[]{:S(2)}) collective-permute-start(bf16[392,512]{1,0:T(8,128)(2,1)S(1)} %fusion.5), channel_id=1, source_target_pairs={{2,0},{4,2},{6,4},{7,6},{5,7},{3,5},{1,3},{0,1},{10,8},{12,10},{14... | collective-permute-start | bytes 1204232 | tf_op jit(solution)/shard_map/ppermute | solution.py:82
  74.2 36.3 %collective-permute-start.23 = (bf16[2,8,576,128]{3,2,1,0:T(8,128)(2,1)}, bf16[2,8,576,128]{3,2,1,0:T(8,128)(2,1)}, u32[]{:S(2)}, u32[]{:S(2)}) collective-permute-start(bf16[2,8,576,128]{3,2,1,0:T(8,128)(2,1)} %pad_maximum_fusion.1), channel_id=1, source_target_pairs={{0,8},{8,0},{16,24},{24,16},{1,9},{9,1},{17,25},{25,17},{2,10},{10... | collective-permute-start | bytes 7077896 | tf_op jit(solution)/shard_map/ppermute | solution.py:132
  74.5 11.8 %collective-permute-start.4 = (bf16[392,512]{1,0:T(8,128)(2,1)S(1)}, bf16[392,512]{1,0:T(8,128)(2,1)S(1)}, u32[]{:S(2)}, u32[]{:S(2)}) collective-permute-start(bf16[392,512]{1,0:T(8,128)(2,1)S(1)} %get-tuple-element.90), channel_id=1, source_target_pairs={{0,2},{2,4},{4,6},{6,7},{7,5},{5,3},{3,1},{1,0},{8,10},{10,12},{12... | collective-permute-start | bytes 1204232 | tf_op jit(solution)/shard_map/ppermute | solution.py:79
  74.9 11.9 %collective-permute-start.9 = (bf16[392,512]{1,0:T(8,128)(2,1)S(1)}, bf16[392,512]{1,0:T(8,128)(2,1)S(1)}, u32[]{:S(2)}, u32[]{:S(2)}) collective-permute-start(bf16[392,512]{1,0:T(8,128)(2,1)S(1)} %get-tuple-element.89), channel_id=1, source_target_pairs={{2,0},{4,2},{6,4},{7,6},{5,7},{3,5},{1,3},{0,1},{10,8},{12,10},{14... | collective-permute-start | bytes 1204232 | tf_op jit(solution)/shard_map/ppermute | solution.py:82
  86.4 11.0 %collective-permute-start.5 = (bf16[392,512]{1,0:T(8,128)(2,1)S(1)}, bf16[392,512]{1,0:T(8,128)(2,1)S(1)}, u32[]{:S(2)}, u32[]{:S(2)}) collective-permute-start(bf16[392,512]{1,0:T(8,128)(2,1)S(1)} %fusion.8), channel_id=1, source_target_pairs={{0,2},{2,4},{4,6},{6,7},{7,5},{5,3},{3,1},{1,0},{8,10},{10,12},{12... | collective-permute-start | bytes 1204232 | tf_op jit(solution)/shard_map/ppermute | solution.py:79
  138.6 10.7 %collective-permute-start.25 = (bf16[392,512]{1,0:T(8,128)(2,1)S(1)}, bf16[392,512]{1,0:T(8,128)(2,1)}, u32[]{:S(2)}, u32[]{:S(2)}) collective-permute-start(bf16[392,512]{1,0:T(8,128)(2,1)S(1)} %collective-permute-done.24.refs_1_), channel_id=1, source_target_pairs={{2,0},{4,2},{6,4},{7,6},{5,7},{3,5},{1,3},{0,1},{10,8},{12,10},{14... | collective-permute-start | bytes 1204232 | tf_op jit(solution)/shard_map/ppermute | solution.py:82
  146.1 22.0 %collective-permute-start.29 = (bf16[392,512]{1,0:T(8,128)(2,1)}, bf16[392,512]{1,0:T(8,128)(2,1)S(1)}, u32[]{:S(2)}, u32[]{:S(2)}) collective-permute-start(bf16[392,512]{1,0:T(8,128)(2,1)} %collective-permute-done.28.refs_7_), channel_id=1, source_target_pairs={{0,2},{2,4},{4,6},{6,7},{7,5},{5,3},{3,1},{1,0},{8,10},{10,12},{12... | collective-permute-start | bytes 1204232 | tf_op jit(solution)/shard_map/ppermute | solution.py:79
  149.3 18.9 %collective-permute-start.26 = (bf16[392,512]{1,0:T(8,128)(2,1)}, bf16[392,512]{1,0:T(8,128)(2,1)}, u32[]{:S(2)}, u32[]{:S(2)}) collective-permute-start(bf16[392,512]{1,0:T(8,128)(2,1)} %collective-permute-done.25.refs_2_), channel_id=1, source_target_pairs={{2,0},{4,2},{6,4},{7,6},{5,7},{3,5},{1,3},{0,1},{10,8},{12,10},{14... | collective-permute-start | bytes 1204232 | tf_op jit(solution)/shard_map/ppermute | solution.py:82
  231.5 11.7 %collective-permute-start.51 = (bf16[392,512]{1,0:T(8,128)(2,1)S(1)}, bf16[392,512]{1,0:T(8,128)(2,1)S(1)}, u32[]{:S(2)}, u32[]{:S(2)}) collective-permute-start(bf16[392,512]{1,0:T(8,128)(2,1)S(1)} %get-tuple-element.84), channel_id=1, source_target_pairs={{2,0},{4,2},{6,4},{7,6},{5,7},{3,5},{1,3},{0,1},{10,8},{12,10},{14... | collective-permute-start | bytes 1204232 | tf_op jit(solution)/shard_map/ppermute | solution.py:82
  235.9 20.2 %collective-permute-start.81 = (bf16[8,64,256]{2,1,0:T(8,128)(2,1)S(1)}, bf16[8,64,256]{2,1,0:T(8,128)(2,1)S(1)}, u32[]{:S(2)}, u32[]{:S(2)}) collective-permute-start(bf16[8,64,256]{2,1,0:T(8,128)(2,1)S(1)} %add_convert_fusion.2), channel_id=1, source_target_pairs={{0,16},{8,24},{16,0},{24,8},{1,17},{9,25},{17,1},{25,9},{2,18},{10... | collective-permute-start | bytes 786440 | tf_op jit(solution)/shard_map/ppermute | solution.py:132
  277.2 33.6 %collective-permute-start.70 = (bf16[2,8,576,128]{3,2,1,0:T(8,128)(2,1)}, bf16[2,8,576,128]{3,2,1,0:T(8,128)(2,1)}, u32[]{:S(2)}, u32[]{:S(2)}) collective-permute-start(bf16[2,8,576,128]{3,2,1,0:T(8,128)(2,1)} %bitcast.45), channel_id=1, source_target_pairs={{0,8},{8,0},{16,24},{24,16},{1,9},{9,1},{17,25},{25,17},{2,10},{10... | collective-permute-start | bytes 7077896 | tf_op jit(solution)/shard_map/ppermute | solution.py:132
  297.5 13.3 %collective-permute-start.63 = (bf16[392,512]{1,0:T(8,128)(2,1)S(1)}, bf16[392,512]{1,0:T(8,128)(2,1)S(1)}, u32[]{:S(2)}, u32[]{:S(2)}) collective-permute-start(bf16[392,512]{1,0:T(8,128)(2,1)S(1)} %shard_map.333.refs_0_), channel_id=1, source_target_pairs={{0,2},{2,4},{4,6},{6,7},{7,5},{5,3},{3,1},{1,0},{8,10},{10,12},{12... | collective-permute-start | bytes 1204232 | tf_op jit(solution)/shard_map/ppermute | solution.py:79
  299.6 16.7 %collective-permute-start.85 = (bf16[64,512]{1,0:T(8,128)(2,1)S(1)}, bf16[64,512]{1,0:T(8,128)(2,1)S(1)}, u32[]{:S(2)}, u32[]{:S(2)}) collective-permute-start(bf16[64,512]{1,0:T(8,128)(2,1)S(1)} %get-tuple-element.104), channel_id=1, source_target_pairs={{0,2},{2,4},{4,6},{6,7},{7,5},{5,3},{3,1},{1,0},{8,10},{10,12},{12... | collective-permute-start | bytes 196616 | tf_op jit(solution)/shard_map/ppermute | solution.py:79
  301.3 15.7 %collective-permute-start.89 = (bf16[64,512]{1,0:T(8,128)(2,1)S(1)}, bf16[64,512]{1,0:T(8,128)(2,1)S(1)}, u32[]{:S(2)}, u32[]{:S(2)}) collective-permute-start(bf16[64,512]{1,0:T(8,128)(2,1)S(1)} %fusion.21), channel_id=1, source_target_pairs={{2,0},{4,2},{6,4},{7,6},{5,7},{3,5},{1,3},{0,1},{10,8},{12,10},{14... | collective-permute-start | bytes 196616 | tf_op jit(solution)/shard_map/ppermute | solution.py:82
  306.9 11.0 %collective-permute-start.91 = (f32[2,512]{1,0:T(2,128)S(1)}, f32[2,512]{1,0:T(2,128)S(1)}, u32[]{:S(2)}, u32[]{:S(2)}) collective-permute-start(f32[2,512]{1,0:T(2,128)S(1)} %add.348.sums), channel_id=1, source_target_pairs={{0,4},{1,5},{2,6},{3,7},{4,0},{5,1},{6,2},{7,3},{8,12},{9,13},{10,... | collective-permute-start | bytes 12296 | tf_op jit(solution)/shard_map/ppermute | solution.py:132
  310.8 11.3 %collective-permute-start.61 = (bf16[392,512]{1,0:T(8,128)(2,1)S(1)}, bf16[392,512]{1,0:T(8,128)(2,1)S(1)}, u32[]{:S(2)}, u32[]{:S(2)}) collective-permute-start(bf16[392,512]{1,0:T(8,128)(2,1)S(1)} %collective-permute-done.60.refs_1_), channel_id=1, source_target_pairs={{2,0},{4,2},{6,4},{7,6},{5,7},{3,5},{1,3},{0,1},{10,8},{12,10},{14... | collective-permute-start | bytes 1204232 | tf_op jit(solution)/shard_map/ppermute | solution.py:82
  310.8 11.3 %collective-permute-start.64 = (bf16[392,512]{1,0:T(8,128)(2,1)S(1)}, bf16[392,512]{1,0:T(8,128)(2,1)S(1)}, u32[]{:S(2)}, u32[]{:S(2)}) collective-permute-start(bf16[392,512]{1,0:T(8,128)(2,1)S(1)} %collective-permute-done.63.refs_8_), channel_id=1, source_target_pairs={{0,2},{2,4},{4,6},{6,7},{7,5},{5,3},{3,1},{1,0},{8,10},{10,12},{12... | collective-permute-start | bytes 1204232 | tf_op jit(solution)/shard_map/ppermute | solution.py:79
  316.4 32.7 %collective-permute-start.71 = (bf16[1,8,576,128]{3,2,1,0:T(8,128)(2,1)}, bf16[1,8,576,128]{3,2,1,0:T(8,128)(2,1)}, u32[]{:S(2)}, u32[]{:S(2)}) collective-permute-start(bf16[1,8,576,128]{3,2,1,0:T(8,128)(2,1)} %slice.450), channel_id=1, source_target_pairs={{0,16},{8,24},{16,0},{24,8},{1,17},{9,25},{17,1},{25,9},{2,18},{10... | collective-permute-start | bytes 3538952 | tf_op jit(solution)/shard_map/ppermute | solution.py:132
  322.1 12.3 %collective-permute-start.62 = (bf16[392,512]{1,0:T(8,128)(2,1)S(1)}, bf16[392,512]{1,0:T(8,128)(2,1)S(1)}, u32[]{:S(2)}, u32[]{:S(2)}) collective-permute-start(bf16[392,512]{1,0:T(8,128)(2,1)S(1)} %collective-permute-done.61.refs_2_), channel_id=1, source_target_pairs={{2,0},{4,2},{6,4},{7,6},{5,7},{3,5},{1,3},{0,1},{10,8},{12,10},{14... | collective-permute-start | bytes 1204232 | tf_op jit(solution)/shard_map/ppermute | solution.py:82
  (109 other events, 868.4 us)

commit v2 on v1

--- a/solution.py
+++ b/solution.py
@@ -12,6 +12,7 @@
 SIDE = 7
 PIXELS = SIDE * SIDE
 TAPS = 9
+VMEM = 24
 F32 = jnp.float32
 BF16 = jnp.bfloat16
 
@@ -81,47 +82,67 @@
     def bw(self, x):
         return lax.ppermute(x, "chan", self.back)
 
-    def gather(self, x, axis):
-        size, half = self.size, x.shape[axis] // 2
-        pieces = [None] * size
-        pieces[0] = x
-        a = b = x
-        for step in range(1, size // 2):
-            a, b = self.fw(a), self.bw(b)
-            pieces[size - step], pieces[step] = a, b
-        low = self.fw(lax.slice_in_dim(a, 0, half, axis=axis))
-        high = self.bw(lax.slice_in_dim(b, half, x.shape[axis], axis=axis))
-        pieces[size // 2] = (low, high)
-        return pieces
-
-    def scatter(self, parts, axis):
-        size = self.size
-        width = parts[0].shape[axis]
-        half = width // 2
-        middle = parts[size // 2]
-        f = self.fw(lax.slice_in_dim(middle, 0, half, axis=axis))
-        b = self.bw(lax.slice_in_dim(middle, half, width, axis=axis))
-        for step in range(size // 2 - 1, 0, -1):
-            left, right = parts[step], parts[size - step]
-            if step == size // 2 - 1:
-                f = jnp.concatenate(
-                    [
-                        add16(lax.slice_in_dim(left, 0, half, axis=axis), f),
-                        lax.slice_in_dim(left, half, width, axis=axis),
-                    ],
-                    axis,
-                )
-                b = jnp.concatenate(
-                    [
-                        lax.slice_in_dim(right, 0, half, axis=axis),
-                        add16(lax.slice_in_dim(right, half, width, axis=axis), b),
-                    ],
-                    axis,
-                )
-            else:
-                f, b = add16(left, f), add16(right, b)
-            f, b = self.fw(f), self.bw(b)
-        return f, b
+
+def tie(x, other):
+    first = lax.slice(other, (0,) * other.ndim, (1,) * other.ndim).reshape(())
+    return jnp.where(first > -3e38, x, jnp.zeros_like(x))
+
+
+class Gather:
+    def __init__(self, ring, x, axis):
+        self.ring, self.axis, self.half = ring, axis, x.shape[axis] // 2
+        self.pieces = [x] + [None] * (ring.size - 1)
+        self.count = 0
+
+    def step(self, other=None):
+        ring, size = self.ring, self.ring.size
+        a, b = self.pieces[(size - self.count) % size], self.pieces[self.count]
+        if other is not None:
+            a, b = tie(a, other), tie(b, other)
+        self.count += 1
+        if self.count < size // 2:
+            got = [ring.fw(a), ring.bw(b)]
+            self.pieces[size - self.count], self.pieces[self.count] = got
+        else:
+            got = [
+                ring.fw(lax.slice_in_dim(a, 0, self.half, axis=self.axis)),
+                ring.bw(lax.slice_in_dim(b, self.half, b.shape[self.axis], axis=self.axis)),
+            ]
+            self.pieces[size // 2] = tuple(got)
+        return got
+
+
+class Scatter:
+    def __init__(self, ring, low, high, part, axis):
+        self.ring, self.part, self.axis = ring, part, axis
+        self.f, self.b = ring.fw(low), ring.bw(high)
+        self.count = 1
+
+    def step(self):
+        size, axis = self.ring.size, self.axis
+        k = size // 2 - self.count
+        left, right = self.part(k), self.part(size - k)
+        if self.count == 1:
+            width = left.shape[axis]
+            half = width // 2
+            f = jnp.concatenate(
+                [
+                    add16(lax.slice_in_dim(left, 0, half, axis=axis), self.f),
+                    lax.slice_in_dim(left, half, width, axis=axis),
+                ],
+                axis,
+            )
+            b = jnp.concatenate(
+                [
+                    lax.slice_in_dim(right, 0, half, axis=axis),
+                    add16(lax.slice_in_dim(right, half, width, axis=axis), self.b),
+                ],
+                axis,
+            )
+        else:
+            f, b = add16(left, self.f), add16(right, self.b)
+        self.count += 1
+        self.f, self.b = self.ring.fw(f), self.ring.bw(b)
 
 
 def add16(one, two):
@@ -142,13 +163,20 @@
     return x
 
 
-def run(body, meta, grid, ins, outs, scratch=(), vmem=48, cost=None):
+def run(body, meta, grid, ins, outs, scratch=(), vmem=VMEM, cost=None, after=(), into=()):
+    extra = list(into) + list(after)
+    first, last = len(ins), len(ins) + len(extra)
+
+    def kernel(meta, *refs):
+        body(meta, *refs[:first], *refs[last:])
+
     return pl.pallas_call(
-        body,
+        kernel if extra else body,
         grid_spec=pltpu.PrefetchScalarGridSpec(
             num_scalar_prefetch=1,
             grid=grid,
-            in_specs=[pl.BlockSpec(b, m) for _, b, m in ins],
+            in_specs=[pl.BlockSpec(b, m) for _, b, m in ins]
+            + [pl.BlockSpec(memory_space=pl.ANY)] * len(extra),
             out_specs=[pl.BlockSpec(b, m) for _, _, b, m in outs],
             scratch_shapes=list(scratch),
         ),
@@ -159,7 +187,8 @@
         )
         if cost
         else None,
-    )(meta, *[a for a, _, _ in ins])
+        input_output_aliases={1 + first + q: q for q in range(len(into))},
+    )(meta, *[a for a, _, _ in ins], *extra)
 
 
 def whole(x):
@@ -175,6 +204,7 @@
 class Sizes:
     def __init__(self, chunks, micro, images):
         self.chunks = chunks
+        self.half = chunks // 2
         self.micro = micro
         self.images = images
         self.rows = PIXELS * images
@@ -182,7 +212,12 @@
         self.live = chunks
         self.batch = 2 * chunks
         self.count = 3 * chunks
-        self.planes = 3 * chunks + micro
+        self.arrive = 3 * chunks + micro
+        self.planes = 4 * chunks + micro
+        self.arrival = [0]
+        for step in range(1, chunks // 2):
+            self.arrival += [chunks - step, step]
+        self.arrival.append(chunks // 2)
 
     def own_count(self, meta):
         batch = meta[self.batch]
@@ -195,6 +230,38 @@
 def split_lanes(value, native):
     for q in range(native.shape[0]):
         native[q] = value[:, q * 128 : (q + 1) * 128]
+
+
+def meta_body(sz, dp, ratio, counts, table, out):
+    d, c = lax.axis_index("dp"), lax.axis_index("chan")
+    per_batch = sz.chunks // sz.micro
+    for k in range(sz.chunks):
+        chunk = table[c, k]
+        batch = lax.div(chunk, per_batch)
+        have = counts[batch, d] - sz.images * lax.rem(chunk, per_batch)
+        out[k] = chunk
+        out[sz.live + k] = jnp.minimum(jnp.maximum(have, 0), sz.images)
+        out[sz.batch + k] = batch
+        out[sz.arrive + k] = jnp.int32(sz.arrival[k])
+    for m in range(sz.micro):
+        total = counts[m, 0]
+        for g in range(1, dp):
+            total += counts[m, g]
+        out[sz.count + m] = PIXELS * total
+    for p in range(dp):
+        out[sz.planes + p] = d ^ ((p % (dp // 2)) * 2 + p // (dp // 2))
+    out[sz.planes + dp] = lax.div(c, ratio)
+    out[sz.planes + dp + 1] = lax.rem(c, ratio)
+
+
+def make_meta(sz, ring, dp, ratio, counts):
+    smem = pl.BlockSpec(memory_space=pltpu.SMEM)
+    return pl.pallas_call(
+        functools.partial(meta_body, sz, dp, ratio),
+        in_specs=[smem, smem],
+        out_specs=smem,
+        out_shape=jax.ShapeDtypeStruct((sz.planes + dp + 2,), jnp.int32),
+    )(counts, jnp.asarray(ring.table))
 
 
 def to_padded(sz, native, padded):
@@ -247,6 +314,17 @@
         taps[b] = strip[b * n : b * n + 72 * n, :].astype(BF16)
 
 
+def first_lead_body(meta, x, weight, low, high):
+    value = jnp.dot(x[0], weight[...], preferred_element_type=F32).astype(BF16)
+    half = low.shape[1]
+    low[...] = value[:, :half]
+    high[...] = value[:, half:]
+
+
+def first_part_body(meta, x, weight, out):
+    out[0] = jnp.dot(x[0], weight[...], preferred_element_type=F32).astype(BF16)
+
+
 def first_body(sz, meta, f, b, own, pre, stat, native):
     split_lanes(f[...].astype(F32) + b[...].astype(F32) + own[0].astype(F32), native)
     to_padded(sz, native, pre)
@@ -255,7 +333,9 @@
     put_sums(stat, kept, kept * kept)
 
 
-def conv_body(sz, meta, pre, stat, params, weight, out, raw, stat_out, taps, strip, total, native):
+def conv_body(
+    sz, meta, pre, stat, params, weight, out, raw, stat_out, acted, strip, taps, total, native
+):
     step = pl.program_id(0)
     n = sz.images
     width = pre.shape[1]
@@ -265,6 +345,7 @@
         average, inv = moments(stat[...], sz.own_count(meta))
         z = params[0:1] * ((pre[...] - average) * inv) + params[1:2]
         act = jnp.where(row_mask(sz, width, None), z * sigmoid(z), 0.0)
+        acted[...] = act.astype(BF16)
         lay_taps(sz, act, strip, taps)
         total[...] = jnp.zeros_like(total)
 
@@ -326,12 +407,13 @@
     return pieces, refs[at:]
 
 
-def expand_body(sz, layout, meta, *refs):
+def expand_body(sz, layout, offset, meta, *refs):
     pieces, rest = split_refs(layout, refs)
     stat, params, weight, act, pre, stat_out, place = rest
     step = pl.program_id(0)
     stage_piece(pieces, place, step)
-    batch = meta[sz.batch + step]
+    k = meta[sz.arrive + offset + step]
+    batch = meta[sz.batch + k]
     average, inv = moments(pick(sz, stat[...], batch), pick_count(sz, meta, batch))
     z = params[2:3] * ((place[...].astype(F32) - average) * inv) + params[3:4]
     acted = (z * sigmoid(z)).astype(BF16)
@@ -344,7 +426,7 @@
         stat_out[...] = jnp.zeros_like(stat_out)
 
     rows = lax.broadcasted_iota(jnp.int32, value.shape, 0)
-    kept = jnp.where(rows < PIXELS * meta[sz.live + step], value, 0.0)
+    kept = jnp.where(rows < PIXELS * meta[sz.live + k], value, 0.0)
     add_sums(sz, stat_out, batch, kept, kept * kept)
 
 
@@ -370,21 +452,31 @@
     add_sums(sz, stat_out, batch, upstream, upstream * normed)
 
 
-def shrink_body(sz, meta, pre, stat, params, grad, sums, weight, back, part):
-    step = pl.program_id(0)
-    batch = meta[sz.batch + step]
+def shrink_body(sz, lead, meta, pre, stat, params, grad, sums, weight, back, *parts):
+    if lead:
+        k = sz.half
+    else:
+        step = pl.program_id(0)
+        k = jnp.where(step < sz.half, step, step + 1)
+    batch = meta[sz.batch + k]
     count = pick_count(sz, meta, batch)
     average, inv = moments(pick(sz, stat[...], batch), count)
     both = pick(sz, sums[...], batch)
     normed = (pre[0] - average) * inv
     rows = lax.broadcasted_iota(jnp.int32, normed.shape, 0)
-    live = rows < PIXELS * meta[sz.live + step]
+    live = rows < PIXELS * meta[sz.live + k]
     value = params[0:1] * inv * (grad[0] - (both[0:1] + normed * both[1:2]) / count)
     value = jnp.where(live, value, 0.0).astype(BF16)
     back[0] = value
-    part[0] = lax.dot_general(
+    part = lax.dot_general(
         value, weight[...], (((1,), (1,)), ((), ())), preferred_element_type=F32
     ).astype(BF16)
+    if lead:
+        half = part.shape[1] // 2
+        parts[0][...] = part[:, :half]
+        parts[1][...] = part[:, half:]
+    else:
+        parts[0][0] = part
 
 
 def middle_up_body(sz, meta, f, b, own, pre, stat, params, up, stat_out, native, padded):
@@ -411,7 +503,8 @@
     stat_one,
     params,
     weight,
-    back,
+    stay,
+    send,
     up_one,
     stat_out,
     strip,
@@ -429,7 +522,15 @@
         normed = (pre_two[...] - average) * inv
         value = params[2:3] * inv * (up[...] - (sums[0:1] + normed * sums[1:2]) / count)
         value = jnp.where(row_mask(sz, width, meta[sz.live]), value, 0.0)
-        back[...] = value.astype(BF16)
+        half, _, lanes = stay.shape
+        for p in range(2 * half):
+            for plane in range(2 * half):
+
+                @pl.when(meta[sz.planes + p] == plane)
+                def _(p=p, plane=plane):
+                    out = stay if p < half else send
+                    out[p % half] = value[:, plane * lanes : (plane + 1) * lanes].astype(BF16)
+
         lay_taps(sz, value, strip, taps)
         total[...] = jnp.zeros_like(total)
 
@@ -463,9 +564,12 @@
     to_native(sz, padded, native, back)
 
 
-def input_body(sz, layout, meta, *refs):
+def input_body(sz, layout, more, meta, *refs):
     pieces, rest = split_refs(layout, refs)
-    grad, x, weight, out, grad_weight, place, total = rest
+    if more:
+        grad, x, weight, had, out, grad_weight, place, total = rest
+    else:
+        grad, x, weight, out, grad_weight, place, total = rest
     step = pl.program_id(0)
     stage_piece(pieces, place, step)
     value = place[...]
@@ -475,73 +579,96 @@
 
     @pl.when(step == 0)
     def _():
-        total[...] = jnp.zeros_like(total)
+        total[...] = had[...] if more else jnp.zeros_like(total)
 
     total[...] += lax.dot_general(
         x[0], value, (((0,), (0,)), ((), ())), preferred_element_type=F32
     )
 
-    @pl.when(step == sz.chunks - 1)
+    @pl.when(step == len(layout) - 1)
     def _():
-        grad_weight[...] = total[...].astype(BF16)
-
-
-def middle_grad_body(sz, dp, meta, taps, back, out, whole_grad):
-    step = pl.program_id(0)
+        grad_weight[...] = total[...].astype(grad_weight.dtype)
+
+
+def middle_grad_body(sz, dp, meta, acts, backs, out, strip, taps, total):
+    source = pl.program_id(0)
     n = sz.images
-    at = pl.multiple_of(lax.div(step, 3) * 8 * n, 8 * n)
-    window = taps[lax.rem(step, 3), pl.ds(at, sz.padded), :]
-    value = lax.dot_general(
-        window, back[...], (((0,), (0,)), ((), ())), preferred_element_type=F32
-    )
-    lanes = value.shape[1] // dp
-    for d in range(dp):
-        whole_grad[d] = value[:, d * lanes : (d + 1) * lanes]
-    depth = value.shape[0] // sz.chunks
-    for p in range(dp):
+    lay_taps(sz, backs[0, 0].astype(F32), strip, taps)
+    shifted = [
+        taps[2 - b, (2 - a) * 8 * n : (2 - a) * 8 * n + sz.padded, :]
+        for a in range(3)
+        for b in range(3)
+    ]
+
+    @pl.when(source == 0)
+    def _():
+        total[...] = jnp.zeros_like(total)
+
+    total[...] += lax.dot_general(
+        acts[0],
+        jnp.concatenate(shifted, axis=1),
+        (((0,), (0,)), ((), ())),
+        preferred_element_type=F32,
+    )
+
+    @pl.when(source == dp - 1)
+    def _():
+        depth, lanes = out.shape[1] // TAPS, out.shape[2]
         for k in range(sz.chunks):
             at = pl.multiple_of(meta[k] * depth, depth)
-            out[p, k, 0] = whole_grad[meta[sz.planes + p], pl.ds(at, depth), :].astype(BF16)
-
-
-def assemble_body(sz, half, meta, near, far, out):
-    @pl.when(pl.program_id(0) < half)
-    def _():
-        out[...] = near[0, 0]
-
-    @pl.when(pl.program_id(0) >= half)
-    def _():
-        out[...] = far[0, 0]
+            for tap in range(TAPS):
+                out[k, tap * depth : (tap + 1) * depth, :] = total[
+                    pl.ds(at, depth), tap * lanes : (tap + 1) * lanes
+                ].astype(BF16)
+
+
+def assemble_body(sz, half, depth, meta, *refs):
+    stacks, out = refs[:-1], refs[-1]
+    early = sz.chunks - 3
+
+    def fill(plane):
+        for q, k in enumerate(sz.arrival):
+            pieces = stacks[plane if q < early else half + plane]
+            at = pl.multiple_of(meta[k] * depth, depth)
+            for tap in range(TAPS):
+                value = pieces[0, q if q < early else q - early, tap * depth : (tap + 1) * depth, :]
+                if len(out.shape) == 3:
+                    out[tap, pl.ds(at, depth), :] = value
+                else:
+                    out[0, tap, pl.ds(at, depth), :] = value
+
+    for p in range(2 * half):
+
+        @pl.when(pl.program_id(0) == p)
+        def _(p=p):
+            fill(p if p < half else half + p)
+
+
+def prepare_body(weights, last, params, out):
+    many, lanes = weights.shape
+    out[:many, :] = weights[...].astype(BF16)
+    depth = last.shape[0]
+    for b in range(last.shape[1] // lanes):
+        out[many + b * depth : many + (b + 1) * depth, :] = last[
+            :, b * lanes : (b + 1) * lanes
+        ].astype(BF16)
+    value = params[...]
+    count, width = value.shape
+    one = value.astype(BF16)
+    left = value - one.astype(F32)
+    two = left.astype(BF16)
+    three = (left - two.astype(F32)).astype(BF16)
+    rest = jnp.zeros((16 - 3 * count, width), F32)
+    rows = jnp.concatenate([part.astype(F32) for part in (one, two, three)] + [rest], axis=0)
+    if width < lanes:
+        rows = jnp.concatenate([rows, jnp.zeros((16, lanes - width), F32)], axis=1)
+    out[out.shape[0] - 16 :, :] = rows.astype(BF16)
 
 
 def last_assemble_body(meta, blocks, out):
     lanes = blocks.shape[3]
     for b in range(blocks.shape[1]):
         out[:, b * lanes : (b + 1) * lanes] = blocks[0, b]
-
-
-def copy_body(meta, source, out):
-    out[...] = source[...]
-
-
-def reorder(sz, meta, x, inward):
-    rest = x.shape[2:]
-
-    def ordered(p, k, meta):
-        return (p, k) + (0,) * len(rest)
-
-    def placed(p, k, meta):
-        return (meta[sz.planes + p], meta[k]) + (0,) * len(rest)
-
-    (moved,) = run(
-        copy_body,
-        meta,
-        x.shape[:2],
-        [(x, (1, 1) + rest, placed if inward else ordered)],
-        [(x.shape, x.dtype, (1, 1) + rest, ordered if inward else placed)],
-        vmem=16,
-    )
-    return moved
 
 
 def last_grad_body(sz, meta, act, back, out, total):
@@ -609,108 +736,105 @@
     own_blocks = deep // lanes
     ratio = last_blocks // own_blocks
 
-    at = lax.dynamic_index_in_dim(jnp.asarray(ring.table), c, keepdims=False)
-    batch = at // per_batch
-    own_counts = lax.dynamic_index_in_dim(image_counts, d, axis=1, keepdims=False)
-    counts_at = own_counts[0]
-    for m in range(1, micro):
-        counts_at = jnp.where(batch == m, own_counts[m], counts_at)
-    live = jnp.clip(counts_at - images * (at % per_batch), 0, images)
-    planes = d ^ jnp.asarray([(p % half) * 2 + p // half for p in range(dp)], jnp.int32)
-    meta = jnp.concatenate(
-        [at, live, batch, PIXELS * jnp.sum(image_counts, axis=1), planes]
-    ).astype(jnp.int32)
-
+    meta = make_meta(sz, ring, dp, ratio, image_counts)
+    at = meta[:chan]
+
+    dp_bits = bits_below(dp)
+    wide_bits = dp_bits[1:]
     first = w_first.astype(BF16)
-    for bit in bits_below(dp):
+    for bit in dp_bits:
         other = swap(first, "dp", bit, dp)
         first = jnp.where(
             (d & bit) == 0,
             jnp.concatenate([first, other], axis=1),
             jnp.concatenate([other, first], axis=1),
         )
-    one = mid_params.astype(BF16)
-    left = mid_params - one.astype(F32)
-    two = left.astype(BF16)
-    three = (left - two.astype(F32)).astype(BF16)
-    param_rows = jnp.concatenate([one, two, three], axis=0)
-    param_rows = jnp.pad(param_rows, ((0, 4), (0, lanes - depth)))
-    low_last = w_last.astype(BF16)
-    payload = jnp.concatenate(
-        [w_middle.astype(BF16).reshape(TAPS * depth, lanes)]
-        + [low_last[:, b * lanes : (b + 1) * lanes] for b in range(last_blocks)]
-        + [param_rows],
-        axis=0,
-    )
-    got = ring.gather(payload, 0)
-    got[chan // 2] = jnp.concatenate(got[chan // 2], axis=0)
-    got = jnp.stack(got)
-    mids = got[:, : TAPS * depth]
-    lasts = got[:, TAPS * depth : (TAPS + last_blocks) * depth].reshape(
-        chan, ratio, own_blocks, depth, lanes
-    )
-    tail = got[:, (TAPS + last_blocks) * depth :, :depth].astype(F32)
+    many = TAPS * depth
+    tail_at = many + last_blocks * depth
+    (payload,) = pl.pallas_call(
+        prepare_body,
+        in_specs=[pl.BlockSpec(memory_space=pltpu.VMEM)] * 3,
+        out_specs=[pl.BlockSpec(memory_space=pltpu.VMEM)],
+        out_shape=[jax.ShapeDtypeStruct((tail_at + 16, lanes), BF16)],
+    )(w_middle.reshape(many, lanes), w_last, mid_params)
+    mids = Gather(ring, payload, 0)
+    while mids.count < chan // 2:
+        mids.step()
+
+    x = inputs.reshape(chan, rows, deep)
+    cot = cotangent.reshape(chan, rows, deep)
+
+    def at_place(k, meta):
+        return (meta[k], 0, 0)
+
+    def in_order(k, meta):
+        return (k, 0, 0)
+
+    opposite = chan // 2
+
+    def skipping(k, meta):
+        return (jnp.where(k < opposite, k, k + 1), 0, 0)
+
+    def skipping_at(k, meta):
+        return (meta[jnp.where(k < opposite, k, k + 1)], 0, 0)
+
+    low, high = run(
+        first_lead_body,
+        meta,
+        (1,),
+        [(x, (1, rows, deep), lambda k, meta: (meta[opposite], 0, 0)), whole(first)],
+        [whole_out((rows, mid // 2), BF16), whole_out((rows, mid // 2), BF16)],
+    )
+    (parts,) = run(
+        first_part_body,
+        meta,
+        (chan - 1,),
+        [(x, (1, rows, deep), skipping_at), whole(first)],
+        [((chan, rows, mid), BF16, (1, rows, mid), skipping)],
+        cost=(2 * chan * rows * deep * mid, 2 * chan * rows * (deep + mid)),
+    )
+    sums = Scatter(ring, low, high, lambda k: parts[k], 1)
+    while sums.count < opposite:
+        sums.step()
+    f, b = sums.f, sums.b
+
+    came = [jnp.concatenate(p, axis=0) if isinstance(p, tuple) else p for p in mids.pieces]
+    tails = jnp.stack([p[many:] for p in came])
+    near, far = [], []
+    for group in (sz.arrival[: chan - 3], sz.arrival[chan - 3 :]):
+        stack = jnp.stack([came[k][:many] for k in group])[None]
+        planes = [stack]
+        for bit in wide_bits:
+            planes += [swap(p, "dp", bit, dp) for p in planes]
+        near.append(planes)
+        far.append([swap(p, "dp", 1, dp) for p in planes])
+    near = [near[g][q] for g in range(2) for q in range(half)]
+    far = [far[g][q] for g in range(2) for q in range(half)]
+    if lanes % 128 == 0:
+        placed = ((TAPS, mid, mid), BF16, (TAPS, mid, lanes), lambda p, meta: (0, 0, meta[sz.planes + p]))
+    else:
+        placed = (
+            (dp, TAPS, mid, lanes),
+            BF16,
+            (1, TAPS, mid, lanes),
+            lambda p, meta: (meta[sz.planes + p], 0, 0, 0),
+        )
+    (middle,) = run(
+        functools.partial(assemble_body, sz, half, depth),
+        meta,
+        (dp,),
+        [whole(p) for p in near + far],
+        [placed],
+    )
+    here = (at[None, :] == jnp.arange(chan)[:, None])[:, :, None, None]
+    tail = tails[:, last_blocks * depth :, :depth].astype(F32)
     tail = (tail[:, 8:12] + tail[:, 4:8]) + tail[:, 0:4]
-    here = (at[None, :] == jnp.arange(chan)[:, None])[:, :, None, None]
     params = jnp.sum(jnp.where(here, tail[None], 0.0), axis=1)
     params = params.transpose(1, 0, 2).reshape(4, mid)
-
-    near = mids[None]
-    for bit in bits_below(dp)[1:]:
-        near = jnp.concatenate([near, swap(near, "dp", bit, dp)], axis=0)
-    far = swap(near, "dp", 1, dp)
-    if lanes % 128 == 0:
-        near = near.reshape(half, chan, TAPS, depth, lanes)
-        far = far.reshape(half, chan, TAPS, depth, lanes)
-        (middle,) = run(
-            functools.partial(assemble_body, sz, half),
-            meta,
-            (dp, chan),
-            [
-                (
-                    near,
-                    (1, 1, TAPS, depth, lanes),
-                    lambda p, k, meta: (
-                        jnp.minimum(p, half - 1),
-                        jnp.where(p < half, k, chan - 1),
-                        0,
-                        0,
-                        0,
-                    ),
-                ),
-                (
-                    far,
-                    (1, 1, TAPS, depth, lanes),
-                    lambda p, k, meta: (
-                        jnp.maximum(p - half, 0),
-                        jnp.where(p < half, 0, k),
-                        0,
-                        0,
-                        0,
-                    ),
-                ),
-            ],
-            [
-                (
-                    (TAPS, mid, mid),
-                    BF16,
-                    (TAPS, depth, lanes),
-                    lambda p, k, meta: (0, meta[k], meta[sz.planes + p]),
-                )
-            ],
-            vmem=16,
-            cost=(0, 4 * TAPS * mid * mid),
-        )
-    else:
-        both = jnp.concatenate([near, far], axis=0)
-        middle = (
-            reorder(sz, meta, both, False)
-            .reshape(dp, chan, TAPS, depth, lanes)
-            .transpose(2, 1, 3, 0, 4)
-            .reshape(TAPS, mid, mid)
-        )
+    if lanes % 128 != 0:
+        middle = middle.transpose(1, 2, 0, 3)
     middle = middle.reshape(3, 3, mid, mid)
-
+    lasts = tails[:, : last_blocks * depth].reshape(chan, ratio, own_blocks, depth, lanes)
     own_last = lax.dynamic_index_in_dim(lasts, c % ratio, axis=1, keepdims=False)
     found = jnp.where(d == c // ratio, own_last, jnp.zeros_like(own_last))
     for shift in range(1, dp):
@@ -724,32 +848,7 @@
         (chan,),
         [(found, (1, own_blocks, depth, lanes), lambda k, meta: (k, 0, 0, 0))],
         [((mid, deep), BF16, (depth, deep), lambda k, meta: (meta[k], 0))],
-        vmem=16,
-        cost=(0, 4 * mid * deep),
-    )
-
-    x = inputs.reshape(chan, rows, deep)
-    cot = cotangent.reshape(chan, rows, deep)
-
-    def at_place(k, meta):
-        return (meta[k], 0, 0)
-
-    def in_order(k, meta):
-        return (k, 0, 0)
-
-    def first_part_body(meta, x_ref, weight, out):
-        out[0] = jnp.dot(x_ref[0], weight[...], preferred_element_type=F32).astype(BF16)
-
-    (parts,) = run(
-        first_part_body,
-        meta,
-        (chan,),
-        [(x, (1, rows, deep), at_place), whole(first)],
-        [((chan, rows, mid), BF16, (1, rows, mid), in_order)],
-        vmem=16,
-        cost=(2 * chan * rows * deep * mid, 2 * chan * rows * (deep + mid)),
-    )
-    f, b = ring.scatter(parts, 1)
+    )
 
     def head(stack):
         return (stack, (1,) + stack.shape[1:], lambda *_: (0, 0, 0))
@@ -757,8 +856,7 @@
     stat_bits = [k for k in bits_below(chan) if k < per_batch]
 
     def total_rows(stat):
-        stat = sum_over(stat, "dp", bits_below(dp), dp)
-        return sum_over(stat, "chan", stat_bits, chan)
+        return sum_over(sum_over(stat, "dp", dp_bits, dp), "chan", stat_bits, chan)
 
     def all_batches(stat):
         for bit in bits_below(chan):
@@ -778,7 +876,7 @@
         [whole(f), whole(b), head(parts)],
         [whole_out((padded, mid), F32), whole_out((2, mid), F32)],
         [pltpu.VMEM((mid // 128, rows, 128), F32)],
-        vmem=16,
+        vmem=VMEM,
         cost=(10 * padded * mid, 10 * padded * mid),
     )
     stat_one = total_rows(stat_one)
@@ -786,7 +884,7 @@
     tap_block = (1, 3, mid, mid)
     conv_flops = 2 * TAPS * padded * mid * mid
     conv_bytes = 2 * TAPS * mid * mid + 16 * padded * mid
-    pre_two, raw, stat_two, taps = run(
+    pre_two, raw, stat_two, acted = run(
         functools.partial(conv_body, sz),
         meta,
         (3,),
@@ -800,35 +898,60 @@
             whole_out((padded, mid), F32),
             whole_out((rows, mid), BF16),
             whole_out((2, mid), F32),
-            whole_out((3, 72 * images, mid), BF16),
+            whole_out((padded, mid), BF16),
         ],
         [
             pltpu.VMEM((74 * images, mid), F32),
+            pltpu.VMEM((3, 72 * images, mid), BF16),
             pltpu.VMEM((padded, mid), F32),
             pltpu.VMEM((mid // 128, rows, 128), F32),
         ],
-        vmem=32,
+        vmem=VMEM,
         cost=(conv_flops, conv_bytes),
     )
-    pieces = ring.gather(raw, 1)
-    stat_two = total_rows(stat_two)
+    gather = Gather(ring, raw, 1)
+    gather.step()
+    stat_two = sum_over(stat_two, "dp", dp_bits, dp)
+    gather.step(stat_two)
+    stat_two = sum_over(stat_two, "chan", stat_bits, chan)
+    if gather.count < opposite - 1:
+        gather.step(stat_two)
     stats_two = all_batches(stat_two)
-
-    ins, layout = pieces_in(sz, pieces)
-    act, pre_three, stat_three = run(
-        functools.partial(expand_body, sz, layout),
-        meta,
-        (chan,),
-        ins + [whole(stats_two), whole(params), whole(last)],
-        [
-            ((chan, rows, mid), BF16, (1, rows, mid), in_order),
-            ((chan, rows, deep), F32, (1, rows, deep), in_order),
-            whole_out((2 * micro, deep), F32),
-        ],
-        [pltpu.VMEM((rows, mid), BF16)],
-        vmem=32,
-        cost=(2 * chan * rows * deep * mid, chan * rows * (4 * mid + 4 * deep)),
-    )
+    while gather.count < opposite - 1:
+        gather.step()
+    gather.step(stats_two)
+    pieces = gather.pieces
+    order = [1] + wide_bits[::-1]
+    acts = acted[None]
+    for bit in order:
+        acts = jnp.concatenate([acts, swap(acts, "dp", bit, dp)], axis=0)
+
+    def expand(start, steps, into):
+        ins, layout = pieces_in(sz, [pieces[k] for k in sz.arrival[start : start + steps]])
+
+        def arrived(k, meta):
+            return (meta[sz.arrive + start + k], 0, 0)
+
+        return run(
+            functools.partial(expand_body, sz, layout, start),
+            meta,
+            (steps,),
+            ins + [whole(stats_two), whole(params), whole(last)],
+            [
+                ((chan, rows, mid), BF16, (1, rows, mid), arrived),
+                ((chan, rows, deep), F32, (1, rows, deep), arrived),
+                whole_out((2 * micro, deep), F32),
+            ],
+            [pltpu.VMEM((rows, mid), BF16)],
+            vmem=VMEM,
+            cost=(2 * steps * rows * deep * mid, steps * rows * (4 * mid + 4 * deep)),
+            into=into,
+        )
+
+    early = chan - 3
+    act, pre_three, stat_early = expand(0, early, [])
+    act, pre_three, stat_late = expand(early, 3, [act, pre_three])
+    stat_three = stat_early + stat_late
     stat_three = sum_over(stat_three, "dp", bits_below(dp), dp)
     block_out, grad_summed, sums_three = run(
         functools.partial(out_body, sz),
@@ -846,31 +969,40 @@
             ((chan, rows, deep), F32, (1, rows, deep), in_order),
             whole_out((2 * micro, deep), F32),
         ],
-        vmem=24,
+        vmem=VMEM,
         cost=(20 * chan * rows * deep, 16 * chan * rows * deep),
     )
     sums_three = sum_over(sums_three, "dp", bits_below(dp), dp)
-    back_last, back_parts = run(
-        functools.partial(shrink_body, sz),
-        meta,
-        (chan,),
-        [
-            (pre_three, (1, rows, deep), in_order),
-            whole(stat_three),
-            whole(out_params),
-            (grad_summed, (1, rows, deep), in_order),
-            whole(sums_three),
-            whole(last),
-        ],
-        [
-            ((chan, rows, deep), BF16, (1, rows, deep), in_order),
-            ((chan, rows, mid), BF16, (1, rows, mid), in_order),
-        ],
-        vmem=24,
-        cost=(2 * chan * rows * deep * mid, chan * rows * (2 * mid + 10 * deep)),
-    )
-    f, b = ring.scatter(back_parts, 1)
-
+
+    def shrink(steps, place, into, lead):
+        if lead:
+            made = [whole_out((rows, mid // 2), BF16), whole_out((rows, mid // 2), BF16)]
+        else:
+            made = [((chan, rows, mid), BF16, (1, rows, mid), place)]
+        return run(
+            functools.partial(shrink_body, sz, lead),
+            meta,
+            (steps,),
+            [
+                (pre_three, (1, rows, deep), place),
+                whole(stat_three),
+                whole(out_params),
+                (grad_summed, (1, rows, deep), place),
+                whole(sums_three),
+                whole(last),
+            ],
+            [((chan, rows, deep), BF16, (1, rows, deep), place)] + made,
+            vmem=VMEM,
+            cost=(2 * steps * rows * deep * mid, steps * rows * (2 * mid + 10 * deep)),
+            into=into,
+        )
+
+    back_last, low, high = shrink(1, lambda k, meta: (opposite, 0, 0), [], True)
+    back_last, back_parts = shrink(chan - 1, skipping, [back_last], False)
+    sums = Scatter(ring, low, high, lambda k: back_parts[k], 1)
+    while sums.count < opposite:
+        sums.step()
+    f, b = sums.f, sums.b
     (grad_last,) = run(
         functools.partial(last_grad_body, sz),
         meta,
@@ -878,18 +1010,22 @@
         [(act, (1, rows, mid), in_order), (back_last, (1, rows, deep), in_order)],
         [whole_out((chan, depth, deep), BF16)],
         [pltpu.VMEM((mid, deep), F32)],
-        vmem=16,
         cost=(2 * chan * rows * deep * mid, 2 * chan * rows * (mid + deep)),
     )
-    for bit in bits_below(dp):
+    for bit in dp_bits:
         grad_last = add16(grad_last, swap(grad_last, "dp", bit, dp))
     held = [
         jnp.where(c % ratio == r, grad_last, jnp.zeros_like(grad_last)) for r in range(ratio)
     ]
     held = jnp.concatenate(held, axis=2)
     held = jnp.where(d == c // ratio, held, jnp.zeros_like(held))
-    last_f, last_b = ring.scatter(held, 1)
-    owned_last = held[0].astype(F32) + last_f.astype(F32) + last_b.astype(F32)
+    cut = held.shape[2] // 2
+    last_sums = Scatter(
+        ring, held[opposite, :, :cut], held[opposite, :, cut:], lambda k: held[k], 1
+    )
+    while last_sums.count < opposite:
+        last_sums.step()
+    owned_last = held[0].astype(F32) + last_sums.f.astype(F32) + last_sums.b.astype(F32)
 
     up_two, sums_two = run(
         functools.partial(middle_up_body, sz),
@@ -905,11 +1041,11 @@
         ],
         [whole_out((padded, mid), F32), whole_out((2, mid), F32)],
         [pltpu.VMEM((mid // 128, rows, 128), F32), pltpu.VMEM((padded, mid), F32)],
-        vmem=16,
+        vmem=VMEM,
         cost=(20 * padded * mid, 14 * padded * mid),
     )
     sums_two = total_rows(sums_two)
-    back_two, up_one, sums_one = run(
+    stay, send, up_one, sums_one = run(
         functools.partial(conv_back_body, sz),
         meta,
         (3,),
@@ -924,7 +1060,8 @@
             (middle, tap_block, lambda s, meta: (s, 0, 0, 0)),
         ],
         [
-            whole_out((padded, mid), BF16),
+            whole_out((half, padded, lanes), BF16),
+            whole_out((half, padded, lanes), BF16),
             whole_out((padded, mid), F32),
             whole_out((2, mid), F32),
         ],
@@ -933,9 +1070,10 @@
             pltpu.VMEM((3, 72 * images, mid), BF16),
             pltpu.VMEM((padded, mid), F32),
         ],
-        vmem=32,
+        vmem=VMEM,
         cost=(conv_flops, conv_bytes),
     )
+
     sums_one = total_rows(sums_one)
     (back_one,) = run(
         functools.partial(first_back_body, sz),
@@ -944,78 +1082,86 @@
         [whole(up_one), whole(sums_one), whole(pre_one), whole(stat_one), whole(params)],
         [whole_out((rows, mid), BF16)],
         [pltpu.VMEM((padded, mid), F32), pltpu.VMEM((mid // 128, rows, 128), F32)],
-        vmem=16,
         cost=(10 * padded * mid, 10 * padded * mid),
     )
-    pieces = ring.gather(back_one, 1)
-
-    if lanes % 128 == 0:
-        (grad_middle,) = run(
-            functools.partial(middle_grad_body, sz, dp),
+    gather = Gather(ring, back_one, 1)
+    while gather.count < opposite:
+        gather.step()
+    pieces = gather.pieces
+
+    backs = jnp.stack([stay, swap(send, "dp", 1, dp)])
+    for bit in wide_bits[::-1]:
+        cut = backs.shape[1] // 2
+        backs = jnp.concatenate(
+            [backs[:, :cut], swap(backs[:, cut:], "dp", bit, dp)], axis=0
+        )
+    (grad_middle,) = run(
+        functools.partial(middle_grad_body, sz, dp),
+        meta,
+        (dp,),
+        [
+            (acts, (1, padded, mid), lambda r, meta: (r, 0, 0)),
+            (backs, (1, 1, padded, lanes), lambda r, meta: (r, 0, 0, 0)),
+        ],
+        [whole_out((chan, TAPS * depth, lanes), BF16)],
+        [
+            pltpu.VMEM((74 * images, lanes), F32),
+            pltpu.VMEM((3, 72 * images, lanes), BF16),
+            pltpu.VMEM((mid, TAPS * lanes), F32),
+        ],
+        cost=(conv_flops, conv_bytes),
+        after=[back_one],
+    )
+    cut = TAPS * depth // 2
+    middle_sums = Scatter(
+        ring,
+        grad_middle[opposite, :cut],
+        grad_middle[opposite, cut:],
+        lambda k: grad_middle[k],
+        0,
+    )
+    middle_steps = [middle_sums.f]
+    while middle_sums.count < opposite:
+        middle_sums.step()
+        middle_steps.append(middle_sums.f)
+    owned_middle = (
+        grad_middle[0].astype(F32) + middle_sums.f.astype(F32) + middle_sums.b.astype(F32)
+    ).reshape(3, 3, depth, lanes)
+
+    def input_back(start, steps, had, into, after):
+        ins, layout = pieces_in(sz, [pieces[k] for k in sz.arrival[start : start + steps]])
+        done = start + steps == chan
+
+        def arrived(k, meta):
+            return (meta[sz.arrive + start + k], 0, 0)
+
+        def arrived_at(k, meta):
+            return (meta[meta[sz.arrive + start + k]], 0, 0)
+
+        return run(
+            functools.partial(input_body, sz, layout, bool(had)),
             meta,
-            (TAPS,),
-            [whole(taps), whole(back_two)],
+            (steps,),
+            ins
+            + [
+                (grad_summed, (1, rows, deep), arrived),
+                (x, (1, rows, deep), arrived_at),
+                whole(first),
+            ]
+            + [whole(h) for h in had],
             [
-                (
-                    (dp, chan, TAPS, depth, lanes),
-                    BF16,
-                    (dp, chan, 1, depth, lanes),
-                    lambda s, meta: (0, 0, s, 0, 0),
-                )
+                ((chan, rows, deep), F32, (1, rows, deep), arrived_at),
+                whole_out((deep, mid), BF16 if done else F32),
             ],
-            [pltpu.VMEM((dp, mid, lanes), F32)],
-            vmem=32,
-            cost=(conv_flops, conv_bytes),
+            [pltpu.VMEM((rows, mid), BF16), pltpu.VMEM((deep, mid), F32)],
+            vmem=VMEM,
+            cost=(4 * steps * rows * deep * mid, steps * rows * (2 * mid + 10 * deep)),
+            into=into,
+            after=after,
         )
-    else:
-
-        def plain_grad_body(meta, taps, back, out):
-            step = pl.program_id(0)
-            start = pl.multiple_of(lax.div(step, 3) * 8 * images, 8 * images)
-            window = taps[lax.rem(step, 3), pl.ds(start, padded), :]
-            out[0] = lax.dot_general(
-                window, back[...], (((0,), (0,)), ((), ())), preferred_element_type=F32
-            ).astype(BF16)
-
-        (grad_middle,) = run(
-            plain_grad_body,
-            meta,
-            (TAPS,),
-            [whole(taps), whole(back_two)],
-            [((TAPS, mid, mid), BF16, (1, mid, mid), lambda s, meta: (s, 0, 0))],
-            vmem=32,
-            cost=(conv_flops, conv_bytes),
-        )
-        grad_middle = grad_middle.reshape(TAPS, chan, depth, dp, lanes).transpose(3, 1, 0, 2, 4)
-        grad_middle = reorder(sz, meta, grad_middle, True)
-    kept = grad_middle.reshape(dp, chan, TAPS * depth, lanes)
-    for bit in [1] + bits_below(dp)[:0:-1]:
-        cut = kept.shape[0] // 2
-        kept = add16(kept[:cut], swap(kept[cut:], "dp", bit, dp))
-    kept = kept[0]
-    middle_f, middle_b = ring.scatter(kept, 0)
-    owned_middle = kept[0].astype(F32) + middle_f.astype(F32) + middle_b.astype(F32)
-    owned_middle = owned_middle.reshape(3, 3, depth, lanes)
-
-    ins, layout = pieces_in(sz, pieces)
-    input_grad, grad_first = run(
-        functools.partial(input_body, sz, layout),
-        meta,
-        (chan,),
-        ins
-        + [
-            (grad_summed, (1, rows, deep), in_order),
-            (x, (1, rows, deep), at_place),
-            whole(first),
-        ],
-        [
-            ((chan, rows, deep), F32, (1, rows, deep), at_place),
-            whole_out((deep, mid), BF16),
-        ],
-        [pltpu.VMEM((rows, mid), BF16), pltpu.VMEM((deep, mid), F32)],
-        vmem=32,
-        cost=(4 * chan * rows * deep * mid, chan * rows * (2 * mid + 10 * deep)),
-    )
+
+    input_grad, grad_early = input_back(0, early, [], [], middle_steps[1:2])
+    input_grad, grad_first = input_back(early, 3, [grad_early], [input_grad], middle_steps[2:3])
     owned_first = scatter_columns(grad_first, d, dp)
 
     sums_first, sums_middle = all_batches(sums_one), all_batches(sums_two)

time: 379 us -> 316 us (0.83)
  waiting for transfers between devices: 175 us -> 136 us
  local copies, waits for them, and re-layouts: 23.5 us -> 13.7 us
  other arithmetic: 22.7 us -> 14.9 us
  starting transfers between devices: 96.2 us -> 90.3 us
    ppermute x28, waiting for transfers between devices: 63.2 us -> 42.3 us  [bw(): return lax.ppermute(x, 'chan', self.back)]
    ppermute x28, waiting for transfers between devices: 66.1 us -> 47.8 us  [fw(): return lax.ppermute(x, 'chan', self.ahead)]
    ppermute x28, starting transfers between devices: 30.2 us -> 23.2 us  [fw(): return lax.ppermute(x, 'chan', self.ahead)]
    slice x21 -> x15, local copies, waits for them, and re-layouts: 9.69 us -> 2.75 us  [the longest x3 1.54 us: tie(): first = lax.slice(other, (0,) * other.ndim, (1,) * other.ndim).reshape(())]
    ppermute x28, starting transfers between devices: 30 us -> 34.5 us  [bw(): return lax.ppermute(x, 'chan', self.back)]
    pallas_call x14 -> x20, Pallas kernels: 59 us -> 56.4 us  [the longest x18 53.4 us: run(): pl.pallas_call(kernel if extra else body, grid_spec=pltpu.PrefetchScalarG...]
    unnamed x93 -> x85, local copies, waits for them, and re-layouts: 11.4 us -> 9.5 us
    ppermute x33 -> x39, starting transfers between devices: 28.3 us -> 27 us  [swap(): return lax.ppermute(x, axis, [(i, i ^ bit) for i in range(size)])]
  transfers between devices with their start and end apart: 92 -> 98, of which waited for: 52 -> 47; matrix products, arithmetic and copies ran while one was open for 7% -> 6% of each run, Pallas kernels for 5% -> 14%
where the time goes in v2:
time: 316 us; the launch traced here: 315 us
  waiting for transfers between devices  136 us (43%)
  starting transfers between devices  90.3 us (29%)
  Pallas kernels  56.4 us (18%)
  other arithmetic  14.9 us (5%)
  local copies, waits for them, and re-layouts  13.7 us (4%)
  between operations  3.81 us (1%)
    pallas_call x18, Pallas kernels, run(): pl.pallas_call(kernel if extra else body, grid_spec=pltpu.PrefetchScalarG...  53.4 us
    ppermute x28, waiting for transfers between devices, fw(): return lax.ppermute(x, 'chan', self.ahead)  47.8 us
    ppermute x39, waiting for transfers between devices, swap(): return lax.ppermute(x, axis, [(i, i ^ bit) for i in range(size)])  46.1 us
    ppermute x28, waiting for transfers between devices, bw(): return lax.ppermute(x, 'chan', self.back)  42.3 us
    ppermute x28, starting transfers between devices, bw(): return lax.ppermute(x, 'chan', self.back)  34.5 us
    ppermute x39, starting transfers between devices, swap(): return lax.ppermute(x, axis, [(i, i ^ bit) for i in range(size)])  27 us
    ppermute x28, starting transfers between devices, fw(): return lax.ppermute(x, 'chan', self.ahead)  23.2 us
    unnamed x85, local copies, waits for them, and re-layouts  9.5 us
  transfers between devices with their start and end apart: 98, of which 47 were waited for; matrix products, arithmetic and copies ran while one was open for 6% of the time, Pallas kernels for 14%

profile of v2, /device:TPU:0, one launch (start us, length us, event | category | flops | bytes accessed | tf_op | source)
XLA Modules:
  0.0 315.4 jit_solution(11269436899817726655)
XLA Ops:
  12.2 3.5 %collective-permute-done.1 = bf16[256,256]{1,0:T(8,128)(2,1)S(1)} collective-permute-done((bf16[256,256]{1,0:T(8,128)(2,1)S(1)}, bf16[256,256]{1,0:T(8,128)(2,1)S(1)}, u32[]{:S(2)}, u32[]{:S(2)}) %collective-permute-start.1) | collective-permute-done | bytes 131104 | tf_op jit(solution)/shard_map/ppermute | solution.py:153
  26.3 3.6 %collective-permute-done.6 = bf16[392,256]{1,0:T(8,128)(2,1)S(1)} collective-permute-done((bf16[392,256]{1,0:T(8,128)(2,1)S(1)}, bf16[392,256]{1,0:T(8,128)(2,1)S(1)}, u32[]{:S(2)}, u32[]{:S(2)}) %collective-permute-start.6) | collective-permute-done | bytes 200736 | tf_op jit(solution)/shard_map/ppermute | solution.py:83
  32.2 4.3 %collective-permute-done.19 = bf16[848,128]{1,0:T(8,128)(2,1)S(1)} collective-permute-done((bf16[848,128]{1,0:T(8,128)(2,1)S(1)}, bf16[848,128]{1,0:T(8,128)(2,1)S(1)}, u32[]{:S(2)}, u32[]{:S(2)}) %collective-permute-start.19) | collective-permute-done | bytes 217120 | tf_op jit(solution)/shard_map/ppermute | solution.py:80
  40.2 6.5 %collective-permute-done.16 = bf16[848,128]{1,0:T(8,128)(2,1)S(1)} collective-permute-done((bf16[848,128]{1,0:T(8,128)(2,1)S(1)}, bf16[848,128]{1,0:T(8,128)(2,1)S(1)}, u32[]{:S(2)}, u32[]{:S(2)}) %collective-permute-start.16) | collective-permute-done | bytes 217120 | tf_op jit(solution)/shard_map/ppermute | solution.py:83
  52.0 9.0 %collective-permute-done.8 = bf16[392,512]{1,0:T(8,128)(2,1)S(1)} collective-permute-done((bf16[392,512]{1,0:T(8,128)(2,1)S(1)}, bf16[392,512]{1,0:T(8,128)(2,1)S(1)}, u32[]{:S(2)}, u32[]{:S(2)}) %collective-permute-start.8) | collective-permute-done | bytes 401440 | tf_op jit(solution)/shard_map/ppermute | solution.py:83
  65.2 6.0 %collective-permute-done.4 = bf16[392,512]{1,0:T(8,128)(2,1)S(1)} collective-permute-done((bf16[392,512]{1,0:T(8,128)(2,1)S(1)}, bf16[392,512]{1,0:T(8,128)(2,1)S(1)}, u32[]{:S(2)}, u32[]{:S(2)}) %collective-permute-start.4) | collective-permute-done | bytes 401440 | tf_op jit(solution)/shard_map/ppermute | solution.py:80
  74.6 6.3 %collective-permute-done.5.f = bf16[392,512]{1,0:T(8,128)(2,1)S(1)} collective-permute-done((bf16[392,512]{1,0:T(8,128)(2,1)S(1)}, bf16[392,512]{1,0:T(8,128)(2,1)S(1)}, u32[]{:S(2)}, u32[]{:S(2)}) %collective-permute-start.5) | collective-permute-done | bytes 401440 | tf_op jit(solution)/shard_map/ppermute | solution.py:80
  93.2 3.4 %shard_map.319 = bf16[9,512,512]{2,1,0:T(8,128)(2,1)S(1)} custom-call(s32[40]{0:T(128)S(1)} %copy-done.18, bf16[1,5,576,128]{3,2,1,0:T(8,128)(2,1)S(1)} %bitcast.236, bf16[1,5,576,128]{3,2,1,0:T(8,128)(2,1)S(1)} %collective-permute-done.21.refs_1_, bf16[1,3,576,128]{3,2,1,0:T(8,128)(2,1)S(1)} %maximum_bitcast_fusion.refs_2_, ...), custom_call_target="tpu_custom_call" | custom-call | tf_op jit(solution)/shard_map/pallas_call | solution.py:173
  96.7 4.8 %shard_map.320 = (f32[448,512]{1,0:T(8,128)S(1)}, bf16[392,512]{1,0:T(8,128)(2,1)S(1)}, f32[2,512]{1,0:T(2,128)S(1)}, bf16[448,512]{1,0:T(8,128)(2,1)}) custom-call(s32[40]{0:T(128)S(1)} %copy-done.18, f32[448,512]{1,0:T(8,128)S(1)} %get-tuple-element.51.pre.pre_one, f32[2,512]{1,0:T(2,128)S(1)} %add.300.stat.stat_one, ...), custom_call_target="tpu_custom_call" | custom-call | flops 2113929216 | bytes 8388608 | tf_op jit(solution)/shard_map/pallas_call | solution.py:173
  114.6 6.8 %collective-permute-done.30 = f32[2,512]{1,0:T(2,128)S(1)} collective-permute-done((f32[2,512]{1,0:T(2,128)S(1)}, f32[2,512]{1,0:T(2,128)S(1)}, u32[]{:S(2)}, u32[]{:S(2)}) %collective-permute-start.30) | collective-permute-done | bytes 4128 | tf_op jit(solution)/shard_map/ppermute | solution.py:153
  141.5 3.6 %shard_map.322 = (bf16[8,392,512]{2,1,0:T(8,128)(2,1)S(1)}, f32[8,392,256]{2,1,0:T(8,128)S(1)}, f32[4,256]{1,0:T(4,128)S(1)}) custom-call(s32[40]{0:T(128)S(1)} %copy-done.18, bf16[392,512]{1,0:T(8,128)(2,1)S(1)} %get-tuple-element.54.refs_0_, bf16[392,512]{1,0:T(8,128)(2,1)S(1)} %collective-permute-done.32.refs_1_, ...), custom_call_target="tpu_custom_call" | custom-call | flops 513802240 | bytes 6021120 | tf_op jit(solution)/shard_map/pallas_call | solution.py:173
  152.7 3.3 %collective-permute-done.45 = f32[4,256]{1,0:T(4,128)S(1)} collective-permute-done((f32[4,256]{1,0:T(4,128)S(1)}, f32[4,256]{1,0:T(4,128)S(1)}, u32[]{:S(2)}, u32[]{:S(2)}) %collective-permute-start.45) | collective-permute-done | bytes 4128 | tf_op jit(solution)/shard_map/ppermute | solution.py:153
  156.1 5.2 %shard_map.324 = (f32[8,392,256]{2,1,0:T(8,128)}, f32[8,392,256]{2,1,0:T(8,128)S(1)}, f32[4,256]{1,0:T(4,128)S(1)}) custom-call(s32[40]{0:T(128)S(1)} %copy-done.18, f32[8,392,256]{2,1,0:T(8,128)S(1)} %get-tuple-element.57.pre.refs_0_, f32[4,256]{1,0:T(4,128)S(1)} %add.314.stat.refs_1_, f32[2,256]{1,0:T(2,128)S(1)} %copy-done.19, ...), custom_call_target="tpu_custom_call" | custom-call | flops 16056320 | bytes 12845056 | tf_op jit(solution)/shard_map/pallas_call | solution.py:173
  174.0 3.6 %shard_map.333 = bf16[8,64,256]{2,1,0:T(8,128)(2,1)S(1)} custom-call(s32[40]{0:T(128)S(1)} %copy-done.18, bf16[8,392,512]{2,1,0:T(8,128)(2,1)S(1)} %copy-done.6, bf16[8,392,256]{2,1,0:T(8,128)(2,1)S(1)} %get-tuple-element.80.back), custom_call_target="tpu_custom_call" | custom-call | flops 822083584 | bytes 4816896 | tf_op jit(solution)/shard_map/pallas_call | solution.py:173
  180.6 8.9 %collective-permute-done.53 = bf16[392,512]{1,0:T(8,128)(2,1)S(1)} collective-permute-done((bf16[392,512]{1,0:T(8,128)(2,1)S(1)}, bf16[392,512]{1,0:T(8,128)(2,1)S(1)}, u32[]{:S(2)}, u32[]{:S(2)}) %collective-permute-start.53) | collective-permute-done | bytes 401440 | tf_op jit(solution)/shard_map/ppermute | solution.py:83
  192.0 8.5 %collective-permute-done.54 = bf16[392,512]{1,0:T(8,128)(2,1)S(1)} collective-permute-done((bf16[392,512]{1,0:T(8,128)(2,1)S(1)}, bf16[392,512]{1,0:T(8,128)(2,1)S(1)}, u32[]{:S(2)}, u32[]{:S(2)}) %collective-permute-start.54) | collective-permute-done | bytes 401440 | tf_op jit(solution)/shard_map/ppermute | solution.py:83
  205.0 6.2 %collective-permute-done.50 = bf16[392,512]{1,0:T(8,128)(2,1)S(1)} collective-permute-done((bf16[392,512]{1,0:T(8,128)(2,1)S(1)}, bf16[392,512]{1,0:T(8,128)(2,1)S(1)}, u32[]{:S(2)}, u32[]{:S(2)}) %collective-permute-start.50) | collective-permute-done | bytes 401440 | tf_op jit(solution)/shard_map/ppermute | solution.py:80
  212.9 8.0 %collective-permute-done.51.f = bf16[392,512]{1,0:T(8,128)(2,1)S(1)} collective-permute-done((bf16[392,512]{1,0:T(8,128)(2,1)S(1)}, bf16[392,512]{1,0:T(8,128)(2,1)S(1)}, u32[]{:S(2)}, u32[]{:S(2)}) %collective-permute-start.51) | collective-permute-done | bytes 401440 | tf_op jit(solution)/shard_map/ppermute | solution.py:80
  234.7 4.6 %shard_map.328 = (bf16[2,448,128]{2,1,0:T(8,128)(2,1)S(1)}, bf16[2,448,128]{2,1,0:T(8,128)(2,1)S(1)}, f32[448,512]{1,0:T(8,128)S(1)}, f32[2,512]{1,0:T(2,128)S(1)}) custom-call(s32[40]{0:T(128)S(1)} %copy-done.18, f32[448,512]{1,0:T(8,128)S(1)} %get-tuple-element.68.up, f32[2,512]{1,0:T(2,128)S(1)} %add.326.sums, f32[448,512]{1,0:T(8,128)S(1)} %copy-done.15, ...), custom_call_target="tpu_custom_call" | custom-call | flops 2113929216 | bytes 8388608 | tf_op jit(solution)/shard_map/pallas_call | solution.py:173
  253.4 4.5 %shard_map.330 = bf16[8,576,128]{2,1,0:T(8,128)(2,1)S(1)} custom-call(s32[40]{0:T(128)S(1)} %copy-done.18, bf16[4,448,512]{2,1,0:T(8,128)(2,1)S(1)} %pad_maximum_fusion.refs_0_, bf16[4,1,448,128]{3,2,1,0:T(8,128)(2,1)S(1)} %pad_maximum_fusion.2.refs_1_, bf16[392,512]{1,0:T(8,128)(2,1)S(1)} %shard_map.329.refs_2_.refs_0_), custom_call_target="tpu_custom_call" | custom-call | flops 2113929216 | bytes 8388608 | tf_op jit(solution)/shard_map/pallas_call | solution.py:173
  265.4 5.3 %collective-permute-done.96 = f32[2,512]{1,0:T(2,128)S(1)} collective-permute-done((f32[2,512]{1,0:T(2,128)S(1)}, f32[2,512]{1,0:T(2,128)S(1)}, u32[]{:S(2)}, u32[]{:S(2)}) %collective-permute-start.96) | collective-permute-done | bytes 4128 | tf_op jit(solution)/shard_map/ppermute | solution.py:153
  276.9 8.0 %collective-permute-done.65.refs_3_ = bf16[392,512]{1,0:T(8,128)(2,1)S(1)} collective-permute-done((bf16[392,512]{1,0:T(8,128)(2,1)S(1)}, bf16[392,512]{1,0:T(8,128)(2,1)S(1)}, u32[]{:S(2)}, u32[]{:S(2)}) %collective-permute-start.65) | collective-permute-done | bytes 401440 | tf_op jit(solution)/shard_map/ppermute | solution.py:80
  290.7 5.9 %shard_map.331 = (f32[8,392,256]{2,1,0:T(8,128)}, f32[256,512]{1,0:T(8,128)S(1)}) custom-call(s32[40]{0:T(128)S(1)} %copy-done.18, bf16[392,512]{1,0:T(8,128)(2,1)S(1)} %shard_map.329.refs_2_.refs_0_, bf16[392,512]{1,0:T(8,128)(2,1)S(1)} %collective-permute-done.64.refs_1_, bf16[392,512]{1,0:T(8,128)(2,1)S(1)} %collective-permute-done.67.refs_2_, ...), custom_call_target="tpu_custom_call" | custom-call | flops 1027604480 | bytes 7024640 | tf_op jit(solution)/shard_map/pallas_call | solution.py:173
  304.1 4.1 %shard_map.332 = (f32[8,392,256]{2,1,0:T(8,128)}, bf16[256,512]{1,0:T(8,128)(2,1)S(1)}) custom-call(s32[40]{0:T(128)S(1)} %copy-done.18, bf16[392,512]{1,0:T(8,128)(2,1)S(1)} %collective-permute-done.66.refs_0_, bf16[392,512]{1,0:T(8,128)(2,1)S(1)} %collective-permute-done.69.refs_1_, ...), custom_call_target="tpu_custom_call", output_to_operand_aliasing={{0}: (9, {})} | custom-call | flops 616562688 | bytes 4214784 | tf_op jit(solution)/shard_map/pallas_call | solution.py:173
  (394 shorter events, 177.7 us)
Async XLA Ops:
  2.4 21.8 %collective-permute-start.14 = (bf16[848,128]{1,0:T(8,128)(2,1)}, bf16[848,128]{1,0:T(8,128)(2,1)S(1)}, u32[]{:S(2)}, u32[]{:S(2)}) collective-permute-start(bf16[848,128]{1,0:T(8,128)(2,1)} %shard_map.318), channel_id=1, source_target_pairs={{2,0},{4,2},{6,4},{7,6},{5,7},{3,5},{1,3},{0,1},{10,8},{12,10},{14... | collective-permute-start | bytes 651272 | tf_op jit(solution)/shard_map/ppermute | solution.py:83
  5.3 20.6 %collective-permute-start.18 = (bf16[848,128]{1,0:T(8,128)(2,1)}, bf16[848,128]{1,0:T(8,128)(2,1)S(1)}, u32[]{:S(2)}, u32[]{:S(2)}) collective-permute-start(bf16[848,128]{1,0:T(8,128)(2,1)} %shard_map.318), channel_id=1, source_target_pairs={{0,2},{2,4},{4,6},{6,7},{7,5},{5,3},{3,1},{1,0},{8,10},{10,12},{12... | collective-permute-start | bytes 651272 | tf_op jit(solution)/shard_map/ppermute | solution.py:80
  24.2 12.4 %collective-permute-start.15 = (bf16[848,128]{1,0:T(8,128)(2,1)S(1)}, bf16[848,128]{1,0:T(8,128)(2,1)S(1)}, u32[]{:S(2)}, u32[]{:S(2)}) collective-permute-start(bf16[848,128]{1,0:T(8,128)(2,1)S(1)} %collective-permute-done.14), channel_id=1, source_target_pairs={{2,0},{4,2},{6,4},{7,6},{5,7},{3,5},{1,3},{0,1},{10,8},{12,10},{14... | collective-permute-start | bytes 651272 | tf_op jit(solution)/shard_map/ppermute | solution.py:83
  29.9 19.8 %collective-permute-start.7 = (bf16[392,512]{1,0:T(8,128)(2,1)S(1)}, bf16[392,512]{1,0:T(8,128)(2,1)S(1)}, u32[]{:S(2)}, u32[]{:S(2)}) collective-permute-start(bf16[392,512]{1,0:T(8,128)(2,1)S(1)} %pad_maximum_fusion.4), channel_id=1, source_target_pairs={{2,0},{4,2},{6,4},{7,6},{5,7},{3,5},{1,3},{0,1},{10,8},{12,10},{14... | collective-permute-start | bytes 1204232 | tf_op jit(solution)/shard_map/ppermute | solution.py:83
  31.9 19.6 %collective-permute-start.3 = (bf16[392,512]{1,0:T(8,128)(2,1)S(1)}, bf16[392,512]{1,0:T(8,128)(2,1)S(1)}, u32[]{:S(2)}, u32[]{:S(2)}) collective-permute-start(bf16[392,512]{1,0:T(8,128)(2,1)S(1)} %pad_maximum_fusion.3), channel_id=1, source_target_pairs={{0,2},{2,4},{4,6},{6,7},{7,5},{5,3},{3,1},{1,0},{8,10},{10,12},{12... | collective-permute-start | bytes 1204232 | tf_op jit(solution)/shard_map/ppermute | solution.py:80
  36.5 37.0 %collective-permute-start.21 = (bf16[1,5,576,128]{3,2,1,0:T(8,128)(2,1)S(1)}, bf16[1,5,576,128]{3,2,1,0:T(8,128)(2,1)S(1)}, u32[]{:S(2)}, u32[]{:S(2)}) collective-permute-start(bf16[1,5,576,128]{3,2,1,0:T(8,128)(2,1)S(1)} %bitcast.234), channel_id=1, source_target_pairs={{0,16},{8,24},{16,0},{24,8},{1,17},{9,25},{17,1},{25,9},{2,18},{10... | collective-permute-start | bytes 2211848 | tf_op jit(solution)/shard_map/ppermute | solution.py:153
  46.7 46.5 %collective-permute-start.24 = (bf16[1,5,576,128]{3,2,1,0:T(8,128)(2,1)S(1)}, bf16[1,5,576,128]{3,2,1,0:T(8,128)(2,1)}, u32[]{:S(2)}, u32[]{:S(2)}) collective-permute-start(bf16[1,5,576,128]{3,2,1,0:T(8,128)(2,1)S(1)} %bitcast.235), channel_id=1, source_target_pairs={{0,8},{8,0},{16,24},{24,16},{1,9},{9,1},{17,25},{25,17},{2,10},{10... | collective-permute-start | bytes 2211848 | tf_op jit(solution)/shard_map/ppermute | solution.py:153
  48.1 14.6 %collective-permute-start.17 = (bf16[424,128]{1,0:T(8,128)(2,1)S(1)}, bf16[424,128]{1,0:T(8,128)(2,1)S(1)}, u32[]{:S(2)}, u32[]{:S(2)}) collective-permute-start(bf16[424,128]{1,0:T(8,128)(2,1)S(1)} %slice.413), channel_id=1, source_target_pairs={{2,0},{4,2},{6,4},{7,6},{5,7},{3,5},{1,3},{0,1},{10,8},{12,10},{14... | collective-permute-start | bytes 325640 | tf_op jit(solution)/shard_map/ppermute | solution.py:83
  62.8 20.0 %collective-permute-start.23 = (bf16[1,3,576,128]{3,2,1,0:T(8,128)(2,1)S(1)}, bf16[1,3,576,128]{3,2,1,0:T(8,128)(2,1)S(1)}, u32[]{:S(2)}, u32[]{:S(2)}) collective-permute-start(bf16[1,3,576,128]{3,2,1,0:T(8,128)(2,1)S(1)} %maximum_bitcast_fusion.refs_2_), channel_id=1, source_target_pairs={{0,16},{8,24},{16,0},{24,8},{1,17},{9,25},{17,1},{25,9},{2,18},{10... | collective-permute-start | bytes 1327112 | tf_op jit(solution)/shard_map/ppermute | solution.py:153
  73.6 19.6 %collective-permute-start.26 = (bf16[1,3,576,128]{3,2,1,0:T(8,128)(2,1)S(1)}, bf16[1,3,576,128]{3,2,1,0:T(8,128)(2,1)}, u32[]{:S(2)}, u32[]{:S(2)}) collective-permute-start(bf16[1,3,576,128]{3,2,1,0:T(8,128)(2,1)S(1)} %maximum_bitcast_fusion.refs_2_), channel_id=1, source_target_pairs={{0,8},{8,0},{16,24},{24,16},{1,9},{9,1},{17,25},{25,17},{2,10},{10... | collective-permute-start | bytes 1327112 | tf_op jit(solution)/shard_map/ppermute | solution.py:153
  74.6 18.6 %collective-permute-start.25 = (bf16[1,5,576,128]{3,2,1,0:T(8,128)(2,1)S(1)}, bf16[1,5,576,128]{3,2,1,0:T(8,128)(2,1)}, u32[]{:S(2)}, u32[]{:S(2)}) collective-permute-start(bf16[1,5,576,128]{3,2,1,0:T(8,128)(2,1)S(1)} %collective-permute-done.21.refs_1_), channel_id=1, source_target_pairs={{0,8},{8,0},{16,24},{24,16},{1,9},{9,1},{17,25},{25,17},{2,10},{10... | collective-permute-start | bytes 2211848 | tf_op jit(solution)/shard_map/ppermute | solution.py:153
  111.2 17.4 %collective-permute-start.33 = (bf16[392,512]{1,0:T(8,128)(2,1)S(1)}, bf16[392,512]{1,0:T(8,128)(2,1)S(1)}, u32[]{:S(2)}, u32[]{:S(2)}) collective-permute-start(bf16[392,512]{1,0:T(8,128)(2,1)S(1)} %broadcast_select_fusion.1), channel_id=1, source_target_pairs={{0,2},{2,4},{4,6},{6,7},{7,5},{5,3},{3,1},{1,0},{8,10},{10,12},{12... | collective-permute-start | bytes 1204232 | tf_op jit(solution)/shard_map/ppermute | solution.py:80
  113.0 17.7 %collective-permute-start.36 = (bf16[392,512]{1,0:T(8,128)(2,1)}, bf16[392,512]{1,0:T(8,128)(2,1)S(1)}, u32[]{:S(2)}, u32[]{:S(2)}) collective-permute-start(bf16[392,512]{1,0:T(8,128)(2,1)} %broadcast_select_fusion), channel_id=1, source_target_pairs={{2,0},{4,2},{6,4},{7,6},{5,7},{3,5},{1,3},{0,1},{10,8},{12,10},{14... | collective-permute-start | bytes 1204232 | tf_op jit(solution)/shard_map/ppermute | solution.py:83
  137.6 25.1 %collective-permute-start.72 = (bf16[1,448,512]{2,1,0:T(8,128)(2,1)}, bf16[1,448,512]{2,1,0:T(8,128)(2,1)}, u32[]{:S(2)}, u32[]{:S(2)}) collective-permute-start(bf16[1,448,512]{2,1,0:T(8,128)(2,1)} %bitcast.41), channel_id=1, source_target_pairs={{0,8},{8,0},{16,24},{24,16},{1,9},{9,1},{17,25},{25,17},{2,10},{10... | collective-permute-start | bytes 1376264 | tf_op jit(solution)/shard_map/ppermute | solution.py:153
  164.0 26.1 %collective-permute-start.73 = (bf16[2,448,512]{2,1,0:T(8,128)(2,1)S(1)}, bf16[2,448,512]{2,1,0:T(8,128)(2,1)S(1)}, u32[]{:S(2)}, u32[]{:S(2)}) collective-permute-start(bf16[2,448,512]{2,1,0:T(8,128)(2,1)S(1)} %pad_maximum_fusion.1), channel_id=1, source_target_pairs={{0,16},{8,24},{16,0},{24,8},{1,17},{9,25},{17,1},{25,9},{2,18},{10... | collective-permute-start | bytes 2752520 | tf_op jit(solution)/shard_map/ppermute | solution.py:153
  178.4 13.7 %collective-permute-start.49 = (bf16[392,512]{1,0:T(8,128)(2,1)S(1)}, bf16[392,512]{1,0:T(8,128)(2,1)S(1)}, u32[]{:S(2)}, u32[]{:S(2)}) collective-permute-start(bf16[392,512]{1,0:T(8,128)(2,1)S(1)} %pad_maximum_fusion.5), channel_id=1, source_target_pairs={{0,2},{2,4},{4,6},{6,7},{7,5},{5,3},{3,1},{1,0},{8,10},{10,12},{12... | collective-permute-start | bytes 1204232 | tf_op jit(solution)/shard_map/ppermute | solution.py:80
  211.7 12.3 %collective-permute-start.89 = (bf16[64,512]{1,0:T(8,128)(2,1)S(1)}, bf16[64,512]{1,0:T(8,128)(2,1)S(1)}, u32[]{:S(2)}, u32[]{:S(2)}) collective-permute-start(bf16[64,512]{1,0:T(8,128)(2,1)S(1)} %pad_maximum_fusion.12), channel_id=1, source_target_pairs={{0,2},{2,4},{4,6},{6,7},{7,5},{5,3},{3,1},{1,0},{8,10},{10,12},{12... | collective-permute-start | bytes 196616 | tf_op jit(solution)/shard_map/ppermute | solution.py:80
  260.1 12.6 %collective-permute-start.64 = (bf16[392,512]{1,0:T(8,128)(2,1)S(1)}, bf16[392,512]{1,0:T(8,128)(2,1)S(1)}, u32[]{:S(2)}, u32[]{:S(2)}) collective-permute-start(bf16[392,512]{1,0:T(8,128)(2,1)S(1)} %shard_map.329.refs_2_.refs_0_), channel_id=1, source_target_pairs={{0,2},{2,4},{4,6},{6,7},{7,5},{5,3},{3,1},{1,0},{8,10},{10,12},{12... | collective-permute-start | bytes 1204232 | tf_op jit(solution)/shard_map/ppermute | solution.py:80
  260.6 12.5 %collective-permute-start.67 = (bf16[392,512]{1,0:T(8,128)(2,1)S(1)}, bf16[392,512]{1,0:T(8,128)(2,1)S(1)}, u32[]{:S(2)}, u32[]{:S(2)}) collective-permute-start(bf16[392,512]{1,0:T(8,128)(2,1)S(1)} %shard_map.329.refs_2_.refs_0_), channel_id=1, source_target_pairs={{2,0},{4,2},{6,4},{7,6},{5,7},{3,5},{1,3},{0,1},{10,8},{12,10},{14... | collective-permute-start | bytes 1204232 | tf_op jit(solution)/shard_map/ppermute | solution.py:83
  272.7 12.2 %collective-permute-start.65 = (bf16[392,512]{1,0:T(8,128)(2,1)S(1)}, bf16[392,512]{1,0:T(8,128)(2,1)S(1)}, u32[]{:S(2)}, u32[]{:S(2)}) collective-permute-start(bf16[392,512]{1,0:T(8,128)(2,1)S(1)} %collective-permute-done.64.refs_1_), channel_id=1, source_target_pairs={{0,2},{2,4},{4,6},{6,7},{7,5},{5,3},{3,1},{1,0},{8,10},{10,12},{12... | collective-permute-start | bytes 1204232 | tf_op jit(solution)/shard_map/ppermute | solution.py:80
  273.1 12.2 %collective-permute-start.68 = (bf16[392,512]{1,0:T(8,128)(2,1)S(1)}, bf16[392,512]{1,0:T(8,128)(2,1)S(1)}, u32[]{:S(2)}, u32[]{:S(2)}) collective-permute-start(bf16[392,512]{1,0:T(8,128)(2,1)S(1)} %collective-permute-done.67.refs_2_), channel_id=1, source_target_pairs={{2,0},{4,2},{6,4},{7,6},{5,7},{3,5},{1,3},{0,1},{10,8},{12,10},{14... | collective-permute-start | bytes 1204232 | tf_op jit(solution)/shard_map/ppermute | solution.py:83
  284.9 12.5 %collective-permute-start.66 = (bf16[392,512]{1,0:T(8,128)(2,1)S(1)}, bf16[392,512]{1,0:T(8,128)(2,1)S(1)}, u32[]{:S(2)}, u32[]{:S(2)}) collective-permute-start(bf16[392,512]{1,0:T(8,128)(2,1)S(1)} %collective-permute-done.65.refs_3_), channel_id=1, source_target_pairs={{0,2},{2,4},{4,6},{6,7},{7,5},{5,3},{3,1},{1,0},{8,10},{10,12},{12... | collective-permute-start | bytes 1204232 | tf_op jit(solution)/shard_map/ppermute | solution.py:80
  285.3 12.6 %collective-permute-start.69 = (bf16[392,512]{1,0:T(8,128)(2,1)S(1)}, bf16[392,512]{1,0:T(8,128)(2,1)S(1)}, u32[]{:S(2)}, u32[]{:S(2)}) collective-permute-start(bf16[392,512]{1,0:T(8,128)(2,1)S(1)} %collective-permute-done.68.refs_4_), channel_id=1, source_target_pairs={{2,0},{4,2},{6,4},{7,6},{5,7},{3,5},{1,3},{0,1},{10,8},{12,10},{14... | collective-permute-start | bytes 1204232 | tf_op jit(solution)/shard_map/ppermute | solution.py:83
  296.6 12.2 %collective-permute-start.81 = (bf16[576,128]{1,0:T(8,128)(2,1)}, bf16[576,128]{1,0:T(8,128)(2,1)}, u32[]{:S(2)}, u32[]{:S(2)}) collective-permute-start(bf16[576,128]{1,0:T(8,128)(2,1)} %get-tuple-element.110), channel_id=1, source_target_pairs={{0,2},{2,4},{4,6},{6,7},{7,5},{5,3},{3,1},{1,0},{8,10},{10,12},{12... | collective-permute-start | bytes 442376 | tf_op jit(solution)/shard_map/ppermute | solution.py:80
  (111 other events, 1051.4 us)

commit v3 on v2

--- a/solution.py
+++ b/solution.py
@@ -86,6 +86,10 @@
 def tie(x, other):
     first = lax.slice(other, (0,) * other.ndim, (1,) * other.ndim).reshape(())
     return jnp.where(first > -3e38, x, jnp.zeros_like(x))
+
+
+def beside(x, other):
+    return jnp.where(other > -3e38, x, jnp.zeros_like(x))
 
 
 class Gather:
@@ -127,7 +131,7 @@
             half = width // 2
             f = jnp.concatenate(
                 [
-                    add16(lax.slice_in_dim(left, 0, half, axis=axis), self.f),
+                    beside(add16(lax.slice_in_dim(left, 0, half, axis=axis), self.f), self.b),
                     lax.slice_in_dim(left, half, width, axis=axis),
                 ],
                 axis,
@@ -135,12 +139,13 @@
             b = jnp.concatenate(
                 [
                     lax.slice_in_dim(right, 0, half, axis=axis),
-                    add16(lax.slice_in_dim(right, half, width, axis=axis), self.b),
+                    beside(add16(lax.slice_in_dim(right, half, width, axis=axis), self.b), self.f),
                 ],
                 axis,
             )
         else:
-            f, b = add16(left, self.f), add16(right, self.b)
+            f = beside(add16(left, self.f), self.b)
+            b = beside(add16(right, self.b), self.f)
         self.count += 1
         self.f, self.b = self.ring.fw(f), self.ring.bw(b)
 

time: 316 us -> 296 us (0.937)
  waiting for transfers between devices: 136 us -> 113 us
  starting transfers between devices: 90.3 us -> 96.4 us
    ppermute x28, waiting for transfers between devices: 42.3 us -> 22.1 us  [bw(): return lax.ppermute(x, 'chan', self.back)]
    ppermute x28, starting transfers between devices: 23.2 us -> 30.2 us  [fw(): return lax.ppermute(x, 'chan', self.ahead)]
    ppermute x28, waiting for transfers between devices: 47.8 us -> 42.9 us  [fw(): return lax.ppermute(x, 'chan', self.ahead)]
    ppermute x28, starting transfers between devices: 34.5 us -> 31.2 us  [bw(): return lax.ppermute(x, 'chan', self.back)]
    unnamed x85 -> x87, local copies, waits for them, and re-layouts: 9.5 us -> 9.69 us
  transfers between devices with their start and end apart: 98 -> 98, of which waited for: 47 -> 51; matrix products, arithmetic and copies ran while one was open for 6% -> 6% of each run, Pallas kernels for 14% -> 13%
where the time goes in v3:
time: 296 us; the launch traced here: 295 us
  waiting for transfers between devices  113 us (38%)
  starting transfers between devices  96.4 us (33%)
  Pallas kernels  55.7 us (19%)
  local copies, waits for them, and re-layouts  13.9 us (5%)
  other arithmetic  12.8 us (4%)
  between operations  3.76 us (1%)
    pallas_call x18, Pallas kernels, run(): pl.pallas_call(kernel if extra else body, grid_spec=pltpu.PrefetchScalarG...  52.6 us
    ppermute x39, waiting for transfers between devices, swap(): return lax.ppermute(x, axis, [(i, i ^ bit) for i in range(size)])  47.6 us
    ppermute x28, waiting for transfers between devices, fw(): return lax.ppermute(x, 'chan', self.ahead)  42.9 us
    ppermute x28, starting transfers between devices, bw(): return lax.ppermute(x, 'chan', self.back)  31.2 us
    ppermute x28, starting transfers between devices, fw(): return lax.ppermute(x, 'chan', self.ahead)  30.2 us
    ppermute x39, starting transfers between devices, swap(): return lax.ppermute(x, axis, [(i, i ^ bit) for i in range(size)])  29.5 us
    ppermute x28, waiting for transfers between devices, bw(): return lax.ppermute(x, 'chan', self.back)  22.1 us
    unnamed x87, local copies, waits for them, and re-layouts  9.69 us
  transfers between devices with their start and end apart: 98, of which 51 were waited for; matrix products, arithmetic and copies ran while one was open for 6% of the time, Pallas kernels for 13%

profile of v3, /device:TPU:0, one launch (start us, length us, event | category | flops | bytes accessed | tf_op | source)
XLA Modules:
  0.0 295.1 jit_solution(17068949135900015046)
XLA Ops:
  12.3 3.5 %collective-permute-done.1 = bf16[256,256]{1,0:T(8,128)(2,1)S(1)} collective-permute-done((bf16[256,256]{1,0:T(8,128)(2,1)S(1)}, bf16[256,256]{1,0:T(8,128)(2,1)S(1)}, u32[]{:S(2)}, u32[]{:S(2)}) %collective-permute-start.1) | collective-permute-done | bytes 131104 | tf_op jit(solution)/shard_map/ppermute | solution.py:158
  25.6 3.6 %collective-permute-done.2 = bf16[392,256]{1,0:T(8,128)(2,1)S(1)} collective-permute-done((bf16[392,256]{1,0:T(8,128)(2,1)S(1)}, bf16[392,256]{1,0:T(8,128)(2,1)S(1)}, u32[]{:S(2)}, u32[]{:S(2)}) %collective-permute-start.2) | collective-permute-done | bytes 200736 | tf_op jit(solution)/shard_map/ppermute | solution.py:83
  38.9 7.1 %collective-permute-done.16 = bf16[848,128]{1,0:T(8,128)(2,1)S(1)} collective-permute-done((bf16[848,128]{1,0:T(8,128)(2,1)S(1)}, bf16[848,128]{1,0:T(8,128)(2,1)S(1)}, u32[]{:S(2)}, u32[]{:S(2)}) %collective-permute-start.16) | collective-permute-done | bytes 217120 | tf_op jit(solution)/shard_map/ppermute | solution.py:83
  47.7 4.8 %collective-permute-done.20 = bf16[848,128]{1,0:T(8,128)(2,1)S(1)} collective-permute-done((bf16[848,128]{1,0:T(8,128)(2,1)S(1)}, bf16[848,128]{1,0:T(8,128)(2,1)S(1)}, u32[]{:S(2)}, u32[]{:S(2)}) %collective-permute-start.20) | collective-permute-done | bytes 217120 | tf_op jit(solution)/shard_map/ppermute | solution.py:80
  61.2 4.6 %collective-permute-done.7 = bf16[392,512]{1,0:T(8,128)(2,1)S(1)} collective-permute-done((bf16[392,512]{1,0:T(8,128)(2,1)S(1)}, bf16[392,512]{1,0:T(8,128)(2,1)S(1)}, u32[]{:S(2)}, u32[]{:S(2)}) %collective-permute-start.7) | collective-permute-done | bytes 401440 | tf_op jit(solution)/shard_map/ppermute | solution.py:80
  68.4 6.2 %collective-permute-done.8.f = bf16[392,512]{1,0:T(8,128)(2,1)S(1)} collective-permute-done((bf16[392,512]{1,0:T(8,128)(2,1)S(1)}, bf16[392,512]{1,0:T(8,128)(2,1)S(1)}, u32[]{:S(2)}, u32[]{:S(2)}) %collective-permute-start.8) | collective-permute-done | bytes 401440 | tf_op jit(solution)/shard_map/ppermute | solution.py:80
  88.6 3.4 %shard_map.319 = bf16[9,512,512]{2,1,0:T(8,128)(2,1)S(1)} custom-call(s32[40]{0:T(128)S(1)} %copy-done.19, bf16[1,5,576,128]{3,2,1,0:T(8,128)(2,1)S(1)} %bitcast.239, bf16[1,5,576,128]{3,2,1,0:T(8,128)(2,1)S(1)} %collective-permute-done.21.refs_1_, bf16[1,3,576,128]{3,2,1,0:T(8,128)(2,1)S(1)} %maximum_bitcast_fusion.refs_2_, ...), custom_call_target="tpu_custom_call" | custom-call | tf_op jit(solution)/shard_map/pallas_call | solution.py:178
  92.1 4.0 %shard_map.320 = (f32[448,512]{1,0:T(8,128)S(1)}, bf16[392,512]{1,0:T(8,128)(2,1)S(1)}, f32[2,512]{1,0:T(2,128)S(1)}, bf16[448,512]{1,0:T(8,128)(2,1)S(1)}) custom-call(s32[40]{0:T(128)S(1)} %copy-done.19, f32[448,512]{1,0:T(8,128)S(1)} %get-tuple-element.51.pre.pre_one, f32[2,512]{1,0:T(2,128)S(1)} %add.300.stat.stat_one, ...), custom_call_target="tpu_custom_call" | custom-call | flops 2113929216 | bytes 8388608 | tf_op jit(solution)/shard_map/pallas_call | solution.py:178
  109.7 7.1 %collective-permute-done.30 = f32[2,512]{1,0:T(2,128)S(1)} collective-permute-done((f32[2,512]{1,0:T(2,128)S(1)}, f32[2,512]{1,0:T(2,128)S(1)}, u32[]{:S(2)}, u32[]{:S(2)}) %collective-permute-start.30) | collective-permute-done | bytes 4128 | tf_op jit(solution)/shard_map/ppermute | solution.py:158
  121.0 3.4 %collective-permute-start.38 = (f32[2,512]{1,0:T(2,128)S(1)}, f32[2,512]{1,0:T(2,128)S(1)}, u32[]{:S(2)}, u32[]{:S(2)}) collective-permute-start(f32[2,512]{1,0:T(2,128)S(1)} %add.306.stat.stat_two), channel_id=1, source_target_pairs={{0,4},{1,5},{2,6},{3,7},{4,0},{5,1},{6,2},{7,3},{8,12},{9,13},{10,... | collective-permute-start | bytes 12296 | tf_op jit(solution)/shard_map/ppermute | solution.py:158
  128.5 2.9 collective-permute-start.42
  137.6 3.6 %shard_map.322 = (bf16[8,392,512]{2,1,0:T(8,128)(2,1)S(1)}, f32[8,392,256]{2,1,0:T(8,128)S(1)}, f32[4,256]{1,0:T(4,128)S(1)}) custom-call(s32[40]{0:T(128)S(1)} %copy-done.19, bf16[392,512]{1,0:T(8,128)(2,1)S(1)} %get-tuple-element.54.refs_0_, bf16[392,512]{1,0:T(8,128)(2,1)S(1)} %collective-permute-done.32.refs_1_, ...), custom_call_target="tpu_custom_call" | custom-call | flops 513802240 | bytes 6021120 | tf_op jit(solution)/shard_map/pallas_call | solution.py:178
  151.7 5.2 %shard_map.324 = (f32[8,392,256]{2,1,0:T(8,128)}, f32[8,392,256]{2,1,0:T(8,128)S(1)}, f32[4,256]{1,0:T(4,128)S(1)}) custom-call(s32[40]{0:T(128)S(1)} %copy-done.19, f32[8,392,256]{2,1,0:T(8,128)S(1)} %get-tuple-element.57.pre.refs_0_, f32[4,256]{1,0:T(4,128)S(1)} %add.314.stat.refs_1_, f32[2,256]{1,0:T(2,128)S(1)} %copy-done.20, ...), custom_call_target="tpu_custom_call" | custom-call | flops 16056320 | bytes 12845056 | tf_op jit(solution)/shard_map/pallas_call | solution.py:178
  169.3 3.6 %shard_map.333 = bf16[8,64,256]{2,1,0:T(8,128)(2,1)S(1)} custom-call(s32[40]{0:T(128)S(1)} %copy-done.19, bf16[8,392,512]{2,1,0:T(8,128)(2,1)S(1)} %copy-done.6, bf16[8,392,256]{2,1,0:T(8,128)(2,1)S(1)} %get-tuple-element.80.back), custom_call_target="tpu_custom_call" | custom-call | flops 822083584 | bytes 4816896 | tf_op jit(solution)/shard_map/pallas_call | solution.py:178
  179.0 4.8 %collective-permute-done.87 = bf16[8,64,256]{2,1,0:T(8,128)(2,1)S(1)} collective-permute-done((bf16[8,64,256]{2,1,0:T(8,128)(2,1)S(1)}, bf16[8,64,256]{2,1,0:T(8,128)(2,1)S(1)}, u32[]{:S(2)}, u32[]{:S(2)}) %collective-permute-start.87) | collective-permute-done | bytes 262176 | tf_op jit(solution)/shard_map/ppermute | solution.py:158
  184.0 3.5 %collective-permute-done.51 = bf16[392,512]{1,0:T(8,128)(2,1)S(1)} collective-permute-done((bf16[392,512]{1,0:T(8,128)(2,1)S(1)}, bf16[392,512]{1,0:T(8,128)(2,1)S(1)}, u32[]{:S(2)}, u32[]{:S(2)}) %collective-permute-start.51) | collective-permute-done | bytes 401440 | tf_op jit(solution)/shard_map/ppermute | solution.py:83
  192.1 6.4 %collective-permute-done.53 = bf16[392,512]{1,0:T(8,128)(2,1)S(1)} collective-permute-done((bf16[392,512]{1,0:T(8,128)(2,1)S(1)}, bf16[392,512]{1,0:T(8,128)(2,1)S(1)}, u32[]{:S(2)}, u32[]{:S(2)}) %collective-permute-start.53) | collective-permute-done | bytes 401440 | tf_op jit(solution)/shard_map/ppermute | solution.py:80
  204.2 4.8 %collective-permute-done.54.f = bf16[392,512]{1,0:T(8,128)(2,1)S(1)} collective-permute-done((bf16[392,512]{1,0:T(8,128)(2,1)S(1)}, bf16[392,512]{1,0:T(8,128)(2,1)S(1)}, u32[]{:S(2)}, u32[]{:S(2)}) %collective-permute-start.54) | collective-permute-done | bytes 401440 | tf_op jit(solution)/shard_map/ppermute | solution.py:80
  223.5 4.6 %shard_map.328 = (bf16[2,448,128]{2,1,0:T(8,128)(2,1)S(1)}, bf16[2,448,128]{2,1,0:T(8,128)(2,1)S(1)}, f32[448,512]{1,0:T(8,128)S(1)}, f32[2,512]{1,0:T(2,128)S(1)}) custom-call(s32[40]{0:T(128)S(1)} %copy-done.19, f32[448,512]{1,0:T(8,128)S(1)} %get-tuple-element.68.up, f32[2,512]{1,0:T(2,128)S(1)} %add.326.sums, f32[448,512]{1,0:T(8,128)S(1)} %copy-done.17, ...), custom_call_target="tpu_custom_call" | custom-call | flops 2113929216 | bytes 8388608 | tf_op jit(solution)/shard_map/pallas_call | solution.py:178
  237.2 3.0 %collective-permute-done.63 = f32[2,512]{1,0:T(2,128)S(1)} collective-permute-done((f32[2,512]{1,0:T(2,128)S(1)}, f32[2,512]{1,0:T(2,128)S(1)}, u32[]{:S(2)}, u32[]{:S(2)}) %collective-permute-start.63) | collective-permute-done | bytes 4128 | tf_op jit(solution)/shard_map/ppermute | solution.py:158
  244.4 4.5 %shard_map.330 = bf16[8,576,128]{2,1,0:T(8,128)(2,1)S(1)} custom-call(s32[40]{0:T(128)S(1)} %copy-done.19, bf16[4,448,512]{2,1,0:T(8,128)(2,1)S(1)} %pad_maximum_fusion.refs_0_, bf16[4,1,448,128]{3,2,1,0:T(8,128)(2,1)S(1)} %pad_maximum_fusion.2.refs_1_, bf16[392,512]{1,0:T(8,128)(2,1)S(1)} %shard_map.329.refs_2_.refs_0_), custom_call_target="tpu_custom_call" | custom-call | flops 2113929216 | bytes 8388608 | tf_op jit(solution)/shard_map/pallas_call | solution.py:178
  257.1 7.1 %collective-permute-done.65.refs_3_ = bf16[392,512]{1,0:T(8,128)(2,1)S(1)} collective-permute-done((bf16[392,512]{1,0:T(8,128)(2,1)S(1)}, bf16[392,512]{1,0:T(8,128)(2,1)S(1)}, u32[]{:S(2)}, u32[]{:S(2)}) %collective-permute-start.65) | collective-permute-done | bytes 401440 | tf_op jit(solution)/shard_map/ppermute | solution.py:80
  270.9 5.9 %shard_map.331 = (f32[8,392,256]{2,1,0:T(8,128)}, f32[256,512]{1,0:T(8,128)S(1)}) custom-call(s32[40]{0:T(128)S(1)} %copy-done.19, bf16[392,512]{1,0:T(8,128)(2,1)S(1)} %shard_map.329.refs_2_.refs_0_, bf16[392,512]{1,0:T(8,128)(2,1)S(1)} %collective-permute-done.64.refs_1_, bf16[392,512]{1,0:T(8,128)(2,1)S(1)} %collective-permute-done.67.refs_2_, ...), custom_call_target="tpu_custom_call" | custom-call | flops 1027604480 | bytes 7024640 | tf_op jit(solution)/shard_map/pallas_call | solution.py:178
  283.8 4.0 %shard_map.332 = (f32[8,392,256]{2,1,0:T(8,128)}, bf16[256,512]{1,0:T(8,128)(2,1)S(1)}) custom-call(s32[40]{0:T(128)S(1)} %copy-done.19, bf16[392,512]{1,0:T(8,128)(2,1)S(1)} %collective-permute-done.66.refs_0_, bf16[392,512]{1,0:T(8,128)(2,1)S(1)} %collective-permute-done.69.refs_1_, ...), custom_call_target="tpu_custom_call", output_to_operand_aliasing={{0}: (9, {})} | custom-call | flops 616562688 | bytes 4214784 | tf_op jit(solution)/shard_map/pallas_call | solution.py:178
  (383 shorter events, 179.8 us)
Async XLA Ops:
  2.4 21.0 %collective-permute-start.14 = (bf16[848,128]{1,0:T(8,128)(2,1)}, bf16[848,128]{1,0:T(8,128)(2,1)S(1)}, u32[]{:S(2)}, u32[]{:S(2)}) collective-permute-start(bf16[848,128]{1,0:T(8,128)(2,1)} %shard_map.318), channel_id=1, source_target_pairs={{2,0},{4,2},{6,4},{7,6},{5,7},{3,5},{1,3},{0,1},{10,8},{12,10},{14... | collective-permute-start | bytes 651272 | tf_op jit(solution)/shard_map/ppermute | solution.py:83
  5.3 19.9 %collective-permute-start.18 = (bf16[848,128]{1,0:T(8,128)(2,1)}, bf16[848,128]{1,0:T(8,128)(2,1)S(1)}, u32[]{:S(2)}, u32[]{:S(2)}) collective-permute-start(bf16[848,128]{1,0:T(8,128)(2,1)} %shard_map.318), channel_id=1, source_target_pairs={{0,2},{2,4},{4,6},{6,7},{7,5},{5,3},{3,1},{1,0},{8,10},{10,12},{12... | collective-permute-start | bytes 651272 | tf_op jit(solution)/shard_map/ppermute | solution.py:80
  23.4 12.3 %collective-permute-start.15 = (bf16[848,128]{1,0:T(8,128)(2,1)S(1)}, bf16[848,128]{1,0:T(8,128)(2,1)S(1)}, u32[]{:S(2)}, u32[]{:S(2)}) collective-permute-start(bf16[848,128]{1,0:T(8,128)(2,1)S(1)} %collective-permute-done.14), channel_id=1, source_target_pairs={{2,0},{4,2},{6,4},{7,6},{5,7},{3,5},{1,3},{0,1},{10,8},{12,10},{14... | collective-permute-start | bytes 651272 | tf_op jit(solution)/shard_map/ppermute | solution.py:83
  31.3 22.9 %collective-permute-start.5 = (bf16[392,512]{1,0:T(8,128)(2,1)S(1)}, bf16[392,512]{1,0:T(8,128)(2,1)S(1)}, u32[]{:S(2)}, u32[]{:S(2)}) collective-permute-start(bf16[392,512]{1,0:T(8,128)(2,1)S(1)} %pad_maximum_fusion.4), channel_id=1, source_target_pairs={{2,0},{4,2},{6,4},{7,6},{5,7},{3,5},{1,3},{0,1},{10,8},{12,10},{14... | collective-permute-start | bytes 1204232 | tf_op jit(solution)/shard_map/ppermute | solution.py:83
  32.9 21.8 %collective-permute-start.4 = (bf16[392,512]{1,0:T(8,128)(2,1)S(1)}, bf16[392,512]{1,0:T(8,128)(2,1)S(1)}, u32[]{:S(2)}, u32[]{:S(2)}) collective-permute-start(bf16[392,512]{1,0:T(8,128)(2,1)S(1)} %pad_maximum_fusion.3), channel_id=1, source_target_pairs={{0,2},{2,4},{4,6},{6,7},{7,5},{5,3},{3,1},{1,0},{8,10},{10,12},{12... | collective-permute-start | bytes 1204232 | tf_op jit(solution)/shard_map/ppermute | solution.py:80
  35.8 32.6 %collective-permute-start.21 = (bf16[1,5,576,128]{3,2,1,0:T(8,128)(2,1)S(1)}, bf16[1,5,576,128]{3,2,1,0:T(8,128)(2,1)S(1)}, u32[]{:S(2)}, u32[]{:S(2)}) collective-permute-start(bf16[1,5,576,128]{3,2,1,0:T(8,128)(2,1)S(1)} %bitcast.237), channel_id=1, source_target_pairs={{0,16},{8,24},{16,0},{24,8},{1,17},{9,25},{17,1},{25,9},{2,18},{10... | collective-permute-start | bytes 2211848 | tf_op jit(solution)/shard_map/ppermute | solution.py:158
  37.3 51.2 %collective-permute-start.24 = (bf16[1,5,576,128]{3,2,1,0:T(8,128)(2,1)S(1)}, bf16[1,5,576,128]{3,2,1,0:T(8,128)(2,1)}, u32[]{:S(2)}, u32[]{:S(2)}) collective-permute-start(bf16[1,5,576,128]{3,2,1,0:T(8,128)(2,1)S(1)} %bitcast.238), channel_id=1, source_target_pairs={{0,8},{8,0},{16,24},{24,16},{1,9},{9,1},{17,25},{25,17},{2,10},{10... | collective-permute-start | bytes 2211848 | tf_op jit(solution)/shard_map/ppermute | solution.py:158
  60.2 17.1 %collective-permute-start.23 = (bf16[1,3,576,128]{3,2,1,0:T(8,128)(2,1)S(1)}, bf16[1,3,576,128]{3,2,1,0:T(8,128)(2,1)S(1)}, u32[]{:S(2)}, u32[]{:S(2)}) collective-permute-start(bf16[1,3,576,128]{3,2,1,0:T(8,128)(2,1)S(1)} %maximum_bitcast_fusion.refs_2_), channel_id=1, source_target_pairs={{0,16},{8,24},{16,0},{24,8},{1,17},{9,25},{17,1},{25,9},{2,18},{10... | collective-permute-start | bytes 1327112 | tf_op jit(solution)/shard_map/ppermute | solution.py:158
  68.3 20.2 %collective-permute-start.26 = (bf16[1,3,576,128]{3,2,1,0:T(8,128)(2,1)S(1)}, bf16[1,3,576,128]{3,2,1,0:T(8,128)(2,1)}, u32[]{:S(2)}, u32[]{:S(2)}) collective-permute-start(bf16[1,3,576,128]{3,2,1,0:T(8,128)(2,1)S(1)} %maximum_bitcast_fusion.refs_2_), channel_id=1, source_target_pairs={{0,8},{8,0},{16,24},{24,16},{1,9},{9,1},{17,25},{25,17},{2,10},{10... | collective-permute-start | bytes 1327112 | tf_op jit(solution)/shard_map/ppermute | solution.py:158
  74.6 14.0 %collective-permute-start.25 = (bf16[1,5,576,128]{3,2,1,0:T(8,128)(2,1)S(1)}, bf16[1,5,576,128]{3,2,1,0:T(8,128)(2,1)}, u32[]{:S(2)}, u32[]{:S(2)}) collective-permute-start(bf16[1,5,576,128]{3,2,1,0:T(8,128)(2,1)S(1)} %collective-permute-done.21.refs_1_), channel_id=1, source_target_pairs={{0,8},{8,0},{16,24},{24,16},{1,9},{9,1},{17,25},{25,17},{2,10},{10... | collective-permute-start | bytes 2211848 | tf_op jit(solution)/shard_map/ppermute | solution.py:158
  77.3 11.3 %collective-permute-start.27 = (bf16[1,3,576,128]{3,2,1,0:T(8,128)(2,1)S(1)}, bf16[1,3,576,128]{3,2,1,0:T(8,128)(2,1)}, u32[]{:S(2)}, u32[]{:S(2)}) collective-permute-start(bf16[1,3,576,128]{3,2,1,0:T(8,128)(2,1)S(1)} %collective-permute-done.23.refs_3_), channel_id=1, source_target_pairs={{0,8},{8,0},{16,24},{24,16},{1,9},{9,1},{17,25},{25,17},{2,10},{10... | collective-permute-start | bytes 1327112 | tf_op jit(solution)/shard_map/ppermute | solution.py:158
  105.9 19.1 %collective-permute-start.33 = (bf16[392,512]{1,0:T(8,128)(2,1)S(1)}, bf16[392,512]{1,0:T(8,128)(2,1)S(1)}, u32[]{:S(2)}, u32[]{:S(2)}) collective-permute-start(bf16[392,512]{1,0:T(8,128)(2,1)S(1)} %broadcast_select_fusion.1), channel_id=1, source_target_pairs={{0,2},{2,4},{4,6},{6,7},{7,5},{5,3},{3,1},{1,0},{8,10},{10,12},{12... | collective-permute-start | bytes 1204232 | tf_op jit(solution)/shard_map/ppermute | solution.py:80
  108.4 18.7 %collective-permute-start.36 = (bf16[392,512]{1,0:T(8,128)(2,1)}, bf16[392,512]{1,0:T(8,128)(2,1)S(1)}, u32[]{:S(2)}, u32[]{:S(2)}) collective-permute-start(bf16[392,512]{1,0:T(8,128)(2,1)} %broadcast_select_fusion), channel_id=1, source_target_pairs={{2,0},{4,2},{6,4},{7,6},{5,7},{3,5},{1,3},{0,1},{10,8},{12,10},{14... | collective-permute-start | bytes 1204232 | tf_op jit(solution)/shard_map/ppermute | solution.py:83
  159.7 18.8 %collective-permute-start.72 = (bf16[1,448,512]{2,1,0:T(8,128)(2,1)}, bf16[1,448,512]{2,1,0:T(8,128)(2,1)S(1)}, u32[]{:S(2)}, u32[]{:S(2)}) collective-permute-start(bf16[1,448,512]{2,1,0:T(8,128)(2,1)} %bitcast.233), channel_id=1, source_target_pairs={{0,8},{8,0},{16,24},{24,16},{1,9},{9,1},{17,25},{25,17},{2,10},{10... | collective-permute-start | bytes 1376264 | tf_op jit(solution)/shard_map/ppermute | solution.py:158
  176.3 11.1 %collective-permute-start.51 = (bf16[392,512]{1,0:T(8,128)(2,1)S(1)}, bf16[392,512]{1,0:T(8,128)(2,1)S(1)}, u32[]{:S(2)}, u32[]{:S(2)}) collective-permute-start(bf16[392,512]{1,0:T(8,128)(2,1)S(1)} %pad_maximum_fusion.6), channel_id=1, source_target_pairs={{2,0},{4,2},{6,4},{7,6},{5,7},{3,5},{1,3},{0,1},{10,8},{12,10},{14... | collective-permute-start | bytes 1204232 | tf_op jit(solution)/shard_map/ppermute | solution.py:83
  178.6 32.8 %collective-permute-start.73 = (bf16[2,448,512]{2,1,0:T(8,128)(2,1)S(1)}, bf16[2,448,512]{2,1,0:T(8,128)(2,1)S(1)}, u32[]{:S(2)}, u32[]{:S(2)}) collective-permute-start(bf16[2,448,512]{2,1,0:T(8,128)(2,1)S(1)} %pad_maximum_fusion.1), channel_id=1, source_target_pairs={{0,16},{8,24},{16,0},{24,8},{1,17},{9,25},{17,1},{25,9},{2,18},{10... | collective-permute-start | bytes 2752520 | tf_op jit(solution)/shard_map/ppermute | solution.py:158
  190.0 12.1 %collective-permute-start.88 = (bf16[64,256]{1,0:T(8,128)(2,1)S(1)}, bf16[64,256]{1,0:T(8,128)(2,1)S(1)}, u32[]{:S(2)}, u32[]{:S(2)}) collective-permute-start(bf16[64,256]{1,0:T(8,128)(2,1)S(1)} %get-tuple-element.130), channel_id=1, source_target_pairs={{2,0},{4,2},{6,4},{7,6},{5,7},{3,5},{1,3},{0,1},{10,8},{12,10},{14... | collective-permute-start | bytes 98312 | tf_op jit(solution)/shard_map/ppermute | solution.py:83
  190.2 11.9 %collective-permute-start.89 = (bf16[64,256]{1,0:T(8,128)(2,1)S(1)}, bf16[64,256]{1,0:T(8,128)(2,1)S(1)}, u32[]{:S(2)}, u32[]{:S(2)}) collective-permute-start(bf16[64,256]{1,0:T(8,128)(2,1)S(1)} %get-tuple-element.131), channel_id=1, source_target_pairs={{0,2},{2,4},{4,6},{6,7},{7,5},{5,3},{3,1},{1,0},{8,10},{10,12},{12... | collective-permute-start | bytes 98312 | tf_op jit(solution)/shard_map/ppermute | solution.py:80
  242.0 11.3 %collective-permute-start.67 = (bf16[392,512]{1,0:T(8,128)(2,1)S(1)}, bf16[392,512]{1,0:T(8,128)(2,1)S(1)}, u32[]{:S(2)}, u32[]{:S(2)}) collective-permute-start(bf16[392,512]{1,0:T(8,128)(2,1)S(1)} %shard_map.329.refs_2_.refs_0_), channel_id=1, source_target_pairs={{2,0},{4,2},{6,4},{7,6},{5,7},{3,5},{1,3},{0,1},{10,8},{12,10},{14... | collective-permute-start | bytes 1204232 | tf_op jit(solution)/shard_map/ppermute | solution.py:83
  251.9 12.3 %collective-permute-start.65 = (bf16[392,512]{1,0:T(8,128)(2,1)S(1)}, bf16[392,512]{1,0:T(8,128)(2,1)S(1)}, u32[]{:S(2)}, u32[]{:S(2)}) collective-permute-start(bf16[392,512]{1,0:T(8,128)(2,1)S(1)} %collective-permute-done.64.refs_1_), channel_id=1, source_target_pairs={{0,2},{2,4},{4,6},{6,7},{7,5},{5,3},{3,1},{1,0},{8,10},{10,12},{12... | collective-permute-start | bytes 1204232 | tf_op jit(solution)/shard_map/ppermute | solution.py:80
  253.3 11.6 %collective-permute-start.68 = (bf16[392,512]{1,0:T(8,128)(2,1)S(1)}, bf16[392,512]{1,0:T(8,128)(2,1)S(1)}, u32[]{:S(2)}, u32[]{:S(2)}) collective-permute-start(bf16[392,512]{1,0:T(8,128)(2,1)S(1)} %collective-permute-done.67.refs_2_), channel_id=1, source_target_pairs={{2,0},{4,2},{6,4},{7,6},{5,7},{3,5},{1,3},{0,1},{10,8},{12,10},{14... | collective-permute-start | bytes 1204232 | tf_op jit(solution)/shard_map/ppermute | solution.py:83
  254.9 12.4 %collective-permute-start.78 = (bf16[576,128]{1,0:T(8,128)(2,1)S(1)}, bf16[576,128]{1,0:T(8,128)(2,1)S(1)}, u32[]{:S(2)}, u32[]{:S(2)}) collective-permute-start(bf16[576,128]{1,0:T(8,128)(2,1)S(1)} %pad_maximum_fusion.9), channel_id=1, source_target_pairs={{0,2},{2,4},{4,6},{6,7},{7,5},{5,3},{3,1},{1,0},{8,10},{10,12},{12... | collective-permute-start | bytes 442376 | tf_op jit(solution)/shard_map/ppermute | solution.py:80
  264.2 12.6 %collective-permute-start.66 = (bf16[392,512]{1,0:T(8,128)(2,1)S(1)}, bf16[392,512]{1,0:T(8,128)(2,1)S(1)}, u32[]{:S(2)}, u32[]{:S(2)}) collective-permute-start(bf16[392,512]{1,0:T(8,128)(2,1)S(1)} %collective-permute-done.65.refs_3_), channel_id=1, source_target_pairs={{0,2},{2,4},{4,6},{6,7},{7,5},{5,3},{3,1},{1,0},{8,10},{10,12},{12... | collective-permute-start | bytes 1204232 | tf_op jit(solution)/shard_map/ppermute | solution.py:80
  264.8 13.2 %collective-permute-start.69 = (bf16[392,512]{1,0:T(8,128)(2,1)S(1)}, bf16[392,512]{1,0:T(8,128)(2,1)S(1)}, u32[]{:S(2)}, u32[]{:S(2)}) collective-permute-start(bf16[392,512]{1,0:T(8,128)(2,1)S(1)} %collective-permute-done.68.refs_4_), channel_id=1, source_target_pairs={{2,0},{4,2},{6,4},{7,6},{5,7},{3,5},{1,3},{0,1},{10,8},{12,10},{14... | collective-permute-start | bytes 1204232 | tf_op jit(solution)/shard_map/ppermute | solution.py:83
  (112 other events, 855.1 us)

commit v4 on v3

--- a/solution.py
+++ b/solution.py
@@ -237,7 +237,7 @@
         native[q] = value[:, q * 128 : (q + 1) * 128]
 
 
-def meta_body(sz, dp, ratio, counts, table, out):
+def meta_body(sz, dp, ratio, counts, table, _, out):
     d, c = lax.axis_index("dp"), lax.axis_index("chan")
     per_batch = sz.chunks // sz.micro
     for k in range(sz.chunks):
@@ -259,14 +259,14 @@
     out[sz.planes + dp + 1] = lax.rem(c, ratio)
 
 
-def make_meta(sz, ring, dp, ratio, counts):
+def make_meta(sz, ring, dp, ratio, counts, other):
     smem = pl.BlockSpec(memory_space=pltpu.SMEM)
     return pl.pallas_call(
         functools.partial(meta_body, sz, dp, ratio),
-        in_specs=[smem, smem],
+        in_specs=[smem, smem, pl.BlockSpec(memory_space=pl.ANY)],
         out_specs=smem,
         out_shape=jax.ShapeDtypeStruct((sz.planes + dp + 2,), jnp.int32),
-    )(counts, jnp.asarray(ring.table))
+    )(counts, jnp.asarray(ring.table), other)
 
 
 def to_padded(sz, native, padded):
@@ -649,7 +649,7 @@
             fill(p if p < half else half + p)
 
 
-def prepare_body(weights, last, params, out):
+def prepare_body(weights, last, params, _, out):
     many, lanes = weights.shape
     out[:many, :] = weights[...].astype(BF16)
     depth = last.shape[0]
@@ -741,14 +741,14 @@
     own_blocks = deep // lanes
     ratio = last_blocks // own_blocks
 
-    meta = make_meta(sz, ring, dp, ratio, image_counts)
-    at = meta[:chan]
 
     dp_bits = bits_below(dp)
     wide_bits = dp_bits[1:]
     first = w_first.astype(BF16)
+    first_stages = []
     for bit in dp_bits:
         other = swap(first, "dp", bit, dp)
+        first_stages.append(other)
         first = jnp.where(
             (d & bit) == 0,
             jnp.concatenate([first, other], axis=1),
@@ -758,10 +758,13 @@
     tail_at = many + last_blocks * depth
     (payload,) = pl.pallas_call(
         prepare_body,
-        in_specs=[pl.BlockSpec(memory_space=pltpu.VMEM)] * 3,
+        in_specs=[pl.BlockSpec(memory_space=pltpu.VMEM)] * 3
+        + [pl.BlockSpec(memory_space=pl.ANY)],
         out_specs=[pl.BlockSpec(memory_space=pltpu.VMEM)],
         out_shape=[jax.ShapeDtypeStruct((tail_at + 16, lanes), BF16)],
-    )(w_middle.reshape(many, lanes), w_last, mid_params)
+    )(w_middle.reshape(many, lanes), w_last, mid_params, first_stages[0])
+    meta = make_meta(sz, ring, dp, ratio, image_counts, payload)
+    at = meta[:chan]
     mids = Gather(ring, payload, 0)
     while mids.count < chan // 2:
         mids.step()
@@ -916,11 +919,12 @@
     )
     gather = Gather(ring, raw, 1)
     gather.step()
+    stat_two = sum_over(stat_two, "chan", stat_bits[:1], chan)
+    gather.step(stat_two)
     stat_two = sum_over(stat_two, "dp", dp_bits, dp)
-    gather.step(stat_two)
-    stat_two = sum_over(stat_two, "chan", stat_bits, chan)
     if gather.count < opposite - 1:
         gather.step(stat_two)
+    stat_two = sum_over(stat_two, "chan", stat_bits[1:], chan)
     stats_two = all_batches(stat_two)
     while gather.count < opposite - 1:
         gather.step()

time: 296 us -> 291 us (0.983)
  starting transfers between devices: 96.4 us -> 92 us
  waiting for transfers between devices: 113 us -> 110 us
    ppermute x28, starting transfers between devices: 30.2 us -> 25.7 us  [fw(): return lax.ppermute(x, 'chan', self.ahead)]
    ppermute x28, waiting for transfers between devices: 22.1 us -> 18 us  [bw(): return lax.ppermute(x, 'chan', self.back)]
    ppermute x28, starting transfers between devices: 31.2 us -> 34.7 us  [bw(): return lax.ppermute(x, 'chan', self.back)]
    ppermute x28, waiting for transfers between devices: 42.9 us -> 45.8 us  [fw(): return lax.ppermute(x, 'chan', self.ahead)]
    unnamed x87 -> x89, local copies, waits for them, and re-layouts: 9.69 us -> 10.7 us
  transfers between devices with their start and end apart: 98 -> 98, of which waited for: 51 -> 51; matrix products, arithmetic and copies ran while one was open for 6% -> 7% of each run, Pallas kernels for 13% -> 13%
where the time goes in v4:
time: 291 us; the launch traced here: 290 us
  waiting for transfers between devices  110 us (38%)
  starting transfers between devices  92 us (32%)
  Pallas kernels  55.8 us (19%)
  local copies, waits for them, and re-layouts  14.8 us (5%)
  other arithmetic  13.9 us (5%)
  between operations  3.76 us (1%)
    pallas_call x18, Pallas kernels, run(): pl.pallas_call(kernel if extra else body, grid_spec=pltpu.PrefetchScalarG...  52.7 us
    ppermute x39, waiting for transfers between devices, swap(): return lax.ppermute(x, axis, [(i, i ^ bit) for i in range(size)])  46.4 us
    ppermute x28, waiting for transfers between devices, fw(): return lax.ppermute(x, 'chan', self.ahead)  45.8 us
    ppermute x28, starting transfers between devices, bw(): return lax.ppermute(x, 'chan', self.back)  34.7 us
    ppermute x39, starting transfers between devices, swap(): return lax.ppermute(x, axis, [(i, i ^ bit) for i in range(size)])  27.3 us
    ppermute x28, starting transfers between devices, fw(): return lax.ppermute(x, 'chan', self.ahead)  25.7 us
    ppermute x28, waiting for transfers between devices, bw(): return lax.ppermute(x, 'chan', self.back)  18 us
    unnamed x89, local copies, waits for them, and re-layouts  10.7 us
  transfers between devices with their start and end apart: 98, of which 51 were waited for; matrix products, arithmetic and copies ran while one was open for 7% of the time, Pallas kernels for 13%

profile of v4, /device:TPU:0, one launch (start us, length us, event | category | flops | bytes accessed | tf_op | source)
XLA Modules:
  0.0 290.4 jit_solution(16395338011119284100)
XLA Ops:
  38.0 6.6 %collective-permute-done.16 = bf16[848,128]{1,0:T(8,128)(2,1)S(1)} collective-permute-done((bf16[848,128]{1,0:T(8,128)(2,1)S(1)}, bf16[848,128]{1,0:T(8,128)(2,1)S(1)}, u32[]{:S(2)}, u32[]{:S(2)}) %collective-permute-start.16) | collective-permute-done | bytes 217120 | tf_op jit(solution)/shard_map/ppermute | solution.py:83
  46.1 5.6 %collective-permute-done.20 = bf16[848,128]{1,0:T(8,128)(2,1)S(1)} collective-permute-done((bf16[848,128]{1,0:T(8,128)(2,1)S(1)}, bf16[848,128]{1,0:T(8,128)(2,1)S(1)}, u32[]{:S(2)}, u32[]{:S(2)}) %collective-permute-start.20) | collective-permute-done | bytes 217120 | tf_op jit(solution)/shard_map/ppermute | solution.py:80
  59.9 5.5 %collective-permute-done.7 = bf16[392,512]{1,0:T(8,128)(2,1)S(1)} collective-permute-done((bf16[392,512]{1,0:T(8,128)(2,1)S(1)}, bf16[392,512]{1,0:T(8,128)(2,1)S(1)}, u32[]{:S(2)}, u32[]{:S(2)}) %collective-permute-start.7) | collective-permute-done | bytes 401440 | tf_op jit(solution)/shard_map/ppermute | solution.py:80
  68.0 6.7 %collective-permute-done.8.f = bf16[392,512]{1,0:T(8,128)(2,1)S(1)} collective-permute-done((bf16[392,512]{1,0:T(8,128)(2,1)S(1)}, bf16[392,512]{1,0:T(8,128)(2,1)S(1)}, u32[]{:S(2)}, u32[]{:S(2)}) %collective-permute-start.8) | collective-permute-done | bytes 401440 | tf_op jit(solution)/shard_map/ppermute | solution.py:80
  88.5 3.4 %shard_map.319 = bf16[9,512,512]{2,1,0:T(8,128)(2,1)S(1)} custom-call(s32[40]{0:T(128)S(1)} %copy-done.19, bf16[1,5,576,128]{3,2,1,0:T(8,128)(2,1)S(1)} %bitcast.239, bf16[1,5,576,128]{3,2,1,0:T(8,128)(2,1)S(1)} %collective-permute-done.21.refs_1_, bf16[1,3,576,128]{3,2,1,0:T(8,128)(2,1)S(1)} %maximum_bitcast_fusion.refs_2_, ...), custom_call_target="tpu_custom_call" | custom-call | tf_op jit(solution)/shard_map/pallas_call | solution.py:178
  92.0 4.0 %shard_map.320 = (f32[448,512]{1,0:T(8,128)S(1)}, bf16[392,512]{1,0:T(8,128)(2,1)S(1)}, f32[2,512]{1,0:T(2,128)S(1)}, bf16[448,512]{1,0:T(8,128)(2,1)S(1)}) custom-call(s32[40]{0:T(128)S(1)} %copy-done.19, f32[448,512]{1,0:T(8,128)S(1)} %get-tuple-element.51.pre.pre_one, f32[2,512]{1,0:T(2,128)S(1)} %add.300.stat.stat_one, ...), custom_call_target="tpu_custom_call" | custom-call | flops 2113929216 | bytes 8388608 | tf_op jit(solution)/shard_map/pallas_call | solution.py:178
  101.0 4.9 %collective-permute-done.28 = f32[2,512]{1,0:T(2,128)S(1)} collective-permute-done((f32[2,512]{1,0:T(2,128)S(1)}, f32[2,512]{1,0:T(2,128)S(1)}, u32[]{:S(2)}, u32[]{:S(2)}) %collective-permute-start.28) | collective-permute-done | bytes 4128 | tf_op jit(solution)/shard_map/ppermute | solution.py:158
  111.7 3.1 %collective-permute-done.30 = f32[2,512]{1,0:T(2,128)S(1)} collective-permute-done((f32[2,512]{1,0:T(2,128)S(1)}, f32[2,512]{1,0:T(2,128)S(1)}, u32[]{:S(2)}, u32[]{:S(2)}) %collective-permute-start.30) | collective-permute-done | bytes 4128 | tf_op jit(solution)/shard_map/ppermute | solution.py:158
  118.4 3.1 %collective-permute-start.38 = (f32[2,512]{1,0:T(2,128)S(1)}, f32[2,512]{1,0:T(2,128)S(1)}, u32[]{:S(2)}, u32[]{:S(2)}) collective-permute-start(f32[2,512]{1,0:T(2,128)S(1)} %add.306.stat.stat_two), channel_id=1, source_target_pairs={{0,4},{1,5},{2,6},{3,7},{4,0},{5,1},{6,2},{7,3},{8,12},{9,13},{10,... | collective-permute-start | bytes 12296 | tf_op jit(solution)/shard_map/ppermute | solution.py:158
  134.8 3.6 %shard_map.322 = (bf16[8,392,512]{2,1,0:T(8,128)(2,1)S(1)}, f32[8,392,256]{2,1,0:T(8,128)S(1)}, f32[4,256]{1,0:T(4,128)S(1)}) custom-call(s32[40]{0:T(128)S(1)} %copy-done.19, bf16[392,512]{1,0:T(8,128)(2,1)S(1)} %get-tuple-element.54.refs_0_, bf16[392,512]{1,0:T(8,128)(2,1)S(1)} %collective-permute-done.31.refs_1_, ...), custom_call_target="tpu_custom_call" | custom-call | flops 513802240 | bytes 6021120 | tf_op jit(solution)/shard_map/pallas_call | solution.py:178
  144.0 3.2 %collective-permute-done.45 = f32[4,256]{1,0:T(4,128)S(1)} collective-permute-done((f32[4,256]{1,0:T(4,128)S(1)}, f32[4,256]{1,0:T(4,128)S(1)}, u32[]{:S(2)}, u32[]{:S(2)}) %collective-permute-start.45) | collective-permute-done | bytes 4128 | tf_op jit(solution)/shard_map/ppermute | solution.py:158
  147.3 5.2 %shard_map.324 = (f32[8,392,256]{2,1,0:T(8,128)}, f32[8,392,256]{2,1,0:T(8,128)S(1)}, f32[4,256]{1,0:T(4,128)S(1)}) custom-call(s32[40]{0:T(128)S(1)} %copy-done.19, f32[8,392,256]{2,1,0:T(8,128)S(1)} %get-tuple-element.57.pre.refs_0_, f32[4,256]{1,0:T(4,128)S(1)} %add.314.stat.refs_1_, f32[2,256]{1,0:T(2,128)S(1)} %copy-done.20, ...), custom_call_target="tpu_custom_call" | custom-call | flops 16056320 | bytes 12845056 | tf_op jit(solution)/shard_map/pallas_call | solution.py:178
  154.0 3.2 %collective-permute-done.47 = f32[4,256]{1,0:T(4,128)S(1)} collective-permute-done((f32[4,256]{1,0:T(4,128)S(1)}, f32[4,256]{1,0:T(4,128)S(1)}, u32[]{:S(2)}, u32[]{:S(2)}) %collective-permute-start.47) | collective-permute-done | bytes 4128 | tf_op jit(solution)/shard_map/ppermute | solution.py:158
  164.9 3.6 %shard_map.333 = bf16[8,64,256]{2,1,0:T(8,128)(2,1)S(1)} custom-call(s32[40]{0:T(128)S(1)} %copy-done.19, bf16[8,392,512]{2,1,0:T(8,128)(2,1)S(1)} %copy-done.6, bf16[8,392,256]{2,1,0:T(8,128)(2,1)S(1)} %get-tuple-element.80.back), custom_call_target="tpu_custom_call" | custom-call | flops 822083584 | bytes 4816896 | tf_op jit(solution)/shard_map/pallas_call | solution.py:178
  174.6 4.8 %collective-permute-done.87 = bf16[8,64,256]{2,1,0:T(8,128)(2,1)S(1)} collective-permute-done((bf16[8,64,256]{2,1,0:T(8,128)(2,1)S(1)}, bf16[8,64,256]{2,1,0:T(8,128)(2,1)S(1)}, u32[]{:S(2)}, u32[]{:S(2)}) %collective-permute-start.87) | collective-permute-done | bytes 262176 | tf_op jit(solution)/shard_map/ppermute | solution.py:158
  187.4 6.1 %collective-permute-done.53 = bf16[392,512]{1,0:T(8,128)(2,1)S(1)} collective-permute-done((bf16[392,512]{1,0:T(8,128)(2,1)S(1)}, bf16[392,512]{1,0:T(8,128)(2,1)S(1)}, u32[]{:S(2)}, u32[]{:S(2)}) %collective-permute-start.53) | collective-permute-done | bytes 401440 | tf_op jit(solution)/shard_map/ppermute | solution.py:80
  198.5 4.8 %collective-permute-done.54.f = bf16[392,512]{1,0:T(8,128)(2,1)S(1)} collective-permute-done((bf16[392,512]{1,0:T(8,128)(2,1)S(1)}, bf16[392,512]{1,0:T(8,128)(2,1)S(1)}, u32[]{:S(2)}, u32[]{:S(2)}) %collective-permute-start.54) | collective-permute-done | bytes 401440 | tf_op jit(solution)/shard_map/ppermute | solution.py:80
  218.0 4.6 %shard_map.328 = (bf16[2,448,128]{2,1,0:T(8,128)(2,1)S(1)}, bf16[2,448,128]{2,1,0:T(8,128)(2,1)S(1)}, f32[448,512]{1,0:T(8,128)S(1)}, f32[2,512]{1,0:T(2,128)S(1)}) custom-call(s32[40]{0:T(128)S(1)} %copy-done.19, f32[448,512]{1,0:T(8,128)S(1)} %get-tuple-element.68.up, f32[2,512]{1,0:T(2,128)S(1)} %add.326.sums, f32[448,512]{1,0:T(8,128)S(1)} %copy-done.17, ...), custom_call_target="tpu_custom_call" | custom-call | flops 2113929216 | bytes 8388608 | tf_op jit(solution)/shard_map/pallas_call | solution.py:178
  231.8 3.0 %collective-permute-done.63 = f32[2,512]{1,0:T(2,128)S(1)} collective-permute-done((f32[2,512]{1,0:T(2,128)S(1)}, f32[2,512]{1,0:T(2,128)S(1)}, u32[]{:S(2)}, u32[]{:S(2)}) %collective-permute-start.63) | collective-permute-done | bytes 4128 | tf_op jit(solution)/shard_map/ppermute | solution.py:158
  239.4 4.5 %shard_map.330 = bf16[8,576,128]{2,1,0:T(8,128)(2,1)S(1)} custom-call(s32[40]{0:T(128)S(1)} %copy-done.19, bf16[4,448,512]{2,1,0:T(8,128)(2,1)S(1)} %pad_maximum_fusion.refs_0_, bf16[4,1,448,128]{3,2,1,0:T(8,128)(2,1)S(1)} %pad_maximum_fusion.2.refs_1_, bf16[392,512]{1,0:T(8,128)(2,1)S(1)} %shard_map.329.refs_2_.refs_0_), custom_call_target="tpu_custom_call" | custom-call | flops 2113929216 | bytes 8388608 | tf_op jit(solution)/shard_map/pallas_call | solution.py:178
  252.3 6.1 %collective-permute-done.65.refs_3_ = bf16[392,512]{1,0:T(8,128)(2,1)S(1)} collective-permute-done((bf16[392,512]{1,0:T(8,128)(2,1)S(1)}, bf16[392,512]{1,0:T(8,128)(2,1)S(1)}, u32[]{:S(2)}, u32[]{:S(2)}) %collective-permute-start.65) | collective-permute-done | bytes 401440 | tf_op jit(solution)/shard_map/ppermute | solution.py:80
  266.4 5.9 %shard_map.331 = (f32[8,392,256]{2,1,0:T(8,128)}, f32[256,512]{1,0:T(8,128)S(1)}) custom-call(s32[40]{0:T(128)S(1)} %copy-done.19, bf16[392,512]{1,0:T(8,128)(2,1)S(1)} %shard_map.329.refs_2_.refs_0_, bf16[392,512]{1,0:T(8,128)(2,1)S(1)} %collective-permute-done.64.refs_1_, bf16[392,512]{1,0:T(8,128)(2,1)S(1)} %collective-permute-done.67.refs_2_, ...), custom_call_target="tpu_custom_call" | custom-call | flops 1027604480 | bytes 7024640 | tf_op jit(solution)/shard_map/pallas_call | solution.py:178
  279.1 4.0 %shard_map.332 = (f32[8,392,256]{2,1,0:T(8,128)}, bf16[256,512]{1,0:T(8,128)(2,1)S(1)}) custom-call(s32[40]{0:T(128)S(1)} %copy-done.19, bf16[392,512]{1,0:T(8,128)(2,1)S(1)} %collective-permute-done.66.refs_0_, bf16[392,512]{1,0:T(8,128)(2,1)S(1)} %collective-permute-done.69.refs_1_, ...), custom_call_target="tpu_custom_call", output_to_operand_aliasing={{0}: (9, {})} | custom-call | flops 616562688 | bytes 4214784 | tf_op jit(solution)/shard_map/pallas_call | solution.py:178
  286.7 2.9 collective-permute-done.82
  (385 shorter events, 178.3 us)
Async XLA Ops:
  6.3 16.5 %collective-permute-start.14 = (bf16[848,128]{1,0:T(8,128)(2,1)}, bf16[848,128]{1,0:T(8,128)(2,1)}, u32[]{:S(2)}, u32[]{:S(2)}) collective-permute-start(bf16[848,128]{1,0:T(8,128)(2,1)} %shard_map.314._), channel_id=1, source_target_pairs={{2,0},{4,2},{6,4},{7,6},{5,7},{3,5},{1,3},{0,1},{10,8},{12,10},{14... | collective-permute-start | bytes 651272 | tf_op jit(solution)/shard_map/ppermute | solution.py:83
  9.2 15.3 %collective-permute-start.18 = (bf16[848,128]{1,0:T(8,128)(2,1)}, bf16[848,128]{1,0:T(8,128)(2,1)S(1)}, u32[]{:S(2)}, u32[]{:S(2)}) collective-permute-start(bf16[848,128]{1,0:T(8,128)(2,1)} %shard_map.314._), channel_id=1, source_target_pairs={{0,2},{2,4},{4,6},{6,7},{7,5},{5,3},{3,1},{1,0},{8,10},{10,12},{12... | collective-permute-start | bytes 651272 | tf_op jit(solution)/shard_map/ppermute | solution.py:80
  22.8 11.9 %collective-permute-start.15 = (bf16[848,128]{1,0:T(8,128)(2,1)}, bf16[848,128]{1,0:T(8,128)(2,1)S(1)}, u32[]{:S(2)}, u32[]{:S(2)}) collective-permute-start(bf16[848,128]{1,0:T(8,128)(2,1)} %collective-permute-done.14), channel_id=1, source_target_pairs={{2,0},{4,2},{6,4},{7,6},{5,7},{3,5},{1,3},{0,1},{10,8},{12,10},{14... | collective-permute-start | bytes 651272 | tf_op jit(solution)/shard_map/ppermute | solution.py:83
  30.3 22.7 %collective-permute-start.5 = (bf16[392,512]{1,0:T(8,128)(2,1)S(1)}, bf16[392,512]{1,0:T(8,128)(2,1)S(1)}, u32[]{:S(2)}, u32[]{:S(2)}) collective-permute-start(bf16[392,512]{1,0:T(8,128)(2,1)S(1)} %pad_maximum_fusion.4), channel_id=1, source_target_pairs={{2,0},{4,2},{6,4},{7,6},{5,7},{3,5},{1,3},{0,1},{10,8},{12,10},{14... | collective-permute-start | bytes 1204232 | tf_op jit(solution)/shard_map/ppermute | solution.py:83
  32.0 21.8 %collective-permute-start.4 = (bf16[392,512]{1,0:T(8,128)(2,1)S(1)}, bf16[392,512]{1,0:T(8,128)(2,1)S(1)}, u32[]{:S(2)}, u32[]{:S(2)}) collective-permute-start(bf16[392,512]{1,0:T(8,128)(2,1)S(1)} %pad_maximum_fusion.3), channel_id=1, source_target_pairs={{0,2},{2,4},{4,6},{6,7},{7,5},{5,3},{3,1},{1,0},{8,10},{10,12},{12... | collective-permute-start | bytes 1204232 | tf_op jit(solution)/shard_map/ppermute | solution.py:80
  34.8 33.1 %collective-permute-start.21 = (bf16[1,5,576,128]{3,2,1,0:T(8,128)(2,1)S(1)}, bf16[1,5,576,128]{3,2,1,0:T(8,128)(2,1)S(1)}, u32[]{:S(2)}, u32[]{:S(2)}) collective-permute-start(bf16[1,5,576,128]{3,2,1,0:T(8,128)(2,1)S(1)} %bitcast.237), channel_id=1, source_target_pairs={{0,16},{8,24},{16,0},{24,8},{1,17},{9,25},{17,1},{25,9},{2,18},{10... | collective-permute-start | bytes 2211848 | tf_op jit(solution)/shard_map/ppermute | solution.py:158
  36.5 52.0 %collective-permute-start.24 = (bf16[1,5,576,128]{3,2,1,0:T(8,128)(2,1)S(1)}, bf16[1,5,576,128]{3,2,1,0:T(8,128)(2,1)}, u32[]{:S(2)}, u32[]{:S(2)}) collective-permute-start(bf16[1,5,576,128]{3,2,1,0:T(8,128)(2,1)S(1)} %bitcast.238), channel_id=1, source_target_pairs={{0,8},{8,0},{16,24},{24,16},{1,9},{9,1},{17,25},{25,17},{2,10},{10... | collective-permute-start | bytes 2211848 | tf_op jit(solution)/shard_map/ppermute | solution.py:158
  54.2 11.1 %collective-permute-start.7 = (bf16[392,512]{1,0:T(8,128)(2,1)S(1)}, bf16[392,512]{1,0:T(8,128)(2,1)S(1)}, u32[]{:S(2)}, u32[]{:S(2)}) collective-permute-start(bf16[392,512]{1,0:T(8,128)(2,1)S(1)} %get-tuple-element.108), channel_id=1, source_target_pairs={{0,2},{2,4},{4,6},{6,7},{7,5},{5,3},{3,1},{1,0},{8,10},{10,12},{12... | collective-permute-start | bytes 1204232 | tf_op jit(solution)/shard_map/ppermute | solution.py:80
  59.1 18.0 %collective-permute-start.23 = (bf16[1,3,576,128]{3,2,1,0:T(8,128)(2,1)S(1)}, bf16[1,3,576,128]{3,2,1,0:T(8,128)(2,1)S(1)}, u32[]{:S(2)}, u32[]{:S(2)}) collective-permute-start(bf16[1,3,576,128]{3,2,1,0:T(8,128)(2,1)S(1)} %maximum_bitcast_fusion.refs_2_), channel_id=1, source_target_pairs={{0,16},{8,24},{16,0},{24,8},{1,17},{9,25},{17,1},{25,9},{2,18},{10... | collective-permute-start | bytes 1327112 | tf_op jit(solution)/shard_map/ppermute | solution.py:158
  67.9 20.5 %collective-permute-start.26 = (bf16[1,3,576,128]{3,2,1,0:T(8,128)(2,1)S(1)}, bf16[1,3,576,128]{3,2,1,0:T(8,128)(2,1)}, u32[]{:S(2)}, u32[]{:S(2)}) collective-permute-start(bf16[1,3,576,128]{3,2,1,0:T(8,128)(2,1)S(1)} %maximum_bitcast_fusion.refs_2_), channel_id=1, source_target_pairs={{0,8},{8,0},{16,24},{24,16},{1,9},{9,1},{17,25},{25,17},{2,10},{10... | collective-permute-start | bytes 1327112 | tf_op jit(solution)/shard_map/ppermute | solution.py:158
  74.7 13.8 %collective-permute-start.25 = (bf16[1,5,576,128]{3,2,1,0:T(8,128)(2,1)S(1)}, bf16[1,5,576,128]{3,2,1,0:T(8,128)(2,1)}, u32[]{:S(2)}, u32[]{:S(2)}) collective-permute-start(bf16[1,5,576,128]{3,2,1,0:T(8,128)(2,1)S(1)} %collective-permute-done.21.refs_1_), channel_id=1, source_target_pairs={{0,8},{8,0},{16,24},{24,16},{1,9},{9,1},{17,25},{25,17},{2,10},{10... | collective-permute-start | bytes 2211848 | tf_op jit(solution)/shard_map/ppermute | solution.py:158
  77.2 11.3 %collective-permute-start.27 = (bf16[1,3,576,128]{3,2,1,0:T(8,128)(2,1)S(1)}, bf16[1,3,576,128]{3,2,1,0:T(8,128)(2,1)}, u32[]{:S(2)}, u32[]{:S(2)}) collective-permute-start(bf16[1,3,576,128]{3,2,1,0:T(8,128)(2,1)S(1)} %collective-permute-done.23.refs_3_), channel_id=1, source_target_pairs={{0,8},{8,0},{16,24},{24,16},{1,9},{9,1},{17,25},{25,17},{2,10},{10... | collective-permute-start | bytes 1327112 | tf_op jit(solution)/shard_map/ppermute | solution.py:158
  107.2 14.4 %collective-permute-start.32 = (bf16[392,512]{1,0:T(8,128)(2,1)S(1)}, bf16[392,512]{1,0:T(8,128)(2,1)S(1)}, u32[]{:S(2)}, u32[]{:S(2)}) collective-permute-start(bf16[392,512]{1,0:T(8,128)(2,1)S(1)} %broadcast_select_fusion.1), channel_id=1, source_target_pairs={{0,2},{2,4},{4,6},{6,7},{7,5},{5,3},{3,1},{1,0},{8,10},{10,12},{12... | collective-permute-start | bytes 1204232 | tf_op jit(solution)/shard_map/ppermute | solution.py:80
  108.7 14.2 %collective-permute-start.35 = (bf16[392,512]{1,0:T(8,128)(2,1)}, bf16[392,512]{1,0:T(8,128)(2,1)S(1)}, u32[]{:S(2)}, u32[]{:S(2)}) collective-permute-start(bf16[392,512]{1,0:T(8,128)(2,1)} %broadcast_select_fusion), channel_id=1, source_target_pairs={{2,0},{4,2},{6,4},{7,6},{5,7},{3,5},{1,3},{0,1},{10,8},{12,10},{14... | collective-permute-start | bytes 1204232 | tf_op jit(solution)/shard_map/ppermute | solution.py:83
  154.0 18.8 %collective-permute-start.72 = (bf16[1,448,512]{2,1,0:T(8,128)(2,1)}, bf16[1,448,512]{2,1,0:T(8,128)(2,1)S(1)}, u32[]{:S(2)}, u32[]{:S(2)}) collective-permute-start(bf16[1,448,512]{2,1,0:T(8,128)(2,1)} %bitcast.233), channel_id=1, source_target_pairs={{0,8},{8,0},{16,24},{24,16},{1,9},{9,1},{17,25},{25,17},{2,10},{10... | collective-permute-start | bytes 1376264 | tf_op jit(solution)/shard_map/ppermute | solution.py:158
  172.9 33.1 %collective-permute-start.73 = (bf16[2,448,512]{2,1,0:T(8,128)(2,1)S(1)}, bf16[2,448,512]{2,1,0:T(8,128)(2,1)S(1)}, u32[]{:S(2)}, u32[]{:S(2)}) collective-permute-start(bf16[2,448,512]{2,1,0:T(8,128)(2,1)S(1)} %pad_maximum_fusion.1), channel_id=1, source_target_pairs={{0,16},{8,24},{16,0},{24,8},{1,17},{9,25},{17,1},{25,9},{2,18},{10... | collective-permute-start | bytes 2752520 | tf_op jit(solution)/shard_map/ppermute | solution.py:158
  196.4 11.8 %collective-permute-start.90 = (bf16[64,512]{1,0:T(8,128)(2,1)S(1)}, bf16[64,512]{1,0:T(8,128)(2,1)S(1)}, u32[]{:S(2)}, u32[]{:S(2)}) collective-permute-start(bf16[64,512]{1,0:T(8,128)(2,1)S(1)} %pad_maximum_fusion.12), channel_id=1, source_target_pairs={{0,2},{2,4},{4,6},{6,7},{7,5},{5,3},{3,1},{1,0},{8,10},{10,12},{12... | collective-permute-start | bytes 196616 | tf_op jit(solution)/shard_map/ppermute | solution.py:80
  235.9 11.5 %collective-permute-start.64 = (bf16[392,512]{1,0:T(8,128)(2,1)S(1)}, bf16[392,512]{1,0:T(8,128)(2,1)S(1)}, u32[]{:S(2)}, u32[]{:S(2)}) collective-permute-start(bf16[392,512]{1,0:T(8,128)(2,1)S(1)} %shard_map.329.refs_2_.refs_0_), channel_id=1, source_target_pairs={{0,2},{2,4},{4,6},{6,7},{7,5},{5,3},{3,1},{1,0},{8,10},{10,12},{12... | collective-permute-start | bytes 1204232 | tf_op jit(solution)/shard_map/ppermute | solution.py:80
  236.5 12.5 %collective-permute-start.67 = (bf16[392,512]{1,0:T(8,128)(2,1)S(1)}, bf16[392,512]{1,0:T(8,128)(2,1)S(1)}, u32[]{:S(2)}, u32[]{:S(2)}) collective-permute-start(bf16[392,512]{1,0:T(8,128)(2,1)S(1)} %shard_map.329.refs_2_.refs_0_), channel_id=1, source_target_pairs={{2,0},{4,2},{6,4},{7,6},{5,7},{3,5},{1,3},{0,1},{10,8},{12,10},{14... | collective-permute-start | bytes 1204232 | tf_op jit(solution)/shard_map/ppermute | solution.py:83
  249.0 11.7 %collective-permute-start.68 = (bf16[392,512]{1,0:T(8,128)(2,1)S(1)}, bf16[392,512]{1,0:T(8,128)(2,1)S(1)}, u32[]{:S(2)}, u32[]{:S(2)}) collective-permute-start(bf16[392,512]{1,0:T(8,128)(2,1)S(1)} %collective-permute-done.67.refs_2_), channel_id=1, source_target_pairs={{2,0},{4,2},{6,4},{7,6},{5,7},{3,5},{1,3},{0,1},{10,8},{12,10},{14... | collective-permute-start | bytes 1204232 | tf_op jit(solution)/shard_map/ppermute | solution.py:83
  250.1 11.4 %collective-permute-start.78 = (bf16[576,128]{1,0:T(8,128)(2,1)S(1)}, bf16[576,128]{1,0:T(8,128)(2,1)S(1)}, u32[]{:S(2)}, u32[]{:S(2)}) collective-permute-start(bf16[576,128]{1,0:T(8,128)(2,1)S(1)} %pad_maximum_fusion.9), channel_id=1, source_target_pairs={{0,2},{2,4},{4,6},{6,7},{7,5},{5,3},{3,1},{1,0},{8,10},{10,12},{12... | collective-permute-start | bytes 442376 | tf_op jit(solution)/shard_map/ppermute | solution.py:80
  251.6 11.9 %collective-permute-start.79 = (bf16[576,128]{1,0:T(8,128)(2,1)S(1)}, bf16[576,128]{1,0:T(8,128)(2,1)S(1)}, u32[]{:S(2)}, u32[]{:S(2)}) collective-permute-start(bf16[576,128]{1,0:T(8,128)(2,1)S(1)} %pad_maximum_fusion.10), channel_id=1, source_target_pairs={{2,0},{4,2},{6,4},{7,6},{5,7},{3,5},{1,3},{0,1},{10,8},{12,10},{14... | collective-permute-start | bytes 442376 | tf_op jit(solution)/shard_map/ppermute | solution.py:83
  258.3 14.0 %collective-permute-start.66 = (bf16[392,512]{1,0:T(8,128)(2,1)S(1)}, bf16[392,512]{1,0:T(8,128)(2,1)S(1)}, u32[]{:S(2)}, u32[]{:S(2)}) collective-permute-start(bf16[392,512]{1,0:T(8,128)(2,1)S(1)} %collective-permute-done.65.refs_3_), channel_id=1, source_target_pairs={{0,2},{2,4},{4,6},{6,7},{7,5},{5,3},{3,1},{1,0},{8,10},{10,12},{12... | collective-permute-start | bytes 1204232 | tf_op jit(solution)/shard_map/ppermute | solution.py:80
  260.7 12.6 %collective-permute-start.69 = (bf16[392,512]{1,0:T(8,128)(2,1)S(1)}, bf16[392,512]{1,0:T(8,128)(2,1)S(1)}, u32[]{:S(2)}, u32[]{:S(2)}) collective-permute-start(bf16[392,512]{1,0:T(8,128)(2,1)S(1)} %collective-permute-done.68.refs_4_), channel_id=1, source_target_pairs={{2,0},{4,2},{6,4},{7,6},{5,7},{3,5},{1,3},{0,1},{10,8},{12,10},{14... | collective-permute-start | bytes 1204232 | tf_op jit(solution)/shard_map/ppermute | solution.py:83
  (113 other events, 867.0 us)

commit v5 on v4

--- a/solution.py
+++ b/solution.py
@@ -958,8 +958,8 @@
         )
 
     early = chan - 3
-    act, pre_three, stat_early = expand(0, early, [])
-    act, pre_three, stat_late = expand(early, 3, [act, pre_three])
+    act, pre_three, stat_early = expand(0, chan - 1, [])
+    act, pre_three, stat_late = expand(chan - 1, 1, [act, pre_three])
     stat_three = stat_early + stat_late
     stat_three = sum_over(stat_three, "dp", bits_below(dp), dp)
     block_out, grad_summed, sums_three = run(

time: 291 us -> 291 us (level)
  transfers between devices with their start and end apart: 98 -> 98, of which waited for: 51 -> 53; matrix products, arithmetic and copies ran while one was open for 7% -> 7% of each run, Pallas kernels for 13% -> 14%
where the time goes in v5:
time: 291 us; the launch traced here: 290 us
  waiting for transfers between devices  110 us (38%)
  starting transfers between devices  92 us (32%)
  Pallas kernels  55.7 us (19%)
  local copies, waits for them, and re-layouts  14.8 us (5%)
  other arithmetic  13.9 us (5%)
  between operations  3.75 us (1%)
    pallas_call x18, Pallas kernels, run(): pl.pallas_call(kernel if extra else body, grid_spec=pltpu.PrefetchScalarG...  52.6 us
    ppermute x39, waiting for transfers between devices, swap(): return lax.ppermute(x, axis, [(i, i ^ bit) for i in range(size)])  46.9 us
    ppermute x28, waiting for transfers between devices, fw(): return lax.ppermute(x, 'chan', self.ahead)  44.8 us
    ppermute x28, starting transfers between devices, bw(): return lax.ppermute(x, 'chan', self.back)  33.1 us
    ppermute x39, starting transfers between devices, swap(): return lax.ppermute(x, axis, [(i, i ^ bit) for i in range(size)])  27.5 us
    ppermute x28, starting transfers between devices, fw(): return lax.ppermute(x, 'chan', self.ahead)  27.2 us
    ppermute x28, waiting for transfers between devices, bw(): return lax.ppermute(x, 'chan', self.back)  18 us
    unnamed x89, local copies, waits for them, and re-layouts  10.7 us
  transfers between devices with their start and end apart: 98, of which 53 were waited for; matrix products, arithmetic and copies ran while one was open for 7% of the time, Pallas kernels for 14%

profile of v5, /device:TPU:0, one launch (start us, length us, event | category | flops | bytes accessed | tf_op | source)
XLA Modules:
  0.0 289.9 jit_solution(2294581438518061071)
XLA Ops:
  6.3 2.8 collective-permute-start.14
  38.0 6.6 %collective-permute-done.16 = bf16[848,128]{1,0:T(8,128)(2,1)S(1)} collective-permute-done((bf16[848,128]{1,0:T(8,128)(2,1)S(1)}, bf16[848,128]{1,0:T(8,128)(2,1)S(1)}, u32[]{:S(2)}, u32[]{:S(2)}) %collective-permute-start.16) | collective-permute-done | bytes 217120 | tf_op jit(solution)/shard_map/ppermute | solution.py:83
  46.1 5.6 %collective-permute-done.20 = bf16[848,128]{1,0:T(8,128)(2,1)S(1)} collective-permute-done((bf16[848,128]{1,0:T(8,128)(2,1)S(1)}, bf16[848,128]{1,0:T(8,128)(2,1)S(1)}, u32[]{:S(2)}, u32[]{:S(2)}) %collective-permute-start.20) | collective-permute-done | bytes 217120 | tf_op jit(solution)/shard_map/ppermute | solution.py:80
  59.9 5.5 %collective-permute-done.7 = bf16[392,512]{1,0:T(8,128)(2,1)S(1)} collective-permute-done((bf16[392,512]{1,0:T(8,128)(2,1)S(1)}, bf16[392,512]{1,0:T(8,128)(2,1)S(1)}, u32[]{:S(2)}, u32[]{:S(2)}) %collective-permute-start.7) | collective-permute-done | bytes 401440 | tf_op jit(solution)/shard_map/ppermute | solution.py:80
  68.0 6.7 %collective-permute-done.8.f = bf16[392,512]{1,0:T(8,128)(2,1)S(1)} collective-permute-done((bf16[392,512]{1,0:T(8,128)(2,1)S(1)}, bf16[392,512]{1,0:T(8,128)(2,1)S(1)}, u32[]{:S(2)}, u32[]{:S(2)}) %collective-permute-start.8) | collective-permute-done | bytes 401440 | tf_op jit(solution)/shard_map/ppermute | solution.py:80
  88.5 3.4 %shard_map.319 = bf16[9,512,512]{2,1,0:T(8,128)(2,1)S(1)} custom-call(s32[40]{0:T(128)S(1)} %copy-done.19, bf16[1,5,576,128]{3,2,1,0:T(8,128)(2,1)S(1)} %bitcast.239, bf16[1,5,576,128]{3,2,1,0:T(8,128)(2,1)S(1)} %collective-permute-done.21.refs_1_, bf16[1,3,576,128]{3,2,1,0:T(8,128)(2,1)S(1)} %maximum_bitcast_fusion.refs_2_, ...), custom_call_target="tpu_custom_call" | custom-call | tf_op jit(solution)/shard_map/pallas_call | solution.py:178
  92.0 4.0 %shard_map.320 = (f32[448,512]{1,0:T(8,128)S(1)}, bf16[392,512]{1,0:T(8,128)(2,1)S(1)}, f32[2,512]{1,0:T(2,128)S(1)}, bf16[448,512]{1,0:T(8,128)(2,1)S(1)}) custom-call(s32[40]{0:T(128)S(1)} %copy-done.19, f32[448,512]{1,0:T(8,128)S(1)} %get-tuple-element.51.pre.pre_one, f32[2,512]{1,0:T(2,128)S(1)} %add.300.stat.stat_one, ...), custom_call_target="tpu_custom_call" | custom-call | flops 2113929216 | bytes 8388608 | tf_op jit(solution)/shard_map/pallas_call | solution.py:178
  101.0 4.9 %collective-permute-done.28 = f32[2,512]{1,0:T(2,128)S(1)} collective-permute-done((f32[2,512]{1,0:T(2,128)S(1)}, f32[2,512]{1,0:T(2,128)S(1)}, u32[]{:S(2)}, u32[]{:S(2)}) %collective-permute-start.28) | collective-permute-done | bytes 4128 | tf_op jit(solution)/shard_map/ppermute | solution.py:158
  111.7 3.1 %collective-permute-done.30 = f32[2,512]{1,0:T(2,128)S(1)} collective-permute-done((f32[2,512]{1,0:T(2,128)S(1)}, f32[2,512]{1,0:T(2,128)S(1)}, u32[]{:S(2)}, u32[]{:S(2)}) %collective-permute-start.30) | collective-permute-done | bytes 4128 | tf_op jit(solution)/shard_map/ppermute | solution.py:158
  118.4 3.1 %collective-permute-start.32 = (f32[2,512]{1,0:T(2,128)S(1)}, f32[2,512]{1,0:T(2,128)S(1)}, u32[]{:S(2)}, u32[]{:S(2)}) collective-permute-start(f32[2,512]{1,0:T(2,128)S(1)} %add.306.stat.stat_two), channel_id=1, source_target_pairs={{0,4},{1,5},{2,6},{3,7},{4,0},{5,1},{6,2},{7,3},{8,12},{9,13},{10,... | collective-permute-start | bytes 12296 | tf_op jit(solution)/shard_map/ppermute | solution.py:158
  134.8 4.8 %shard_map.322 = (bf16[8,392,512]{2,1,0:T(8,128)(2,1)S(1)}, f32[8,392,256]{2,1,0:T(8,128)S(1)}, f32[4,256]{1,0:T(4,128)S(1)}) custom-call(s32[40]{0:T(128)S(1)} %copy-done.19, bf16[392,512]{1,0:T(8,128)(2,1)S(1)} %get-tuple-element.54.refs_0_, bf16[392,512]{1,0:T(8,128)(2,1)S(1)} %collective-permute-done.33.refs_1_, ...), custom_call_target="tpu_custom_call" | custom-call | flops 719323136 | bytes 8429568 | tf_op jit(solution)/shard_map/pallas_call | solution.py:178
  144.0 3.2 %collective-permute-done.45 = f32[4,256]{1,0:T(4,128)S(1)} collective-permute-done((f32[4,256]{1,0:T(4,128)S(1)}, f32[4,256]{1,0:T(4,128)S(1)}, u32[]{:S(2)}, u32[]{:S(2)}) %collective-permute-start.45) | collective-permute-done | bytes 4128 | tf_op jit(solution)/shard_map/ppermute | solution.py:158
  147.2 5.2 %shard_map.324 = (f32[8,392,256]{2,1,0:T(8,128)}, f32[8,392,256]{2,1,0:T(8,128)S(1)}, f32[4,256]{1,0:T(4,128)S(1)}) custom-call(s32[40]{0:T(128)S(1)} %copy-done.19, f32[8,392,256]{2,1,0:T(8,128)S(1)} %get-tuple-element.57.pre.refs_0_, f32[4,256]{1,0:T(4,128)S(1)} %add.314.stat.refs_1_, f32[2,256]{1,0:T(2,128)S(1)} %copy-done.20, ...), custom_call_target="tpu_custom_call" | custom-call | flops 16056320 | bytes 12845056 | tf_op jit(solution)/shard_map/pallas_call | solution.py:178
  154.0 3.2 %collective-permute-done.47 = f32[4,256]{1,0:T(4,128)S(1)} collective-permute-done((f32[4,256]{1,0:T(4,128)S(1)}, f32[4,256]{1,0:T(4,128)S(1)}, u32[]{:S(2)}, u32[]{:S(2)}) %collective-permute-start.47) | collective-permute-done | bytes 4128 | tf_op jit(solution)/shard_map/ppermute | solution.py:158
  164.9 3.6 %shard_map.333 = bf16[8,64,256]{2,1,0:T(8,128)(2,1)S(1)} custom-call(s32[40]{0:T(128)S(1)} %copy-done.19, bf16[8,392,512]{2,1,0:T(8,128)(2,1)S(1)} %copy-done.6, bf16[8,392,256]{2,1,0:T(8,128)(2,1)S(1)} %get-tuple-element.80.back), custom_call_target="tpu_custom_call" | custom-call | flops 822083584 | bytes 4816896 | tf_op jit(solution)/shard_map/pallas_call | solution.py:178
  174.6 4.8 %collective-permute-done.87 = bf16[8,64,256]{2,1,0:T(8,128)(2,1)S(1)} collective-permute-done((bf16[8,64,256]{2,1,0:T(8,128)(2,1)S(1)}, bf16[8,64,256]{2,1,0:T(8,128)(2,1)S(1)}, u32[]{:S(2)}, u32[]{:S(2)}) %collective-permute-start.87) | collective-permute-done | bytes 262176 | tf_op jit(solution)/shard_map/ppermute | solution.py:158
  186.4 6.3 %collective-permute-done.53 = bf16[392,512]{1,0:T(8,128)(2,1)S(1)} collective-permute-done((bf16[392,512]{1,0:T(8,128)(2,1)S(1)}, bf16[392,512]{1,0:T(8,128)(2,1)S(1)}, u32[]{:S(2)}, u32[]{:S(2)}) %collective-permute-start.53) | collective-permute-done | bytes 401440 | tf_op jit(solution)/shard_map/ppermute | solution.py:80
  198.5 4.8 %collective-permute-done.54.f = bf16[392,512]{1,0:T(8,128)(2,1)S(1)} collective-permute-done((bf16[392,512]{1,0:T(8,128)(2,1)S(1)}, bf16[392,512]{1,0:T(8,128)(2,1)S(1)}, u32[]{:S(2)}, u32[]{:S(2)}) %collective-permute-start.54) | collective-permute-done | bytes 401440 | tf_op jit(solution)/shard_map/ppermute | solution.py:80
  218.0 4.6 %shard_map.328 = (bf16[2,448,128]{2,1,0:T(8,128)(2,1)S(1)}, bf16[2,448,128]{2,1,0:T(8,128)(2,1)S(1)}, f32[448,512]{1,0:T(8,128)S(1)}, f32[2,512]{1,0:T(2,128)S(1)}) custom-call(s32[40]{0:T(128)S(1)} %copy-done.19, f32[448,512]{1,0:T(8,128)S(1)} %get-tuple-element.68.up, f32[2,512]{1,0:T(2,128)S(1)} %add.326.sums, f32[448,512]{1,0:T(8,128)S(1)} %copy-done.17, ...), custom_call_target="tpu_custom_call" | custom-call | flops 2113929216 | bytes 8388608 | tf_op jit(solution)/shard_map/pallas_call | solution.py:178
  231.7 3.0 %collective-permute-done.63 = f32[2,512]{1,0:T(2,128)S(1)} collective-permute-done((f32[2,512]{1,0:T(2,128)S(1)}, f32[2,512]{1,0:T(2,128)S(1)}, u32[]{:S(2)}, u32[]{:S(2)}) %collective-permute-start.63) | collective-permute-done | bytes 4128 | tf_op jit(solution)/shard_map/ppermute | solution.py:158
  239.6 4.5 %shard_map.330 = bf16[8,576,128]{2,1,0:T(8,128)(2,1)S(1)} custom-call(s32[40]{0:T(128)S(1)} %copy-done.19, bf16[4,448,512]{2,1,0:T(8,128)(2,1)S(1)} %pad_maximum_fusion.refs_0_, bf16[4,1,448,128]{3,2,1,0:T(8,128)(2,1)S(1)} %pad_maximum_fusion.2.refs_1_, bf16[392,512]{1,0:T(8,128)(2,1)S(1)} %shard_map.329.refs_2_.refs_0_), custom_call_target="tpu_custom_call" | custom-call | flops 2113929216 | bytes 8388608 | tf_op jit(solution)/shard_map/pallas_call | solution.py:178
  252.3 6.3 %collective-permute-done.65.refs_3_ = bf16[392,512]{1,0:T(8,128)(2,1)S(1)} collective-permute-done((bf16[392,512]{1,0:T(8,128)(2,1)S(1)}, bf16[392,512]{1,0:T(8,128)(2,1)S(1)}, u32[]{:S(2)}, u32[]{:S(2)}) %collective-permute-start.65) | collective-permute-done | bytes 401440 | tf_op jit(solution)/shard_map/ppermute | solution.py:80
  265.2 5.9 %shard_map.331 = (f32[8,392,256]{2,1,0:T(8,128)}, f32[256,512]{1,0:T(8,128)S(1)}) custom-call(s32[40]{0:T(128)S(1)} %copy-done.19, bf16[392,512]{1,0:T(8,128)(2,1)S(1)} %shard_map.329.refs_2_.refs_0_, bf16[392,512]{1,0:T(8,128)(2,1)S(1)} %collective-permute-done.64.refs_1_, bf16[392,512]{1,0:T(8,128)(2,1)S(1)} %collective-permute-done.67.refs_2_, ...), custom_call_target="tpu_custom_call" | custom-call | flops 1027604480 | bytes 7024640 | tf_op jit(solution)/shard_map/pallas_call | solution.py:178
  278.6 4.0 %shard_map.332 = (f32[8,392,256]{2,1,0:T(8,128)}, bf16[256,512]{1,0:T(8,128)(2,1)S(1)}) custom-call(s32[40]{0:T(128)S(1)} %copy-done.19, bf16[392,512]{1,0:T(8,128)(2,1)S(1)} %collective-permute-done.66.refs_0_, bf16[392,512]{1,0:T(8,128)(2,1)S(1)} %collective-permute-done.69.refs_1_, ...), custom_call_target="tpu_custom_call", output_to_operand_aliasing={{0}: (9, {})} | custom-call | flops 616562688 | bytes 4214784 | tf_op jit(solution)/shard_map/pallas_call | solution.py:178
  (385 shorter events, 176.2 us)
Async XLA Ops:
  6.3 16.5 %collective-permute-start.14 = (bf16[848,128]{1,0:T(8,128)(2,1)}, bf16[848,128]{1,0:T(8,128)(2,1)}, u32[]{:S(2)}, u32[]{:S(2)}) collective-permute-start(bf16[848,128]{1,0:T(8,128)(2,1)} %shard_map.314._), channel_id=1, source_target_pairs={{2,0},{4,2},{6,4},{7,6},{5,7},{3,5},{1,3},{0,1},{10,8},{12,10},{14... | collective-permute-start | bytes 651272 | tf_op jit(solution)/shard_map/ppermute | solution.py:83
  9.2 15.3 %collective-permute-start.18 = (bf16[848,128]{1,0:T(8,128)(2,1)}, bf16[848,128]{1,0:T(8,128)(2,1)S(1)}, u32[]{:S(2)}, u32[]{:S(2)}) collective-permute-start(bf16[848,128]{1,0:T(8,128)(2,1)} %shard_map.314._), channel_id=1, source_target_pairs={{0,2},{2,4},{4,6},{6,7},{7,5},{5,3},{3,1},{1,0},{8,10},{10,12},{12... | collective-permute-start | bytes 651272 | tf_op jit(solution)/shard_map/ppermute | solution.py:80
  22.8 11.9 %collective-permute-start.15 = (bf16[848,128]{1,0:T(8,128)(2,1)}, bf16[848,128]{1,0:T(8,128)(2,1)S(1)}, u32[]{:S(2)}, u32[]{:S(2)}) collective-permute-start(bf16[848,128]{1,0:T(8,128)(2,1)} %collective-permute-done.14), channel_id=1, source_target_pairs={{2,0},{4,2},{6,4},{7,6},{5,7},{3,5},{1,3},{0,1},{10,8},{12,10},{14... | collective-permute-start | bytes 651272 | tf_op jit(solution)/shard_map/ppermute | solution.py:83
  30.3 22.7 %collective-permute-start.5 = (bf16[392,512]{1,0:T(8,128)(2,1)S(1)}, bf16[392,512]{1,0:T(8,128)(2,1)S(1)}, u32[]{:S(2)}, u32[]{:S(2)}) collective-permute-start(bf16[392,512]{1,0:T(8,128)(2,1)S(1)} %pad_maximum_fusion.4), channel_id=1, source_target_pairs={{2,0},{4,2},{6,4},{7,6},{5,7},{3,5},{1,3},{0,1},{10,8},{12,10},{14... | collective-permute-start | bytes 1204232 | tf_op jit(solution)/shard_map/ppermute | solution.py:83
  32.0 21.8 %collective-permute-start.4 = (bf16[392,512]{1,0:T(8,128)(2,1)S(1)}, bf16[392,512]{1,0:T(8,128)(2,1)S(1)}, u32[]{:S(2)}, u32[]{:S(2)}) collective-permute-start(bf16[392,512]{1,0:T(8,128)(2,1)S(1)} %pad_maximum_fusion.3), channel_id=1, source_target_pairs={{0,2},{2,4},{4,6},{6,7},{7,5},{5,3},{3,1},{1,0},{8,10},{10,12},{12... | collective-permute-start | bytes 1204232 | tf_op jit(solution)/shard_map/ppermute | solution.py:80
  34.8 33.1 %collective-permute-start.21 = (bf16[1,5,576,128]{3,2,1,0:T(8,128)(2,1)S(1)}, bf16[1,5,576,128]{3,2,1,0:T(8,128)(2,1)S(1)}, u32[]{:S(2)}, u32[]{:S(2)}) collective-permute-start(bf16[1,5,576,128]{3,2,1,0:T(8,128)(2,1)S(1)} %bitcast.237), channel_id=1, source_target_pairs={{0,16},{8,24},{16,0},{24,8},{1,17},{9,25},{17,1},{25,9},{2,18},{10... | collective-permute-start | bytes 2211848 | tf_op jit(solution)/shard_map/ppermute | solution.py:158
  36.5 52.0 %collective-permute-start.24 = (bf16[1,5,576,128]{3,2,1,0:T(8,128)(2,1)S(1)}, bf16[1,5,576,128]{3,2,1,0:T(8,128)(2,1)}, u32[]{:S(2)}, u32[]{:S(2)}) collective-permute-start(bf16[1,5,576,128]{3,2,1,0:T(8,128)(2,1)S(1)} %bitcast.238), channel_id=1, source_target_pairs={{0,8},{8,0},{16,24},{24,16},{1,9},{9,1},{17,25},{25,17},{2,10},{10... | collective-permute-start | bytes 2211848 | tf_op jit(solution)/shard_map/ppermute | solution.py:158
  59.1 18.0 %collective-permute-start.23 = (bf16[1,3,576,128]{3,2,1,0:T(8,128)(2,1)S(1)}, bf16[1,3,576,128]{3,2,1,0:T(8,128)(2,1)S(1)}, u32[]{:S(2)}, u32[]{:S(2)}) collective-permute-start(bf16[1,3,576,128]{3,2,1,0:T(8,128)(2,1)S(1)} %maximum_bitcast_fusion.refs_2_), channel_id=1, source_target_pairs={{0,16},{8,24},{16,0},{24,8},{1,17},{9,25},{17,1},{25,9},{2,18},{10... | collective-permute-start | bytes 1327112 | tf_op jit(solution)/shard_map/ppermute | solution.py:158
  67.9 20.5 %collective-permute-start.26 = (bf16[1,3,576,128]{3,2,1,0:T(8,128)(2,1)S(1)}, bf16[1,3,576,128]{3,2,1,0:T(8,128)(2,1)}, u32[]{:S(2)}, u32[]{:S(2)}) collective-permute-start(bf16[1,3,576,128]{3,2,1,0:T(8,128)(2,1)S(1)} %maximum_bitcast_fusion.refs_2_), channel_id=1, source_target_pairs={{0,8},{8,0},{16,24},{24,16},{1,9},{9,1},{17,25},{25,17},{2,10},{10... | collective-permute-start | bytes 1327112 | tf_op jit(solution)/shard_map/ppermute | solution.py:158
  74.7 13.8 %collective-permute-start.25 = (bf16[1,5,576,128]{3,2,1,0:T(8,128)(2,1)S(1)}, bf16[1,5,576,128]{3,2,1,0:T(8,128)(2,1)}, u32[]{:S(2)}, u32[]{:S(2)}) collective-permute-start(bf16[1,5,576,128]{3,2,1,0:T(8,128)(2,1)S(1)} %collective-permute-done.21.refs_1_), channel_id=1, source_target_pairs={{0,8},{8,0},{16,24},{24,16},{1,9},{9,1},{17,25},{25,17},{2,10},{10... | collective-permute-start | bytes 2211848 | tf_op jit(solution)/shard_map/ppermute | solution.py:158
  77.2 11.3 %collective-permute-start.27 = (bf16[1,3,576,128]{3,2,1,0:T(8,128)(2,1)S(1)}, bf16[1,3,576,128]{3,2,1,0:T(8,128)(2,1)}, u32[]{:S(2)}, u32[]{:S(2)}) collective-permute-start(bf16[1,3,576,128]{3,2,1,0:T(8,128)(2,1)S(1)} %collective-permute-done.23.refs_3_), channel_id=1, source_target_pairs={{0,8},{8,0},{16,24},{24,16},{1,9},{9,1},{17,25},{25,17},{2,10},{10... | collective-permute-start | bytes 1327112 | tf_op jit(solution)/shard_map/ppermute | solution.py:158
  107.2 14.4 %collective-permute-start.34 = (bf16[392,512]{1,0:T(8,128)(2,1)S(1)}, bf16[392,512]{1,0:T(8,128)(2,1)S(1)}, u32[]{:S(2)}, u32[]{:S(2)}) collective-permute-start(bf16[392,512]{1,0:T(8,128)(2,1)S(1)} %broadcast_select_fusion.1), channel_id=1, source_target_pairs={{0,2},{2,4},{4,6},{6,7},{7,5},{5,3},{3,1},{1,0},{8,10},{10,12},{12... | collective-permute-start | bytes 1204232 | tf_op jit(solution)/shard_map/ppermute | solution.py:80
  108.7 14.2 %collective-permute-start.38 = (bf16[392,512]{1,0:T(8,128)(2,1)}, bf16[392,512]{1,0:T(8,128)(2,1)S(1)}, u32[]{:S(2)}, u32[]{:S(2)}) collective-permute-start(bf16[392,512]{1,0:T(8,128)(2,1)} %broadcast_select_fusion), channel_id=1, source_target_pairs={{2,0},{4,2},{6,4},{7,6},{5,7},{3,5},{1,3},{0,1},{10,8},{12,10},{14... | collective-permute-start | bytes 1204232 | tf_op jit(solution)/shard_map/ppermute | solution.py:83
  154.0 18.8 %collective-permute-start.72 = (bf16[1,448,512]{2,1,0:T(8,128)(2,1)}, bf16[1,448,512]{2,1,0:T(8,128)(2,1)S(1)}, u32[]{:S(2)}, u32[]{:S(2)}) collective-permute-start(bf16[1,448,512]{2,1,0:T(8,128)(2,1)} %bitcast.233), channel_id=1, source_target_pairs={{0,8},{8,0},{16,24},{24,16},{1,9},{9,1},{17,25},{25,17},{2,10},{10... | collective-permute-start | bytes 1376264 | tf_op jit(solution)/shard_map/ppermute | solution.py:158
  172.8 33.1 %collective-permute-start.73 = (bf16[2,448,512]{2,1,0:T(8,128)(2,1)S(1)}, bf16[2,448,512]{2,1,0:T(8,128)(2,1)S(1)}, u32[]{:S(2)}, u32[]{:S(2)}) collective-permute-start(bf16[2,448,512]{2,1,0:T(8,128)(2,1)S(1)} %pad_maximum_fusion.1), channel_id=1, source_target_pairs={{0,16},{8,24},{16,0},{24,8},{1,17},{9,25},{17,1},{25,9},{2,18},{10... | collective-permute-start | bytes 2752520 | tf_op jit(solution)/shard_map/ppermute | solution.py:158
  184.4 12.0 %collective-permute-start.88 = (bf16[64,256]{1,0:T(8,128)(2,1)S(1)}, bf16[64,256]{1,0:T(8,128)(2,1)S(1)}, u32[]{:S(2)}, u32[]{:S(2)}) collective-permute-start(bf16[64,256]{1,0:T(8,128)(2,1)S(1)} %get-tuple-element.130), channel_id=1, source_target_pairs={{2,0},{4,2},{6,4},{7,6},{5,7},{3,5},{1,3},{0,1},{10,8},{12,10},{14... | collective-permute-start | bytes 98312 | tf_op jit(solution)/shard_map/ppermute | solution.py:83
  196.4 11.8 %collective-permute-start.90 = (bf16[64,512]{1,0:T(8,128)(2,1)S(1)}, bf16[64,512]{1,0:T(8,128)(2,1)S(1)}, u32[]{:S(2)}, u32[]{:S(2)}) collective-permute-start(bf16[64,512]{1,0:T(8,128)(2,1)S(1)} %pad_maximum_fusion.12), channel_id=1, source_target_pairs={{0,2},{2,4},{4,6},{6,7},{7,5},{5,3},{3,1},{1,0},{8,10},{10,12},{12... | collective-permute-start | bytes 196616 | tf_op jit(solution)/shard_map/ppermute | solution.py:80
  235.8 11.4 %collective-permute-start.64 = (bf16[392,512]{1,0:T(8,128)(2,1)S(1)}, bf16[392,512]{1,0:T(8,128)(2,1)S(1)}, u32[]{:S(2)}, u32[]{:S(2)}) collective-permute-start(bf16[392,512]{1,0:T(8,128)(2,1)S(1)} %shard_map.329.refs_2_.refs_0_), channel_id=1, source_target_pairs={{0,2},{2,4},{4,6},{6,7},{7,5},{5,3},{3,1},{1,0},{8,10},{10,12},{12... | collective-permute-start | bytes 1204232 | tf_op jit(solution)/shard_map/ppermute | solution.py:80
  236.7 11.8 %collective-permute-start.67 = (bf16[392,512]{1,0:T(8,128)(2,1)S(1)}, bf16[392,512]{1,0:T(8,128)(2,1)S(1)}, u32[]{:S(2)}, u32[]{:S(2)}) collective-permute-start(bf16[392,512]{1,0:T(8,128)(2,1)S(1)} %shard_map.329.refs_2_.refs_0_), channel_id=1, source_target_pairs={{2,0},{4,2},{6,4},{7,6},{5,7},{3,5},{1,3},{0,1},{10,8},{12,10},{14... | collective-permute-start | bytes 1204232 | tf_op jit(solution)/shard_map/ppermute | solution.py:83
  247.3 11.2 %collective-permute-start.65 = (bf16[392,512]{1,0:T(8,128)(2,1)S(1)}, bf16[392,512]{1,0:T(8,128)(2,1)S(1)}, u32[]{:S(2)}, u32[]{:S(2)}) collective-permute-start(bf16[392,512]{1,0:T(8,128)(2,1)S(1)} %collective-permute-done.64.refs_1_), channel_id=1, source_target_pairs={{0,2},{2,4},{4,6},{6,7},{7,5},{5,3},{3,1},{1,0},{8,10},{10,12},{12... | collective-permute-start | bytes 1204232 | tf_op jit(solution)/shard_map/ppermute | solution.py:80
  248.5 11.4 %collective-permute-start.68 = (bf16[392,512]{1,0:T(8,128)(2,1)S(1)}, bf16[392,512]{1,0:T(8,128)(2,1)S(1)}, u32[]{:S(2)}, u32[]{:S(2)}) collective-permute-start(bf16[392,512]{1,0:T(8,128)(2,1)S(1)} %collective-permute-done.67.refs_2_), channel_id=1, source_target_pairs={{2,0},{4,2},{6,4},{7,6},{5,7},{3,5},{1,3},{0,1},{10,8},{12,10},{14... | collective-permute-start | bytes 1204232 | tf_op jit(solution)/shard_map/ppermute | solution.py:83
  250.1 11.6 %collective-permute-start.78 = (bf16[576,128]{1,0:T(8,128)(2,1)S(1)}, bf16[576,128]{1,0:T(8,128)(2,1)S(1)}, u32[]{:S(2)}, u32[]{:S(2)}) collective-permute-start(bf16[576,128]{1,0:T(8,128)(2,1)S(1)} %pad_maximum_fusion.9), channel_id=1, source_target_pairs={{0,2},{2,4},{4,6},{6,7},{7,5},{5,3},{3,1},{1,0},{8,10},{10,12},{12... | collective-permute-start | bytes 442376 | tf_op jit(solution)/shard_map/ppermute | solution.py:80
  258.5 12.6 %collective-permute-start.66 = (bf16[392,512]{1,0:T(8,128)(2,1)S(1)}, bf16[392,512]{1,0:T(8,128)(2,1)S(1)}, u32[]{:S(2)}, u32[]{:S(2)}) collective-permute-start(bf16[392,512]{1,0:T(8,128)(2,1)S(1)} %collective-permute-done.65.refs_3_), channel_id=1, source_target_pairs={{0,2},{2,4},{4,6},{6,7},{7,5},{5,3},{3,1},{1,0},{8,10},{10,12},{12... | collective-permute-start | bytes 1204232 | tf_op jit(solution)/shard_map/ppermute | solution.py:80
  259.8 13.0 %collective-permute-start.69 = (bf16[392,512]{1,0:T(8,128)(2,1)S(1)}, bf16[392,512]{1,0:T(8,128)(2,1)S(1)}, u32[]{:S(2)}, u32[]{:S(2)}) collective-permute-start(bf16[392,512]{1,0:T(8,128)(2,1)S(1)} %collective-permute-done.68.refs_4_), channel_id=1, source_target_pairs={{2,0},{4,2},{6,4},{7,6},{5,7},{3,5},{1,3},{0,1},{10,8},{12,10},{14... | collective-permute-start | bytes 1204232 | tf_op jit(solution)/shard_map/ppermute | solution.py:83
  (113 other events, 859.6 us)
